TPU v7x, 32 devices: a whole 2x2x4 slice. The times are simulated.
32 devices in a mesh: gx: 4 (over y, core), gy: 4 (over z), gz: 2 (over x).
Axes of the slice: x: 2, y: 2, z: 4, core: 2. Of those that a mesh axis runs over, the one named last changes fastest.
Arguments:
- residual_in: float32 [32, 128, 512], P('gz', 'gy', 'gx'), may hold values from -6 to 6
- labels: int32 [32, 128, 512], P('gz', 'gy', 'gx'), may hold values 0 or 1
- factor: float32 [3, 32, 128, 512], P(None, 'gz', 'gy', 'gx'), may hold values from 0.5 to 2
- basis: float32 [4, 8, 8, 8], replicated, may hold values from 0.05 to 0.25
- basis_index: int32 [4, 16, 64], P('gz', 'gy', 'gx'), may hold values from 0 to 3
Outputs:
- preconditioned: float32 [32, 128, 512], P('gz', 'gy', 'gx')
- coarse_correction: float32 [4, 16, 64], P('gz', 'gy', 'gx')
All inputs are finite; a program needn't handle non-finite values. No bound on the sum of `labels` on one device may be relied on, other than what follows from the above.
Results may differ from a plain program's by a relative error of at most 0.0003.
Values sent between devices are 32-bit elements; how exact they have to be, the bound alone decides.
No kernel may reach another device: no remote copies, remote signals or barrier semaphores. Data moves between devices by JAX's collectives and lax.ppermute only.
A program may use at most 64 MiB of HBM per device.

v0:
```python
import math

import jax
import jax.numpy as jnp
from jax import lax
from jax.sharding import PartitionSpec as P

BLK = 8
CITERS = 4


BRICK = (0.6, 1.0, 1.0)
MORTAR = (0.25, 0.3, 0.3)
MASS = 0.05
OMEGA = 0.8
WEIGHT_ONE = 1.0 / (1.05 - 0.95 * math.cos(math.pi / 4))
WEIGHT_TWO = 1.0 / (1.05 + 0.95 * math.cos(math.pi / 4))
STENCIL_W = {1: 1.0, 2: 0.5, 3: 0.25}
OFFSETS = [
    (i, j, k) for i in (-1, 0, 1) for j in (-1, 0, 1) for k in (-1, 0, 1) if (i, j, k) != (0, 0, 0)
]


def padded_2(cells, sides, width):
    for axis, dim in sides:
        count = lax.axis_size(axis)
        ends = count - 1
        head = lax.slice_in_dim(cells, 0, width, axis=dim)
        tail = lax.slice_in_dim(cells, cells.shape[dim] - width, cells.shape[dim], axis=dim)
        cells = jnp.concatenate(
            [
                lax.ppermute(tail, axis, [(i, (i + 1) % count) for i in range(ends)]),
                cells,
                lax.ppermute(head, axis, [((i + 1) % count, i) for i in range(ends)]),
            ],
            axis=dim,
        )
    return cells


def material(labels, factor):
    rows = [
        jnp.where(labels == 1, MORTAR[axis_id], BRICK[axis_id]).astype(jnp.float32)
        * factor[axis_id]
        for axis_id in range(3)
    ]
    return jnp.stack(rows)


def subset_means(padded):
    means = {}
    for offset in OFFSETS:
        subset = tuple((axis_id for axis_id in range(3) if offset[axis_id] != 0))
        if subset not in means:
            total = padded[subset[0]]
            for axis_id in subset[1:]:
                total = total + padded[axis_id]
            means[subset] = total / float(len(subset))
    return means


def window(values, lead, offset, extent):
    return values[
        lead + offset[0] : lead + offset[0] + extent[0],
        lead + offset[1] : lead + offset[1] + extent[1],
        lead + offset[2] : lead + offset[2] + extent[2],
    ]


def couplings(padded, lead, extent, field):
    means = subset_means(padded)
    if field is None:
        full = (padded[0] + padded[1] + padded[2]) / 3.0
        total = MASS * window(full, lead, (0, 0, 0), extent)
    else:
        total = jnp.zeros(extent, jnp.float32)
    for offset in OFFSETS:
        subset = tuple((axis_id for axis_id in range(3) if offset[axis_id] != 0))
        values = means[subset]
        coupling = (
            0.5
            * STENCIL_W[len(subset)]
            * (window(values, lead, (0, 0, 0), extent) + window(values, lead, offset, extent))
        )
        if field is None:
            total = total + coupling
        else:
            total = total + coupling * window(field, 1, offset, extent)
    return total


def coarse_terms(padded, field):
    center = padded[:, 1:-1, 1:-1, 1:-1]
    extent = center.shape[1:]
    if field is None:
        total = MASS * (center[0] + center[1] + center[2]) / 3.0
    else:
        total = jnp.zeros(extent, jnp.float32)
    for axis_id in range(3):
        for step in (-1, 1):
            offset = tuple((step if d == axis_id else 0 for d in range(3)))
            coupling = 0.5 * (center[axis_id] + window(padded[axis_id], 1, offset, extent))
            if field is None:
                total = total + coupling
            else:
                total = total + coupling * window(field, 1, offset, extent)
    return total


def coarse_solve(coarse_rhs, coarse_kappa, pad_kappa, pad_field):
    coarse_pad = pad_kappa(coarse_kappa)
    coarse_diag = coarse_terms(coarse_pad, None)
    estimate = OMEGA * coarse_rhs / coarse_diag
    for sweep in range(CITERS - 1):
        off_coarse = coarse_terms(coarse_pad, pad_field(estimate))
        estimate = (
            estimate + OMEGA * (coarse_rhs - (coarse_diag * estimate - off_coarse)) / coarse_diag
        )
    return estimate


def restrict(residual, basis, basis_index):
    zc, yc, xc = basis_index.shape
    blocks = residual.reshape(zc, BLK, yc, BLK, xc, BLK)
    terms = jnp.einsum("aibjck,nijk->abcn", blocks, basis, precision=lax.Precision.HIGHEST)
    onehot = (basis_index[..., None] == jnp.arange(basis.shape[0], dtype=jnp.int32)).astype(
        jnp.float32
    )
    return (jnp.sum(terms * onehot, axis=-1), onehot)


def prolong(coarse, onehot, basis):
    zc, yc, xc = coarse.shape
    weighted = coarse[..., None] * onehot
    fine = jnp.einsum("abcn,nijk->aibjck", weighted, basis, precision=lax.Precision.HIGHEST)
    return fine.reshape(zc * BLK, yc * BLK, xc * BLK)


def block_mean(kappa):
    comps, zn, yn, xn = kappa.shape
    return kappa.reshape(comps, zn // BLK, BLK, yn // BLK, BLK, xn // BLK, BLK).mean(axis=(2, 4, 6))


def body(residual_in, labels, factor, basis, basis_index):
    kappa = material(labels, factor)
    extent = residual_in.shape
    padded = padded_2(kappa, (("gx", 3), ("gy", 2), ("gz", 1)), 1)
    diag = couplings(padded, 1, extent, None)
    first = WEIGHT_ONE * residual_in / diag
    first_pad = padded_2(first, (("gx", 2), ("gy", 1), ("gz", 0)), 1)
    off = couplings(padded, 1, extent, first_pad)
    image = diag * first - off
    smooth = first + WEIGHT_TWO * (residual_in - image) / diag
    coarse_rhs, onehot = restrict(residual_in, basis, basis_index)
    coarse_kappa = block_mean(kappa)
    estimate = coarse_solve(
        coarse_rhs,
        coarse_kappa,
        lambda values: padded_2(values, (("gx", 3), ("gy", 2), ("gz", 1)), 1),
        lambda values: padded_2(values, (("gx", 2), ("gy", 1), ("gz", 0)), 1),
    )
    preconditioned = smooth + prolong(estimate, onehot, basis)
    return (preconditioned, estimate)


def solution(mesh):
    in_specs = (
        P("gz", "gy", "gx"),
        P("gz", "gy", "gx"),
        P(None, "gz", "gy", "gx"),
        P(),
        P("gz", "gy", "gx"),
    )
    out_specs = (P("gz", "gy", "gx"), P("gz", "gy", "gx"))
    return jax.shard_map(body, mesh=mesh, in_specs=in_specs, out_specs=out_specs, check_vma=False)
```

profile of v0, /device:TPU:20, one launch (start us, length us, event | category | flops | bytes accessed | tf_op | source)
XLA Modules:
  0.0 188.7 jit_solution(16617397643768243520)
XLA Ops:
  2.8 3.6 %stack.26 = f32[1,2,8,4,8,16,8]{6,5,4,3,2,1,0:T(8,128)} reshape(f32[16,32,128]{2,1,0:T(8,128)S(1)} %get-tuple-element.24) | data formatting | bytes 524288 | tf_op jit(solution)/shard_map/stack | solution.py:47
  6.5 3.7 %stack.25 = f32[1,2,8,4,8,16,8]{6,5,4,3,2,1,0:T(8,128)} reshape(f32[16,32,128]{2,1,0:T(8,128)S(1)} %get-tuple-element.23) | data formatting | bytes 524288 | tf_op jit(solution)/shard_map/stack | solution.py:47
  10.2 3.7 %stack.24 = f32[1,2,8,4,8,16,8]{6,5,4,3,2,1,0:T(8,128)} reshape(f32[16,32,128]{2,1,0:T(8,128)S(1)} %get-tuple-element.10) | data formatting | bytes 524288 | tf_op jit(solution)/shard_map/stack | solution.py:47
  13.9 6.0 %maximum_reduce_fusion = f32[3,2,4,16]{3,2,1,0:T(4,128)S(1)} fusion(f32[1,2,8,4,8,16,8]{6,5,4,3,2,1,0:T(8,128)} %stack.26, f32[1,2,8,4,8,16,8]{6,5,4,3,2,1,0:T(8,128)} %stack.25, f32[1,2,8,4,8,16,8]{6,5,4,3,2,1,0:T(8,128)} %stack.24), kind=kLoop, calls=%fused_computation | loop fusion | flops 589440 | bytes 787968 | tf_op jit(solution)/shard_map/reduce_sum | solution.py:141
  24.5 3.6 %reshape.19 = f32[2,8,4,8,16,8]{5,4,3,2,1,0:T(8,128)} reshape(f32[16,32,128]{2,1,0:T(8,128)S(1)} %copy-done.8) | data formatting | bytes 524288 | tf_op jit(solution)/shard_map/reshape | solution.py:124
  28.1 16.4 %convolution_bitcast_fusion.1 = f32[2,4,16,4,1,1]{2,3,5,1,0,4:T(4,128)S(1)} fusion(f32[2,8,4,8,16,8]{5,4,3,2,1,0:T(8,128)} %reshape.19, f32[4,8,8,8,1,1]{3,2,1,0,5,4:T(8,128)S(1)} %bitcast.78), kind=kOutput, calls=%fused_computation.3 | convolution fusion | flops 3145728 | bytes 272384 | tf_op jit(solution)/shard_map/aibjck,nijk->abcn/dot_general | solution.py:125
  47.0 3.5 %collective-permute-start.14 = (f32[3,2,1,18]{3,1,2,0:T(2,128)S(1)}, f32[3,2,1,18]{3,1,2,0:T(2,128)S(1)}, u32[]{:S(2)}, u32[]{:S(2)}) collective-permute-start(f32[3,2,1,18]{3,1,2,0:T(2,128)S(1)} %get-tuple-element.40), channel_id=1, source_target_pairs={{0,2},{2,4},{4,6},{1,3},{3,5},{5,7},{8,10},{10,12},{12,14},{9,11},... | collective-permute-start | bytes 1304 | tf_op jit(solution)/shard_map/ppermute | solution.py:32
  53.9 4.5 %collective-permute-start.16 = (f32[3,1,6,18]{3,1,2,0:T(1,128)S(1)}, f32[3,1,6,18]{3,1,2,0:T(1,128)S(1)}, u32[]{:S(2)}, u32[]{:S(2)}) collective-permute-start(f32[3,1,6,18]{3,1,2,0:T(1,128)S(1)} %get-tuple-element.42), channel_id=1, source_target_pairs={{0,1},{2,3},{4,5},{6,7},{8,9},{10,11},{12,13},{14,15},{16,17},{18,... | collective-permute-start | bytes 3896 | tf_op jit(solution)/shard_map/ppermute | solution.py:32
  69.4 3.5 %collective-permute-start.20 = (f32[2,1,18]{2,0,1:T(2,128)S(1)}, f32[2,1,18]{2,0,1:T(2,128)S(1)}, u32[]{:S(2)}, u32[]{:S(2)}) collective-permute-start(f32[2,1,18]{2,0,1:T(2,128)S(1)} %get-tuple-element.48), channel_id=1, source_target_pairs={{0,2},{2,4},{4,6},{1,3},{3,5},{5,7},{8,10},{10,12},{12,14},{9,11},... | collective-permute-start | bytes 440 | tf_op jit(solution)/shard_map/ppermute | solution.py:32
  76.3 4.5 %collective-permute-start.22 = (f32[1,6,18]{2,0,1:T(1,128)S(1)}, f32[1,6,18]{2,0,1:T(1,128)S(1)}, u32[]{:S(2)}, u32[]{:S(2)}) collective-permute-start(f32[1,6,18]{2,0,1:T(1,128)S(1)} %get-tuple-element.59), channel_id=1, source_target_pairs={{0,1},{2,3},{4,5},{6,7},{8,9},{10,11},{12,13},{14,15},{16,17},{18,... | collective-permute-start | bytes 1304 | tf_op jit(solution)/shard_map/ppermute | solution.py:32
  91.2 3.9 %collective-permute-start.26 = (f32[2,1,18]{2,0,1:T(2,128)S(1)}, f32[2,1,18]{2,0,1:T(2,128)S(1)}, u32[]{:S(2)}, u32[]{:S(2)}) collective-permute-start(f32[2,1,18]{2,0,1:T(2,128)S(1)} %get-tuple-element.46), channel_id=1, source_target_pairs={{0,2},{2,4},{4,6},{1,3},{3,5},{5,7},{8,10},{10,12},{12,14},{9,11},... | collective-permute-start | bytes 440 | tf_op jit(solution)/shard_map/ppermute | solution.py:32
  98.0 4.5 %collective-permute-start.28 = (f32[1,6,18]{2,0,1:T(1,128)S(1)}, f32[1,6,18]{2,0,1:T(1,128)S(1)}, u32[]{:S(2)}, u32[]{:S(2)}) collective-permute-start(f32[1,6,18]{2,0,1:T(1,128)S(1)} %get-tuple-element.57), channel_id=1, source_target_pairs={{0,1},{2,3},{4,5},{6,7},{8,9},{10,11},{12,13},{14,15},{16,17},{18,... | collective-permute-start | bytes 1304 | tf_op jit(solution)/shard_map/ppermute | solution.py:32
  108.2 3.2 %collective-permute-start.31 = (f32[2,4,1]{2,0,1:T(2,128)S(1)}, f32[2,4,1]{2,0,1:T(2,128)S(1)}, u32[]{:S(2)}, u32[]{:S(2)}) collective-permute-start(f32[2,4,1]{2,0,1:T(2,128)S(1)} %get-tuple-element.62), channel_id=1, source_target_pairs={{8,0},{16,8},{24,16},{9,1},{17,9},{25,17},{10,2},{18,10},{26,18},{... | collective-permute-start | bytes 104 | tf_op jit(solution)/shard_map/ppermute | solution.py:34
  118.2 4.1 %collective-permute-start.32 = (f32[2,1,18]{2,0,1:T(2,128)S(1)}, f32[2,1,18]{2,0,1:T(2,128)S(1)}, u32[]{:S(2)}, u32[]{:S(2)}) collective-permute-start(f32[2,1,18]{2,0,1:T(2,128)S(1)} %get-tuple-element.44), channel_id=1, source_target_pairs={{0,2},{2,4},{4,6},{1,3},{3,5},{5,7},{8,10},{10,12},{12,14},{9,11},... | collective-permute-start | bytes 440 | tf_op jit(solution)/shard_map/ppermute | solution.py:32
  125.4 3.9 %collective-permute-start.2 = (f32[3,16,1,130]{3,2,1,0:T(1,128)S(1)}, f32[3,16,1,130]{3,2,1,0:T(1,128)S(1)}, u32[]{:S(2)}, u32[]{:S(2)}) collective-permute-start(f32[3,16,1,130]{3,2,1,0:T(1,128)S(1)} %get-tuple-element.14), channel_id=1, source_target_pairs={{0,2},{2,4},{4,6},{1,3},{3,5},{5,7},{8,10},{10,12},{12,14},{9,11},... | collective-permute-start | bytes 74888 | tf_op jit(solution)/shard_map/ppermute | solution.py:32
  132.9 4.6 %collective-permute-start.4 = (f32[3,1,34,130]{3,2,1,0:T(8,128)S(1)}, f32[3,1,34,130]{3,2,1,0:T(8,128)S(1)}, u32[]{:S(2)}, u32[]{:S(2)}) collective-permute-start(f32[3,1,34,130]{3,2,1,0:T(8,128)S(1)} %get-tuple-element.12), channel_id=1, source_target_pairs={{0,1},{2,3},{4,5},{6,7},{8,9},{10,11},{12,13},{14,15},{16,17},{18,... | collective-permute-start | bytes 159128 | tf_op jit(solution)/shard_map/ppermute | solution.py:32
  138.7 4.5 %collective-permute-start.34 = (f32[1,6,18]{2,0,1:T(1,128)S(1)}, f32[1,6,18]{2,0,1:T(1,128)S(1)}, u32[]{:S(2)}, u32[]{:S(2)}) collective-permute-start(f32[1,6,18]{2,0,1:T(1,128)S(1)} %get-tuple-element.55), channel_id=1, source_target_pairs={{0,1},{2,3},{4,5},{6,7},{8,9},{10,11},{12,13},{14,15},{16,17},{18,... | collective-permute-start | bytes 1304 | tf_op jit(solution)/shard_map/ppermute | solution.py:32
  153.1 3.8 %collective-permute-done.6 = f32[16,32,1]{2,1,0:T(8,128)S(1)} collective-permute-done((f32[16,32,1]{2,1,0:T(8,128)S(1)}, f32[16,32,1]{2,1,0:T(8,128)S(1)}, u32[]{:S(2)}, u32[]{:S(2)}) %collective-permute-start.6) | collective-permute-done | bytes 2080 | tf_op jit(solution)/shard_map/ppermute | solution.py:32
  159.7 3.9 %collective-permute-start.8 = (f32[16,1,130]{2,1,0:T(1,128)S(1)}, f32[16,1,130]{2,1,0:T(1,128)S(1)}, u32[]{:S(2)}, u32[]{:S(2)}) collective-permute-start(f32[16,1,130]{2,1,0:T(1,128)S(1)} %get-tuple-element.31), channel_id=1, source_target_pairs={{0,2},{2,4},{4,6},{1,3},{3,5},{5,7},{8,10},{10,12},{12,14},{9,11},... | collective-permute-start | bytes 24968 | tf_op jit(solution)/shard_map/ppermute | solution.py:32
  163.7 3.2 %convolution_bitcast_fusion = f32[2,8,4,8,16,8]{4,5,3,1,2,0:T(8,128)} fusion(f32[4,8,8,8,1,1]{3,2,1,0,5,4:T(8,128)S(1)} %bitcast.79, f32[2,4,16]{2,0,1:T(2,128)S(1)} %divide_add_fusion, s32[2,4,16]{2,0,1:T(2,128)S(1)} %copy.52), kind=kOutput, calls=%fused_computation.2 | convolution fusion | flops 3146752 | bytes 271360 | tf_op jit(solution)/shard_map/abcn,nijk->aibjck/dot_general | solution.py:135
  167.4 3.8 %copy.70 = f32[2,8,4,8,16,8]{5,4,3,2,1,0:T(8,128)} copy(f32[2,8,4,8,16,8]{4,5,3,1,2,0:T(8,128)} %convolution_bitcast_fusion) | data formatting | bytes 524288 | tf_op jit(solution)/shard_map/abcn,nijk->aibjck/transpose | solution.py:135
  171.3 4.3 %reshape.20 = f32[16,32,128]{2,1,0:T(8,128)} reshape(f32[2,8,4,8,16,8]{5,4,3,2,1,0:T(8,128)} %copy.70) | data formatting | bytes 524288 | tf_op jit(solution)/shard_map/reshape | solution.py:136
  181.0 3.0 %collective-permute-done.11 = f32[1,34,130]{2,1,0:T(8,128)S(1)} collective-permute-done((f32[1,34,130]{2,1,0:T(8,128)S(1)}, f32[1,34,130]{2,1,0:T(8,128)S(1)}, u32[]{:S(2)}, u32[]{:S(2)}) %collective-permute-start.11) | collective-permute-done | bytes 17712 | tf_op jit(solution)/shard_map/ppermute | solution.py:34
  184.6 4.1 %fusion.6 = f32[16,32,128]{2,1,0:T(8,128)} fusion(f32[16,32,128]{2,1,0:T(8,128)S(1)} %copy-done.11, f32[16,32,128]{2,1,0:T(8,128)S(1)} %get-tuple-element.6, f32[16,32,128]{2,1,0:T(8,128)S(1)} %copy-done.10, f32[16,32,128]{2,1,0:T(8,128)S(1)} %copy-done.9, f32[17,34,130]{2,1,0:T(8,128)S(1)} %get-tuple-element.26, f32[16,33,130]{2,1,0:T(8,128)S(1)} %get-tuple-element.30, ...), kind=kLoop, calls=%fused_computation.25 | loop fusion | flops 7340032 | bytes 16257024 | tf_op jit(solution)/shard_map/add | solution.py:162
  (136 shorter events, 79.3 us)
Async XLA Ops:
  20.0 24.6 %collective-permute-start.13 = (f32[3,2,4,1]{3,1,2,0:T(2,128)S(1)}, f32[3,2,4,1]{3,1,2,0:T(2,128)S(1)}, u32[]{:S(2)}, u32[]{:S(2)}) collective-permute-start(f32[3,2,4,1]{3,1,2,0:T(2,128)S(1)} %get-tuple-element.54), channel_id=1, source_target_pairs={{8,0},{16,8},{24,16},{9,1},{17,9},{25,17},{10,2},{18,10},{26,18},{... | collective-permute-start | bytes 296 | tf_op jit(solution)/shard_map/ppermute | solution.py:34
  21.9 22.6 %collective-permute-start.12 = (f32[3,2,4,1]{3,1,2,0:T(2,128)S(1)}, f32[3,2,4,1]{3,1,2,0:T(2,128)S(1)}, u32[]{:S(2)}, u32[]{:S(2)}) collective-permute-start(f32[3,2,4,1]{3,1,2,0:T(2,128)S(1)} %get-tuple-element.53), channel_id=1, source_target_pairs={{0,8},{8,16},{16,24},{1,9},{9,17},{17,25},{2,10},{10,18},{18,26},{... | collective-permute-start | bytes 296 | tf_op jit(solution)/shard_map/ppermute | solution.py:32
  44.6 5.9 %collective-permute-start.15 = (f32[3,2,1,18]{3,1,2,0:T(2,128)S(1)}, f32[3,2,1,18]{3,1,2,0:T(2,128)S(1)}, u32[]{:S(2)}, u32[]{:S(2)}) collective-permute-start(f32[3,2,1,18]{3,1,2,0:T(2,128)S(1)} %get-tuple-element.41), channel_id=1, source_target_pairs={{2,0},{4,2},{6,4},{3,1},{5,3},{7,5},{10,8},{12,10},{14,12},{11,9},... | collective-permute-start | bytes 1304 | tf_op jit(solution)/shard_map/ppermute | solution.py:34
  52.6 5.9 %collective-permute-start.17 = (f32[3,1,6,18]{3,1,2,0:T(1,128)S(1)}, f32[3,1,6,18]{3,1,2,0:T(1,128)S(1)}, u32[]{:S(2)}, u32[]{:S(2)}) collective-permute-start(f32[3,1,6,18]{3,1,2,0:T(1,128)S(1)} %get-tuple-element.43), channel_id=1, source_target_pairs={{1,0},{3,2},{5,4},{7,6},{9,8},{11,10},{13,12},{15,14},{17,16},{19,... | collective-permute-start | bytes 3896 | tf_op jit(solution)/shard_map/ppermute | solution.py:34
  53.9 5.9 %collective-permute-start.16 = (f32[3,1,6,18]{3,1,2,0:T(1,128)S(1)}, f32[3,1,6,18]{3,1,2,0:T(1,128)S(1)}, u32[]{:S(2)}, u32[]{:S(2)}) collective-permute-start(f32[3,1,6,18]{3,1,2,0:T(1,128)S(1)} %get-tuple-element.42), channel_id=1, source_target_pairs={{0,1},{2,3},{4,5},{6,7},{8,9},{10,11},{12,13},{14,15},{16,17},{18,... | collective-permute-start | bytes 3896 | tf_op jit(solution)/shard_map/ppermute | solution.py:32
  75.0 5.9 %collective-permute-start.23 = (f32[1,6,18]{2,0,1:T(1,128)S(1)}, f32[1,6,18]{2,0,1:T(1,128)S(1)}, u32[]{:S(2)}, u32[]{:S(2)}) collective-permute-start(f32[1,6,18]{2,0,1:T(1,128)S(1)} %get-tuple-element.60), channel_id=1, source_target_pairs={{1,0},{3,2},{5,4},{7,6},{9,8},{11,10},{13,12},{15,14},{17,16},{19,... | collective-permute-start | bytes 1304 | tf_op jit(solution)/shard_map/ppermute | solution.py:34
  76.3 5.9 %collective-permute-start.22 = (f32[1,6,18]{2,0,1:T(1,128)S(1)}, f32[1,6,18]{2,0,1:T(1,128)S(1)}, u32[]{:S(2)}, u32[]{:S(2)}) collective-permute-start(f32[1,6,18]{2,0,1:T(1,128)S(1)} %get-tuple-element.59), channel_id=1, source_target_pairs={{0,1},{2,3},{4,5},{6,7},{8,9},{10,11},{12,13},{14,15},{16,17},{18,... | collective-permute-start | bytes 1304 | tf_op jit(solution)/shard_map/ppermute | solution.py:32
  89.3 5.9 %collective-permute-start.27 = (f32[2,1,18]{2,0,1:T(2,128)S(1)}, f32[2,1,18]{2,0,1:T(2,128)S(1)}, u32[]{:S(2)}, u32[]{:S(2)}) collective-permute-start(f32[2,1,18]{2,0,1:T(2,128)S(1)} %get-tuple-element.47), channel_id=1, source_target_pairs={{2,0},{4,2},{6,4},{3,1},{5,3},{7,5},{10,8},{12,10},{14,12},{11,9},... | collective-permute-start | bytes 440 | tf_op jit(solution)/shard_map/ppermute | solution.py:34
  96.7 11.2 %collective-permute-start.29 = (f32[1,6,18]{2,0,1:T(1,128)S(1)}, f32[1,6,18]{2,0,1:T(1,128)S(1)}, u32[]{:S(2)}, u32[]{:S(2)}) collective-permute-start(f32[1,6,18]{2,0,1:T(1,128)S(1)} %get-tuple-element.58), channel_id=1, source_target_pairs={{1,0},{3,2},{5,4},{7,6},{9,8},{11,10},{13,12},{15,14},{17,16},{19,... | collective-permute-start | bytes 1304 | tf_op jit(solution)/shard_map/ppermute | solution.py:34
  98.0 9.9 %collective-permute-start.28 = (f32[1,6,18]{2,0,1:T(1,128)S(1)}, f32[1,6,18]{2,0,1:T(1,128)S(1)}, u32[]{:S(2)}, u32[]{:S(2)}) collective-permute-start(f32[1,6,18]{2,0,1:T(1,128)S(1)} %get-tuple-element.57), channel_id=1, source_target_pairs={{0,1},{2,3},{4,5},{6,7},{8,9},{10,11},{12,13},{14,15},{16,17},{18,... | collective-permute-start | bytes 1304 | tf_op jit(solution)/shard_map/ppermute | solution.py:32
  103.2 19.1 %collective-permute-start.1 = (f32[3,16,32,1]{2,1,3,0:T(8,128)S(1)}, f32[3,16,32,1]{2,1,3,0:T(8,128)S(1)}, u32[]{:S(2)}, u32[]{:S(2)}) collective-permute-start(f32[3,16,32,1]{2,1,3,0:T(8,128)S(1)} %copy.49), channel_id=1, source_target_pairs={{8,0},{16,8},{24,16},{9,1},{17,9},{25,17},{10,2},{18,10},{26,18},{... | collective-permute-start | bytes 18440 | tf_op jit(solution)/shard_map/ppermute | solution.py:34
  105.5 17.2 %collective-permute-start = (f32[3,16,32,1]{2,1,3,0:T(8,128)S(1)}, f32[3,16,32,1]{2,1,3,0:T(8,128)S(1)}, u32[]{:S(2)}, u32[]{:S(2)}) collective-permute-start(f32[3,16,32,1]{2,1,3,0:T(8,128)S(1)} %copy.48), channel_id=1, source_target_pairs={{0,8},{8,16},{16,24},{1,9},{9,17},{17,25},{2,10},{10,18},{18,26},{... | collective-permute-start | bytes 18440 | tf_op jit(solution)/shard_map/ppermute | solution.py:32
  116.3 13.0 %collective-permute-start.33 = (f32[2,1,18]{2,0,1:T(2,128)S(1)}, f32[2,1,18]{2,0,1:T(2,128)S(1)}, u32[]{:S(2)}, u32[]{:S(2)}) collective-permute-start(f32[2,1,18]{2,0,1:T(2,128)S(1)} %get-tuple-element.45), channel_id=1, source_target_pairs={{2,0},{4,2},{6,4},{3,1},{5,3},{7,5},{10,8},{12,10},{14,12},{11,9},... | collective-permute-start | bytes 440 | tf_op jit(solution)/shard_map/ppermute | solution.py:34
  118.2 11.1 %collective-permute-start.32 = (f32[2,1,18]{2,0,1:T(2,128)S(1)}, f32[2,1,18]{2,0,1:T(2,128)S(1)}, u32[]{:S(2)}, u32[]{:S(2)}) collective-permute-start(f32[2,1,18]{2,0,1:T(2,128)S(1)} %get-tuple-element.44), channel_id=1, source_target_pairs={{0,2},{2,4},{4,6},{1,3},{3,5},{5,7},{8,10},{10,12},{12,14},{9,11},... | collective-permute-start | bytes 440 | tf_op jit(solution)/shard_map/ppermute | solution.py:32
  123.5 6.0 %collective-permute-start.3 = (f32[3,16,1,130]{3,2,1,0:T(1,128)S(1)}, f32[3,16,1,130]{3,2,1,0:T(1,128)S(1)}, u32[]{:S(2)}, u32[]{:S(2)}) collective-permute-start(f32[3,16,1,130]{3,2,1,0:T(1,128)S(1)} %get-tuple-element.15), channel_id=1, source_target_pairs={{2,0},{4,2},{6,4},{3,1},{5,3},{7,5},{10,8},{12,10},{14,12},{11,9},... | collective-permute-start | bytes 74888 | tf_op jit(solution)/shard_map/ppermute | solution.py:34
  125.4 6.0 %collective-permute-start.2 = (f32[3,16,1,130]{3,2,1,0:T(1,128)S(1)}, f32[3,16,1,130]{3,2,1,0:T(1,128)S(1)}, u32[]{:S(2)}, u32[]{:S(2)}) collective-permute-start(f32[3,16,1,130]{3,2,1,0:T(1,128)S(1)} %get-tuple-element.14), channel_id=1, source_target_pairs={{0,2},{2,4},{4,6},{1,3},{3,5},{5,7},{8,10},{10,12},{12,14},{9,11},... | collective-permute-start | bytes 74888 | tf_op jit(solution)/shard_map/ppermute | solution.py:32
  131.6 11.7 %collective-permute-start.5 = (f32[3,1,34,130]{3,2,1,0:T(8,128)S(1)}, f32[3,1,34,130]{3,2,1,0:T(8,128)S(1)}, u32[]{:S(2)}, u32[]{:S(2)}) collective-permute-start(f32[3,1,34,130]{3,2,1,0:T(8,128)S(1)} %get-tuple-element.13), channel_id=1, source_target_pairs={{1,0},{3,2},{5,4},{7,6},{9,8},{11,10},{13,12},{15,14},{17,16},{19,... | collective-permute-start | bytes 159128 | tf_op jit(solution)/shard_map/ppermute | solution.py:34
  132.9 10.4 %collective-permute-start.4 = (f32[3,1,34,130]{3,2,1,0:T(8,128)S(1)}, f32[3,1,34,130]{3,2,1,0:T(8,128)S(1)}, u32[]{:S(2)}, u32[]{:S(2)}) collective-permute-start(f32[3,1,34,130]{3,2,1,0:T(8,128)S(1)} %get-tuple-element.12), channel_id=1, source_target_pairs={{0,1},{2,3},{4,5},{6,7},{8,9},{10,11},{12,13},{14,15},{16,17},{18,... | collective-permute-start | bytes 159128 | tf_op jit(solution)/shard_map/ppermute | solution.py:32
  137.4 14.2 %collective-permute-start.35 = (f32[1,6,18]{2,0,1:T(1,128)S(1)}, f32[1,6,18]{2,0,1:T(1,128)S(1)}, u32[]{:S(2)}, u32[]{:S(2)}) collective-permute-start(f32[1,6,18]{2,0,1:T(1,128)S(1)} %get-tuple-element.56), channel_id=1, source_target_pairs={{1,0},{3,2},{5,4},{7,6},{9,8},{11,10},{13,12},{15,14},{17,16},{19,... | collective-permute-start | bytes 1304 | tf_op jit(solution)/shard_map/ppermute | solution.py:34
  138.7 12.9 %collective-permute-start.34 = (f32[1,6,18]{2,0,1:T(1,128)S(1)}, f32[1,6,18]{2,0,1:T(1,128)S(1)}, u32[]{:S(2)}, u32[]{:S(2)}) collective-permute-start(f32[1,6,18]{2,0,1:T(1,128)S(1)} %get-tuple-element.55), channel_id=1, source_target_pairs={{0,1},{2,3},{4,5},{6,7},{8,9},{10,11},{12,13},{14,15},{16,17},{18,... | collective-permute-start | bytes 1304 | tf_op jit(solution)/shard_map/ppermute | solution.py:32
  149.2 7.7 %collective-permute-start.6 = (f32[16,32,1]{2,1,0:T(8,128)S(1)}, f32[16,32,1]{2,1,0:T(8,128)S(1)}, u32[]{:S(2)}, u32[]{:S(2)}) collective-permute-start(f32[16,32,1]{2,1,0:T(8,128)S(1)} %get-tuple-element.35), channel_id=1, source_target_pairs={{0,8},{8,16},{16,24},{1,9},{9,17},{17,25},{2,10},{10,18},{18,26},{... | collective-permute-start | bytes 6152 | tf_op jit(solution)/shard_map/ppermute | solution.py:32
  157.8 17.7 %collective-permute-start.9 = (f32[16,1,130]{2,1,0:T(1,128)S(1)}, f32[16,1,130]{2,1,0:T(1,128)S(1)}, u32[]{:S(2)}, u32[]{:S(2)}) collective-permute-start(f32[16,1,130]{2,1,0:T(1,128)S(1)} %get-tuple-element.32), channel_id=1, source_target_pairs={{2,0},{4,2},{6,4},{3,1},{5,3},{7,5},{10,8},{12,10},{14,12},{11,9},... | collective-permute-start | bytes 24968 | tf_op jit(solution)/shard_map/ppermute | solution.py:34
  159.7 15.8 %collective-permute-start.8 = (f32[16,1,130]{2,1,0:T(1,128)S(1)}, f32[16,1,130]{2,1,0:T(1,128)S(1)}, u32[]{:S(2)}, u32[]{:S(2)}) collective-permute-start(f32[16,1,130]{2,1,0:T(1,128)S(1)} %get-tuple-element.31), channel_id=1, source_target_pairs={{0,2},{2,4},{4,6},{1,3},{3,5},{5,7},{8,10},{10,12},{12,14},{9,11},... | collective-permute-start | bytes 24968 | tf_op jit(solution)/shard_map/ppermute | solution.py:32
  177.8 6.2 %collective-permute-start.11 = (f32[1,34,130]{2,1,0:T(8,128)S(1)}, f32[1,34,130]{2,1,0:T(8,128)S(1)}, u32[]{:S(2)}, u32[]{:S(2)}) collective-permute-start(f32[1,34,130]{2,1,0:T(8,128)S(1)} %get-tuple-element.28), channel_id=1, source_target_pairs={{1,0},{3,2},{5,4},{7,6},{9,8},{11,10},{13,12},{15,14},{17,16},{19,... | collective-permute-start | bytes 53048 | tf_op jit(solution)/shard_map/ppermute | solution.py:34
  (27 other events, 176.9 us)
where the time goes:
time: 190 us; the launch traced here: 189 us
  starting transfers between devices  94 us (49%)
  local copies, waits for them, and re-layouts  26.5 us (14%)
  waiting for transfers between devices  26.1 us (14%)
  other arithmetic  21.1 us (11%)
  matrix products  19.6 us (10%)
    ppermute x18, starting transfers between devices, padded_2(): lax.ppermute(tail, axis, [(i, (i + 1) % count) for i in range(ends)])  60.9 us
    ppermute x18, starting transfers between devices, padded_2(): lax.ppermute(head, axis, [((i + 1) % count, i) for i in range(ends)])  33.1 us
    ppermute x18, waiting for transfers between devices, padded_2(): lax.ppermute(tail, axis, [(i, (i + 1) % count) for i in range(ends)])  21.8 us
    dot_general x1, matrix products, restrict(): jnp.einsum('aibjck,nijk->abcn', blocks, basis, precision=lax.Precision.HI...  16.4 us
    another operation x3, local copies, waits for them, and re-layouts, material(): return jnp.stack(rows)  11.1 us
    reduce_sum x1, other arithmetic, block_mean(): kappa.reshape(comps, zn // BLK, BLK, yn // BLK, BLK, xn // BLK, BLK)  6 us
    ppermute x18, waiting for transfers between devices, padded_2(): lax.ppermute(head, axis, [((i + 1) % count, i) for i in range(ends)])  4.34 us
    reshape x1, local copies, waits for them, and re-layouts, prolong(): return fine.reshape(zc * BLK, yc * BLK, xc * BLK)  4.26 us
  transfers between devices with their start and end apart: 36, of which 12 were waited for; matrix products, arithmetic and copies ran while one was open for 21% of the time, Pallas kernels for 0%

commit v1 on v0

v1 whole, which is shorter than its diff:
```python
import math

import jax
import jax.numpy as jnp
from jax import lax
from jax.experimental import pallas as pl
from jax.experimental.pallas import tpu as pltpu
from jax.sharding import PartitionSpec as P

BLK = 8
CITERS = 4
BRICK = (0.6, 1.0, 1.0)
MORTAR = (0.25, 0.3, 0.3)
MASS = 0.05
OMEGA = 0.8
WEIGHT_ONE = 1.0 / (1.05 - 0.95 * math.cos(math.pi / 4))
WEIGHT_TWO = 1.0 / (1.05 + 0.95 * math.cos(math.pi / 4))
SELF = 1.0 + 1.0 + 1.0 / 3.0 + MASS / 3.0
KEEP = 1.0 + WEIGHT_TWO / WEIGHT_ONE - WEIGHT_TWO

NZ, NY, NX = 16, 32, 128
CZ, CY, CX = 2, 4, 16
F32 = jnp.float32
HIGHEST = lax.Precision.HIGHEST

ZPAY = 7 * NY + 8
KROWS = 36
RROW = 3 * KROWS
YCO = 128
YPAY = YCO + 8
XPAY = 40 + 8
RLANE = 110


def iota(shape, dim):
    return lax.broadcasted_iota(jnp.int32, shape, dim)


def roll(values, shift, axis):
    size = values.shape[axis]
    shift = shift % size
    return values if shift == 0 else pltpu.roll(values, shift, axis)


def both(values, step, axis):
    return roll(values, step, axis) + roll(values, -step, axis)


def take(values, lanes):
    return jnp.take_along_axis(values, lanes, axis=1, mode="promise_in_bounds")


def pair_stiffness(own, below, above):
    k0, k1, k2 = own
    d0, d1, d2 = (a + b if a is not None else b for a, b in zip(below, above))
    part_y = 0.5 * k1 + 0.125 * (d0 + d1)
    part_yx = 0.125 * (k1 + k2) + (1.0 / 24.0) * (d0 + d1 + d2)
    part_0 = 0.5 * d0
    part_x = 0.5 * k2 + 0.125 * (d0 + d2)
    return part_0, part_y, part_x, part_yx


def first_kernel(r_ref, lab_ref, fac_ref, bas_ref, bix_ref, kap_ref, rr_ref, sel_ref, zpay_ref, tile_ref, sum_ref):
    gz = lax.axis_index("gz")
    tiled = lax.dot_general(
        bas_ref[...].reshape(4 * BLK * BLK, BLK),
        (iota((BLK, NX), 1) % BLK == iota((BLK, NX), 0)).astype(F32),
        (((1,), (0,)), ((), ())),
        precision=HIGHEST,
        preferred_element_type=F32,
    )
    tile_ref[...] = tiled.reshape(4, BLK, BLK, NX)
    sum_ref[...] = jnp.zeros(sum_ref.shape, F32)
    spread = (iota((CX, NX), 1) // BLK == iota((CX, NX), 0)).astype(F32)
    for zc in range(CZ):
        index = lax.dot_general(
            bix_ref[jnp.where(gz == 0, zc, CZ - 1 - zc)].astype(F32),
            spread,
            (((1,), (0,)), ((), ())),
            precision=HIGHEST,
            preferred_element_type=F32,
        )
        index = jnp.concatenate([jnp.broadcast_to(index[y : y + 1], (BLK, NX)) for y in range(CY)], axis=0)
        sums = [None] * 4
        for i in range(BLK):
            zp = zc * BLK + i
            z = jnp.where(gz == 0, zp, NZ - 1 - zp)
            zi = jnp.where(gz == 0, i, BLK - 1 - i)
            mortar = lab_ref[z] == 1
            b0, b1, b2, b3 = (jnp.concatenate([tile_ref[n, zi]] * CY, axis=0) for n in range(4))
            basis = jnp.where(index < 1.5, jnp.where(index < 0.5, b0, b1), jnp.where(index < 2.5, b2, b3))
            res = r_ref[z]
            rr_ref[zp] = res
            sel_ref[zp] = basis
            terms = []
            for a in range(3):
                k = jnp.where(mortar, MORTAR[a], BRICK[a]) * fac_ref[a, z]
                kap_ref[a, zp] = k
                terms.append(k)
                if zp == NZ - 1:
                    zpay_ref[2 * a * NY : (2 * a + 1) * NY] = k
                if zp == NZ - 2:
                    zpay_ref[(2 * a + 1) * NY : (2 * a + 2) * NY] = k
            if zp == NZ - 1:
                zpay_ref[6 * NY : 7 * NY] = res
            terms.append(basis * res)
            sums = [t if s is None else s + t for s, t in zip(sums, terms)]
        for q in range(4):
            total = sums[q].reshape(CY, BLK, NX).sum(axis=1)
            sum_ref[(q * 2 + zc) * 8 : (q * 2 + zc) * 8 + CY] = total if q == 3 else total * (1.0 / BLK**3)
    bricks = lax.dot_general(
        sum_ref[...],
        (iota((NX, NX), 0) // BLK == iota((NX, NX), 1) % CX).astype(F32),
        (((1,), (0,)), ((), ())),
        precision=HIGHEST,
        preferred_element_type=F32,
    )
    group = iota((8, NX), 1) // CX
    coarse = bricks[0:8]
    for g in range(1, 8):
        coarse = jnp.where(group == g, bricks[g * 8 : g * 8 + 8], coarse)
    zpay_ref[7 * NY : 7 * NY + 8] = coarse


def rows_kernel(kap_ref, rr_ref, ya_ref, yb_ref):
    even = lax.axis_index("gy") % 2 == 0

    def put(at, low, high):
        ya_ref[at : at + low.shape[0]] = jnp.where(even, high, low)
        yb_ref[at : at + low.shape[0]] = jnp.where(even, low, high)

    for zp in range(NZ):
        for a in range(3):
            put(a * KROWS + 2 * zp, kap_ref[a, zp, 0:2], kap_ref[a, zp, NY - 2 : NY])
        put(RROW + zp, rr_ref[zp, 0:1], rr_ref[zp, NY - 1 : NY])


def rows_more_kernel(za_ref, zpay_ref, ya_in, yb_in, ya_ref, yb_ref):
    even = lax.axis_index("gy") % 2 == 0
    ya_ref[0:YCO] = ya_in[0:YCO]
    yb_ref[0:YCO] = yb_in[0:YCO]

    def put(at, low, high):
        ya_ref[at : at + low.shape[0]] = jnp.where(even, high, low)
        yb_ref[at : at + low.shape[0]] = jnp.where(even, low, high)

    for a in range(3):
        for s in range(2):
            base = (2 * a + s) * NY
            put(a * KROWS + 2 * (NZ + s), za_ref[base : base + 2], za_ref[base + NY - 2 : base + NY])
    put(RROW + NZ, za_ref[6 * NY : 6 * NY + 1], za_ref[7 * NY - 1 : 7 * NY])
    coarse = jnp.concatenate([zpay_ref[7 * NY : 7 * NY + CY], za_ref[7 * NY : 7 * NY + CY]], axis=0)
    ya_ref[YCO : YCO + 8] = coarse
    yb_ref[YCO : YCO + 8] = coarse


def pack_columns(planes, residuals, rows):
    lane = iota((rows, NX), 1)
    left = jnp.zeros((rows, NX), F32)
    right = jnp.zeros((rows, NX), F32)
    for a in range(3):
        for zp in range(NZ + 2):
            at = 2 + a * KROWS + 2 * zp
            moved = roll(planes(a, zp), at, 1)
            left = jnp.where((lane == at) | (lane == at + 1), moved, left)
            right = jnp.where((lane == at - 2) | (lane == at - 1), moved, right)
    for zp in range(NZ + 1):
        at = RLANE + zp
        moved = roll(residuals(zp), at, 1)
        left = jnp.where(lane == at, moved, left)
        right = jnp.where(lane == at - 1, moved, right)
    return left, right


def columns_kernel(kap_ref, rr_ref, za_ref, left_ref, right_ref):
    def plane(a, zp):
        if zp < NZ:
            return kap_ref[a, zp]
        base = (2 * a + zp - NZ) * NY
        return za_ref[base : base + NY]

    def residual(zp):
        return rr_ref[zp] if zp < NZ else za_ref[6 * NY : 7 * NY]

    left_ref[...], right_ref[...] = pack_columns(plane, residual, NY)


def columns_more_kernel(
    ra_ref, rb_ref, yb_ref, left_in, right_in, xa_ref, xb_ref, left_ref, right_ref, hal_ref, hr_ref, cor_ref, lo_ref, hi_ref
):
    gx, gy = lax.axis_index("gx"), lax.axis_index("gy")
    even = gy % 2 == 0
    zero = jnp.zeros((YPAY, NX), F32)
    hi_ref[...] = jnp.where(gy < lax.axis_size("gy") - 1, jnp.where(even, ra_ref[...], rb_ref[...]), zero)
    lo_ref[...] = jnp.where(gy > 0, jnp.where(even, rb_ref[...], ra_ref[...]), zero)
    hal_ref[...] = jnp.zeros(hal_ref.shape, F32)
    hr_ref[...] = jnp.zeros(hr_ref.shape, F32)
    for zp in range(NZ + 2):
        for a in range(3):
            at = a * KROWS + 2 * zp
            hal_ref[a, zp, 0:2] = hi_ref[at : at + 2]
            hal_ref[a, zp, 6:8] = lo_ref[at : at + 2]
        if zp <= NZ:
            hr_ref[zp, 0:1] = hi_ref[RROW + zp : RROW + zp + 1]
            hr_ref[zp, 7:8] = lo_ref[RROW + zp : RROW + zp + 1]
    more_left, more_right = pack_columns(lambda a, zp: hal_ref[a, zp], lambda zp: hr_ref[zp], 8)
    left_ref[0:NY] = left_in[...]
    right_ref[0:NY] = right_in[...]
    left_ref[NY : NY + 8] = more_left
    right_ref[NY : NY + 8] = more_right
    even_x = gx % 2 == 0
    xa_ref[0:40] = jnp.where(even_x, right_ref[...], left_ref[...])
    xb_ref[0:40] = jnp.where(even_x, left_ref[...], right_ref[...])
    tiles = [yb_ref[YCO : YCO + 8], lo_ref[YCO : YCO + 8], hi_ref[YCO : YCO + 8]]
    lane = iota((8, NX), 1)
    source = (lane % 32) // 4 * CX + lane % 4
    sides = []
    for shift in (0, CX - 4):
        parts = [take(t, source + shift) for t in tiles]
        sides.append(jnp.where(lane < 32, parts[0], jnp.where(lane < 64, parts[1], parts[2])))
    xa_ref[40:48] = jnp.where(even_x, sides[1], sides[0])
    xb_ref[40:48] = jnp.where(even_x, sides[0], sides[1])
    for i in range(3):
        cor_ref[i] = tiles[i]


def interior_kernel(kap_ref, rr_ref, za_ref, hal_ref, hr_ref, s1_ref, s2_ref, f_ref):
    rows = NY + 8
    lane = iota((rows, NX), 1)
    inner = (lane > 0) & (lane < NX - 1)
    not_first, not_last = lane > 0, lane < NX - 1

    def stiff(zp):
        if zp < 0:
            return (None, None, None)
        own = []
        for a in range(3):
            if zp < NZ:
                plane = kap_ref[a, zp]
            else:
                base = (2 * a + zp - NZ) * NY
                plane = za_ref[base : base + NY]
            own.append(jnp.concatenate([plane, hal_ref[a, zp]], axis=0))
        return own

    def along_x(values):
        n = values.shape[0]
        back = jnp.where(not_first[:n], roll(values, 1, 1), 0.0)
        return back + jnp.where(not_last[:n], roll(values, -1, 1), 0.0)

    def residual(zp):
        own = rr_ref[zp] if zp < NZ else za_ref[6 * NY : 7 * NY]
        return jnp.concatenate([own, hr_ref[zp]], axis=0)

    def first(zp):
        k = stiff(zp)
        part_0, part_y, part_x, part_yx = pair_stiffness(k, stiff(zp - 1), stiff(zp + 1))
        diag = SELF * (k[0] + k[1] + k[2]) + part_0 + both(part_y, 1, 0)
        diag = diag + along_x(part_x + both(part_yx, 1, 0))
        inv = 1.0 / diag
        return jnp.where(inner, WEIGHT_ONE * residual(zp) * inv, 0.0), inv

    def image(zp, inv):
        k = [v[:NY] for v in stiff(zp)]
        f = f_ref[zp]
        fz = f_ref[zp + 1]
        p = [v * f for v in stiff(zp)]
        above = [v * f_ref[zp + 1] for v in stiff(zp + 1)]
        if zp > 0:
            fz = fz + f_ref[zp - 1]
            above = [u + v * f_ref[zp - 1] for u, v in zip(above, stiff(zp - 1))]
        own_y = 0.5 * p[1] + 0.125 * (above[0] + above[1])
        own_yx = 0.125 * (p[1] + p[2]) + (1.0 / 24.0) * (above[0] + above[1] + above[2])
        own_x = 0.5 * p[2] + 0.125 * (above[0] + above[2])
        dy = lambda v: both(v, 1, 0)[:NY]
        fy, fyz = dy(f), dy(fz)
        fc, fz = f[:NY], fz[:NY]
        total = 0.5 * above[0][:NY] + dy(own_y) + along_x(own_x[:NY] + dy(own_yx))
        t24 = (1.0 / 24.0) * fyz
        t8 = 0.125 * fyz
        total = total + k[0] * (0.5 * fz + t8 + along_x(0.125 * fz + t24))
        total = total + k[1] * (0.5 * fy + t8 + along_x(0.125 * fy + t24))
        total = total + k[2] * along_x(0.5 * fc + 0.125 * (fz + fy) + t24)
        scaled = WEIGHT_TWO * inv
        s1_ref[zp] = jnp.where(inner[:NY], scaled, total)
        s2_ref[zp] = jnp.where(inner[:NY], KEEP * fc + scaled * total, 0.0)

    waiting = None
    for zp in range(NZ + 1):
        f, inv = first(zp)
        f_ref[zp] = f
        if zp > 0:
            image(zp - 1, waiting)
        waiting = inv[:NY]


def slab_terms(mine, other, left):
    rows = NY + 8
    lane = iota((rows, NX), 1)
    zp, c = lane // 4, lane % 4
    real = zp < NZ + 2
    outer = c < 2 if left else c >= 2
    offset_k = jnp.where(outer, 0, 2) if left else jnp.where(outer, 2, 0)
    k = []
    for a in range(3):
        at = jnp.where(real, a * KROWS + 2 * zp + c % 2 + offset_k, 0)
        k.append(jnp.where(real, jnp.where(outer, take(other, at), take(mine, at)), 0.0))
    near = (c == 1) | (c == 2)
    near = near & (zp < NZ + 1)
    offset_r = jnp.where(outer, RLANE - 1, RLANE) if left else jnp.where(outer, RLANE, RLANE - 1)
    at = jnp.where(near, zp + offset_r, 0)
    res = jnp.where(outer, take(other, at), take(mine, at))

    dz = [both(v, 4, 1) for v in k]
    part_0, part_y, part_x, part_yx = pair_stiffness(k, (None, None, None), dz)
    diag = SELF * (k[0] + k[1] + k[2]) + part_0 + both(part_y, 1, 0)
    diag = diag + both(part_x + both(part_yx, 1, 0), 1, 1)
    inv = 1.0 / diag
    f = jnp.where(near, WEIGHT_ONE * res * inv, 0.0)

    p = [v * f for v in k]
    d0, d1, d2 = (both(v, 4, 1) for v in p)
    own_y = 0.5 * p[1] + 0.125 * (d0 + d1)
    own_yx = 0.125 * (p[1] + p[2]) + (1.0 / 24.0) * (d0 + d1 + d2)
    own_x = 0.5 * p[2] + 0.125 * (d0 + d2)
    fz = both(f, 4, 1)
    fy, fyz = both(f, 1, 0), both(fz, 1, 0)
    t24, t8 = (1.0 / 24.0) * fyz, 0.125 * fyz
    total = 0.5 * d0 + both(own_y, 1, 0) + both(own_x + both(own_yx, 1, 0), 1, 1)
    total = total + k[0] * (0.5 * fz + t8 + both(0.125 * fz + t24, 1, 1))
    total = total + k[1] * (0.5 * fy + t8 + both(0.125 * fy + t24, 1, 1))
    total = total + k[2] * both(0.5 * f + 0.125 * (fz + fy) + t24, 1, 1)
    face = c == 2 if left else c == 1
    scaled = WEIGHT_TWO * inv
    times = jnp.where(face, scaled, total)
    plus = jnp.where(face, KEEP * f + scaled * total, 0.0)
    return times[:NY], plus[:NY]


def coarse_solve(tiles, lower, upper):
    lane = iota((8, NX), 1)
    row = iota((8, NX), 0)
    zc, xs = lane // 32, lane % 32
    pair = jnp.where(zc < 2, zc, 3 - zc)
    arrays = []
    for q in range(4):
        at_own = (q * 2 + pair) * CX + jnp.clip(xs - 4, 0, CX - 1)
        blocks = []
        for b in range(3):
            at_low = b * 32 + (q * 2 + pair) * 4 + jnp.clip(xs, 0, 3)
            at_high = b * 32 + (q * 2 + pair) * 4 + jnp.clip(xs - 20, 0, 3)
            far = jnp.where(xs < 4, take(lower, at_low), jnp.where(xs < 24, take(upper, at_high), 0.0))
            whole = jnp.where((xs >= 4) & (xs < 20), take(tiles[b], at_own), far)
            blocks.append((whole, roll(whole, 4, 0)))
        own, below, above = blocks
        first_half = jnp.where(row < 4, jnp.where(lane < 64, below[0], below[1]), jnp.where(lane < 64, own[1], own[0]))
        second_half = jnp.where(row < 4, jnp.where(lane < 64, above[0], above[1]), 0.0)
        arrays.append(jnp.concatenate([first_half, second_half], axis=0))
    kc, rhs = arrays[:3], arrays[3]
    lane = iota((16, NX), 1)

    def sides(values, axis):
        if axis == 0:
            return (
                jnp.where(lane >= 32, roll(values, 32, 1), 0.0),
                jnp.where(lane < 96, roll(values, -32, 1), 0.0),
            )
        if axis == 1:
            return roll(values, 1, 0), roll(values, -1, 0)
        return roll(values, 1, 1), roll(values, -1, 1)

    couple = [[0.5 * (kc[a] + v) for v in sides(kc[a], a)] for a in range(3)]
    diag = (MASS / 3.0) * (kc[0] + kc[1] + kc[2])
    for a in range(3):
        diag = diag + (couple[a][0] + couple[a][1])
    inside = kc[0] > 0.0
    scaled = jnp.where(inside, OMEGA / jnp.where(inside, diag, 1.0), 0.0)
    estimate = scaled * rhs
    for _ in range(CITERS - 1):
        off = None
        for a in range(3):
            low, high = sides(estimate, a)
            term = couple[a][0] * low + couple[a][1] * high
            off = term if off is None else off + term
        estimate = estimate + scaled * (rhs - (diag * estimate - off))
    return estimate[0:8]


def last_kernel(ra_ref, rb_ref, left_ref, right_ref, cor_ref, s1_ref, s2_ref, sel_ref, out_ref, est_ref):
    gx, gz = lax.axis_index("gx"), lax.axis_index("gz")
    even = gx % 2 == 0
    zero = jnp.zeros((XPAY, NX), F32)
    right = jnp.where(gx < lax.axis_size("gx") - 1, jnp.where(even, ra_ref[...], rb_ref[...]), zero)
    left = jnp.where(gx > 0, jnp.where(even, rb_ref[...], ra_ref[...]), zero)
    left_times, left_plus = slab_terms(left_ref[...], left[:40], True)
    right_times, right_plus = slab_terms(right_ref[...], right[:40], False)
    lane = iota((NY, NX), 1)
    times = jnp.where(lane % 4 < 2, right_times, left_times)
    plus = jnp.where(lane % 4 < 2, right_plus, left_plus)

    estimate = coarse_solve([cor_ref[0], cor_ref[1], cor_ref[2]], left[40:48], right[40:48])
    lane8 = iota((8, NX), 1)
    rim = (lane < 2) | (lane >= NX - 2)
    for zc in range(CZ):
        z_out = jnp.where(gz == 0, zc, CZ - 1 - zc)
        est_ref[z_out] = roll(estimate, -(zc * 32 + 4), 1)[4:8, 0:CX]
        wide = take(estimate, zc * 32 + 4 + lane8 // BLK)
        fine = jnp.concatenate([jnp.broadcast_to(wide[4 + y : 5 + y], (BLK, NX)) for y in range(CY)], axis=0)
        for i in range(BLK):
            zp = zc * BLK + i
            z = jnp.where(gz == 0, zp, NZ - 1 - zp)
            x_times = jnp.where(rim, roll(times, -(4 * zp + 2), 1), 0.0)
            x_plus = jnp.where(rim, roll(plus, -(4 * zp + 2), 1), 0.0)
            out_ref[z] = s2_ref[zp] + x_plus + s1_ref[zp] * x_times + sel_ref[zp] * fine


def near(values):
    return pltpu.with_memory_space_constraint(values, pltpu.VMEM)


def call(kernel, inputs, outputs, scratch=(), aliases=None, cost=0, name=None):
    space = pl.BlockSpec(memory_space=pltpu.VMEM)
    return pl.pallas_call(
        kernel,
        out_shape=outputs,
        in_specs=[space] * len(inputs),
        out_specs=[space] * len(outputs),
        scratch_shapes=list(scratch),
        input_output_aliases=aliases or {},
        cost_estimate=pl.CostEstimate(flops=cost, bytes_accessed=cost, transcendentals=0),
        compiler_params=pltpu.CompilerParams(vmem_limit_bytes=32 * 2**20),
        name=name,
    )(*inputs)


def vmem(*shape):
    return pltpu.VMEM(shape, F32)


def exchange(values, sizes, move):
    nx, ny, nz = sizes
    pairs = []
    for x in range(nx):
        for y in range(ny):
            for z in range(nz):
                a, b, c = move(x, y, z)
                pairs.append(((x * ny + y) * nz + z, (a * ny + b) * nz + c))
    return lax.ppermute(values, ("gx", "gy", "gz"), pairs)


def solution(mesh):
    sizes = (mesh.shape["gx"], mesh.shape["gy"], mesh.shape["gz"])
    nx, ny, nz = sizes

    def swap_z(values):
        return exchange(values, sizes, lambda x, y, z: (x, y, nz - 1 - z))

    def swap_y(values, odd):
        def move(x, y, z):
            b = y + 1 if y % 2 == odd else y - 1
            return (x, b, z) if 0 <= b < ny else (x ^ 1, y, z)

        return exchange(values, sizes, move)

    def swap_x(values, odd):
        return exchange(values, sizes, lambda x, y, z: ((x + 1 if x % 2 == odd else x - 1) % nx, y, z))

    def body(residual_in, labels, factor, basis, basis_index):
        kap, rr, sel, zpay = call(
            first_kernel,
            [residual_in, labels, factor, basis, basis_index],
            [vmem(3, NZ, NY, NX), vmem(NZ, NY, NX), vmem(NZ, NY, NX), vmem(ZPAY, NX)],
            [pltpu.VMEM((4, BLK, BLK, NX), F32), pltpu.VMEM((64, NX), F32)],
            name="stiffness",
        )
        kap, rr, sel, zpay = near(kap), near(rr), near(sel), near(zpay)
        za = near(swap_z(zpay))
        ya, yb = call(rows_kernel, [kap, rr], [vmem(YPAY, NX), vmem(YPAY, NX)], name="rows")
        ya, yb = call(
            rows_more_kernel,
            [za, zpay, near(ya), near(yb)],
            [vmem(YPAY, NX), vmem(YPAY, NX)],
            name="rows_more",
        )
        ya, yb = near(ya), near(yb)
        ra, rb = near(swap_y(ya, 0)), near(swap_y(yb, 1))
        left, right = call(columns_kernel, [kap, rr, za], [vmem(NY, NX), vmem(NY, NX)], name="columns")
        xa, xb, left, right, hal, hr, cor = call(
            columns_more_kernel,
            [ra, rb, yb, near(left), near(right)],
            [vmem(XPAY, NX), vmem(XPAY, NX), vmem(40, NX), vmem(40, NX), vmem(3, NZ + 2, 8, NX), vmem(NZ + 1, 8, NX), vmem(3, 8, NX)],
            [pltpu.VMEM((YPAY, NX), F32), pltpu.VMEM((YPAY, NX), F32)],
            name="columns_more",
        )
        xa, xb = near(xa), near(xb)
        wb, wa = near(swap_x(xb, 1)), near(swap_x(xa, 0))
        s1, s2 = call(
            interior_kernel,
            [kap, rr, za, near(hal), near(hr)],
            [vmem(NZ, NY, NX), vmem(NZ, NY, NX)],
            [pltpu.VMEM((NZ + 1, 40, NX), F32)],
            name="interior",
        )
        out, estimate = call(
            last_kernel,
            [wa, wb, near(left), near(right), near(cor), near(s1), near(s2), sel],
            [jax.ShapeDtypeStruct((NZ, NY, NX), F32), jax.ShapeDtypeStruct((CZ, CY, CX), F32)],
            name="last",
        )
        return out, estimate

    in_specs = (
        P("gz", "gy", "gx"),
        P("gz", "gy", "gx"),
        P(None, "gz", "gy", "gx"),
        P(),
        P("gz", "gy", "gx"),
    )
    out_specs = (P("gz", "gy", "gx"), P("gz", "gy", "gx"))
    return jax.shard_map(body, mesh=mesh, in_specs=in_specs, out_specs=out_specs, check_vma=False)
```

time: 190 us -> 23.4 us (0.12)
  the two profiles are of different devices: /device:TPU:20 before, /device:TPU:19 now
where the time goes in v1:
time: 23.4 us; the launch traced here: 23.1 us
  waiting for transfers between devices  6.87 us (29%)
  starting transfers between devices  5.59 us (24%)
  Pallas kernels  5.31 us (23%)
  local copies, waits for them, and re-layouts  4.62 us (20%)
  between operations  0.7 us (3%)
    ppermute x5, waiting for transfers between devices, exchange(): return lax.ppermute(values, ('gx', 'gy', 'gz'), pairs)  6.87 us
    ppermute x5, starting transfers between devices, exchange(): return lax.ppermute(values, ('gx', 'gy', 'gz'), pairs)  5.59 us
    pallas_call x7, Pallas kernels, call(): pl.pallas_call(kernel, out_shape=outputs, in_specs=[space] * len(inputs),...  5.31 us
    unnamed x10, local copies, waits for them, and re-layouts  4.62 us
  transfers between devices with their start and end apart: 5, of which 3 were waited for; matrix products, arithmetic and copies ran while one was open for 0% of the time, Pallas kernels for 11%

profile of v1, /device:TPU:19, one launch (start us, length us, event | category | flops | bytes accessed | tf_op | source)
XLA Modules:
  0.0 23.1 jit_solution(15040987781900907086)
XLA Ops:
  0.6 0.0 copy-start
  0.6 1.1 %copy-done = f32[3,16,32,128]{3,2,1,0:T(8,128)S(1)} copy-done((f32[3,16,32,128]{3,2,1,0:T(8,128)S(1)}, f32[3,16,32,128]{3,2,1,0:T(8,128)}, u32[]{:S(2)}) %copy-start) | copy-done | bytes 786456
  1.8 0.9 %copy-done.1 = f32[16,32,128]{2,1,0:T(8,128)S(1)} copy-done((f32[16,32,128]{2,1,0:T(8,128)S(1)}, f32[16,32,128]{2,1,0:T(8,128)}, u32[]{:S(2)}) %copy-start.1) | copy-done | bytes 262168
  2.7 0.0 copy-start.2
  2.7 0.9 %copy-done.2 = s32[16,32,128]{2,1,0:T(8,128)S(1)} copy-done((s32[16,32,128]{2,1,0:T(8,128)S(1)}, s32[16,32,128]{2,1,0:T(8,128)}, u32[]{:S(2)}) %copy-start.2) | copy-done | bytes 262168
  3.7 0.0 copy-start.3
  3.7 0.9 %copy-done.3 = f32[4,8,8,8]{3,2,1,0:T(8,128)S(1)} copy-done((f32[4,8,8,8]{3,2,1,0:T(8,128)S(1)}, f32[4,8,8,8]{3,2,1,0:T(8,128)}, u32[]{:S(2)}) %copy-start.3) | copy-done | bytes 8216
  4.6 0.7 %copy-done.4 = s32[2,4,16]{2,1,0:T(4,128)S(1)} copy-done((s32[2,4,16]{2,1,0:T(4,128)S(1)}, s32[2,4,16]{2,1,0:T(4,128)}, u32[]{:S(2)}) %copy-start.4) | copy-done | bytes 536
  5.3 0.7 %stiffness.1 = (f32[3,16,32,128]{3,2,1,0:T(8,128)S(1)}, f32[16,32,128]{2,1,0:T(8,128)S(1)}, f32[16,32,128]{2,1,0:T(8,128)S(1)}, f32[232,128]{1,0:T(8,128)S(1)}) custom-call(f32[16,32,128]{2,1,0:T(8,128)S(1)} %copy-done.1, s32[16,32,128]{2,1,0:T(8,128)S(1)} %copy-done.2, f32[3,16,32,128]{3,2,1,0:T(8,128)S(1)} %copy-done, f32[4,8,8,8]{3,2,1,0:T(8,128)S(1)} %copy-done.3, ...), custom_call_target="tpu_custom_call" | custom-call | tf_op jit(solution)/shard_map/stiffness/pallas_call | solution.py:423
  5.9 0.3 %collective-permute-start = (f32[232,128]{1,0:T(8,128)S(1)}, f32[232,128]{1,0:T(8,128)S(1)}, u32[]{:S(2)}, u32[]{:S(2)}) collective-permute-start(f32[232,128]{1,0:T(8,128)S(1)} %get-tuple-element.21.zpay_ref), channel_id=1, source_target_pairs={{0,1},{1,0},{2,3},{3,2},{4,5},{5,4},{6,7},{7,6},{8,9},{9,8},{10,11... | collective-permute-start | bytes 356360 | tf_op jit(solution)/shard_map/ppermute | solution.py:448
  6.2 0.1 rows.1
  6.3 3.8 %collective-permute-done.za_ref = f32[232,128]{1,0:T(8,128)S(1)} collective-permute-done((f32[232,128]{1,0:T(8,128)S(1)}, f32[232,128]{1,0:T(8,128)S(1)}, u32[]{:S(2)}, u32[]{:S(2)}) %collective-permute-start) | collective-permute-done | bytes 118816 | tf_op jit(solution)/shard_map/ppermute | solution.py:448
  10.1 1.4 %collective-permute-start.1 = (f32[136,128]{1,0:T(8,128)S(1)}, f32[136,128]{1,0:T(8,128)S(1)}, u32[]{:S(2)}, u32[]{:S(2)}) collective-permute-start(f32[136,128]{1,0:T(8,128)S(1)} %get-tuple-element.26), channel_id=1, source_target_pairs={{0,2},{1,3},{2,0},{3,1},{4,6},{5,7},{6,4},{7,5},{8,10},{9,11},{10,... | collective-permute-start | bytes 208904 | tf_op jit(solution)/shard_map/ppermute | solution.py:448
  11.4 0.0 collective-permute-start.2
  11.5 0.4 %columns.1 = (f32[32,128]{1,0:T(8,128)S(1)}, f32[32,128]{1,0:T(8,128)S(1)}) custom-call(f32[3,16,32,128]{3,2,1,0:T(8,128)S(1)} %get-tuple-element.22.kap_ref, f32[16,32,128]{2,1,0:T(8,128)S(1)} %get-tuple-element.23.rr_ref, f32[232,128]{1,0:T(8,128)S(1)} %collective-permute-done.za_ref), custom_call_target="tpu_custom_call" | custom-call | tf_op jit(solution)/shard_map/columns/pallas_call | solution.py:423
  11.8 1.5 %collective-permute-done.1.ra_ref = f32[136,128]{1,0:T(8,128)S(1)} collective-permute-done((f32[136,128]{1,0:T(8,128)S(1)}, f32[136,128]{1,0:T(8,128)S(1)}, u32[]{:S(2)}, u32[]{:S(2)}) %collective-permute-start.1) | collective-permute-done | bytes 69664 | tf_op jit(solution)/shard_map/ppermute | solution.py:448
  13.3 1.6 %collective-permute-done.2.rb_ref = f32[136,128]{1,0:T(8,128)S(1)} collective-permute-done((f32[136,128]{1,0:T(8,128)S(1)}, f32[136,128]{1,0:T(8,128)S(1)}, u32[]{:S(2)}, u32[]{:S(2)}) %collective-permute-start.2) | collective-permute-done | bytes 69664 | tf_op jit(solution)/shard_map/ppermute | solution.py:448
  14.9 0.2 columns_more.1
  15.1 2.7 %collective-permute-start.3 = (f32[48,128]{1,0:T(8,128)S(1)}, f32[48,128]{1,0:T(8,128)S(1)}, u32[]{:S(2)}, u32[]{:S(2)}) collective-permute-start(f32[48,128]{1,0:T(8,128)S(1)} %get-tuple-element.30), channel_id=1, source_target_pairs={{0,8},{1,9},{2,10},{3,11},{4,12},{5,13},{6,14},{7,15},{8,0},{9,1},... | collective-permute-start | bytes 73736 | tf_op jit(solution)/shard_map/ppermute | solution.py:448
  17.9 1.2 %collective-permute-start.4 = (f32[48,128]{1,0:T(8,128)S(1)}, f32[48,128]{1,0:T(8,128)S(1)}, u32[]{:S(2)}, u32[]{:S(2)}) collective-permute-start(f32[48,128]{1,0:T(8,128)S(1)} %get-tuple-element.31), channel_id=1, source_target_pairs={{0,24},{1,25},{2,26},{3,27},{4,28},{5,29},{6,30},{7,31},{8,16},{9,... | collective-permute-start | bytes 73736 | tf_op jit(solution)/shard_map/ppermute | solution.py:448
  19.1 2.1 %interior.1 = (f32[16,32,128]{2,1,0:T(8,128)S(1)}, f32[16,32,128]{2,1,0:T(8,128)S(1)}) custom-call(f32[3,16,32,128]{3,2,1,0:T(8,128)S(1)} %get-tuple-element.22.kap_ref, f32[16,32,128]{2,1,0:T(8,128)S(1)} %get-tuple-element.23.rr_ref, f32[232,128]{1,0:T(8,128)S(1)} %collective-permute-done.za_ref, f32[3,18,8,128]{3,2,1,0:T(8,128)S(1)} %get-tuple-element.35.hal_ref, ...), custom_call_target="tpu_custom_call" | custom-call | tf_op jit(solution)/shard_map/interior/pallas_call | solution.py:423
  21.2 0.0 collective-permute-done.3.ra_ref
  21.2 0.0 collective-permute-done.4.rb_ref
  21.2 1.9 %last.1 = (f32[16,32,128]{2,1,0:T(8,128)}, f32[2,4,16]{2,1,0:T(4,128)}) custom-call(f32[48,128]{1,0:T(8,128)S(1)} %collective-permute-done.3.ra_ref, f32[48,128]{1,0:T(8,128)S(1)} %collective-permute-done.4.rb_ref, f32[40,128]{1,0:T(8,128)S(1)} %get-tuple-element.32.left_ref, f32[40,128]{1,0:T(8,128)S(1)} %get-tuple-element.33.right_ref, ...), custom_call_target="tpu_custom_call" | custom-call | tf_op jit(solution)/shard_map/last/pallas_call | solution.py:423
  (3 shorter events, 0.0 us)
Async XLA Ops:
  0.6 1.1 %copy-start = (f32[3,16,32,128]{3,2,1,0:T(8,128)S(1)}, f32[3,16,32,128]{3,2,1,0:T(8,128)}, u32[]{:S(2)}) copy-start(f32[3,16,32,128]{3,2,1,0:T(8,128)} %fac_ref.1) | copy-start | bytes 2359300
  1.8 0.9 %copy-start.1 = (f32[16,32,128]{2,1,0:T(8,128)S(1)}, f32[16,32,128]{2,1,0:T(8,128)}, u32[]{:S(2)}) copy-start(f32[16,32,128]{2,1,0:T(8,128)} %r_ref.1) | copy-start | bytes 786436
  2.7 0.9 %copy-start.2 = (s32[16,32,128]{2,1,0:T(8,128)S(1)}, s32[16,32,128]{2,1,0:T(8,128)}, u32[]{:S(2)}) copy-start(s32[16,32,128]{2,1,0:T(8,128)} %lab_ref.1) | copy-start | bytes 786436
  3.7 0.9 %copy-start.3 = (f32[4,8,8,8]{3,2,1,0:T(8,128)S(1)}, f32[4,8,8,8]{3,2,1,0:T(8,128)}, u32[]{:S(2)}) copy-start(f32[4,8,8,8]{3,2,1,0:T(8,128)} %bas_ref.1) | copy-start | bytes 24580
  4.6 0.7 %copy-start.4 = (s32[2,4,16]{2,1,0:T(4,128)S(1)}, s32[2,4,16]{2,1,0:T(4,128)}, u32[]{:S(2)}) copy-start(s32[2,4,16]{2,1,0:T(4,128)} %bix_ref.1) | copy-start | bytes 1540
  5.9 4.1 %collective-permute-start = (f32[232,128]{1,0:T(8,128)S(1)}, f32[232,128]{1,0:T(8,128)S(1)}, u32[]{:S(2)}, u32[]{:S(2)}) collective-permute-start(f32[232,128]{1,0:T(8,128)S(1)} %get-tuple-element.21.zpay_ref), channel_id=1, source_target_pairs={{0,1},{1,0},{2,3},{3,2},{4,5},{5,4},{6,7},{7,6},{8,9},{9,8},{10,11... | collective-permute-start | bytes 356360 | tf_op jit(solution)/shard_map/ppermute | solution.py:448
  10.1 3.2 %collective-permute-start.1 = (f32[136,128]{1,0:T(8,128)S(1)}, f32[136,128]{1,0:T(8,128)S(1)}, u32[]{:S(2)}, u32[]{:S(2)}) collective-permute-start(f32[136,128]{1,0:T(8,128)S(1)} %get-tuple-element.26), channel_id=1, source_target_pairs={{0,2},{1,3},{2,0},{3,1},{4,6},{5,7},{6,4},{7,5},{8,10},{9,11},{10,... | collective-permute-start | bytes 208904 | tf_op jit(solution)/shard_map/ppermute | solution.py:448
  11.4 3.5 %collective-permute-start.2 = (f32[136,128]{1,0:T(8,128)S(1)}, f32[136,128]{1,0:T(8,128)S(1)}, u32[]{:S(2)}, u32[]{:S(2)}) collective-permute-start(f32[136,128]{1,0:T(8,128)S(1)} %get-tuple-element.27.yb_ref), channel_id=1, source_target_pairs={{0,8},{1,9},{2,4},{3,5},{4,2},{5,3},{6,14},{7,15},{8,0},{9,1},{10,... | collective-permute-start | bytes 208904 | tf_op jit(solution)/shard_map/ppermute | solution.py:448
  15.1 6.1 %collective-permute-start.3 = (f32[48,128]{1,0:T(8,128)S(1)}, f32[48,128]{1,0:T(8,128)S(1)}, u32[]{:S(2)}, u32[]{:S(2)}) collective-permute-start(f32[48,128]{1,0:T(8,128)S(1)} %get-tuple-element.30), channel_id=1, source_target_pairs={{0,8},{1,9},{2,10},{3,11},{4,12},{5,13},{6,14},{7,15},{8,0},{9,1},... | collective-permute-start | bytes 73736 | tf_op jit(solution)/shard_map/ppermute | solution.py:448
  17.9 3.3 %collective-permute-start.4 = (f32[48,128]{1,0:T(8,128)S(1)}, f32[48,128]{1,0:T(8,128)S(1)}, u32[]{:S(2)}, u32[]{:S(2)}) collective-permute-start(f32[48,128]{1,0:T(8,128)S(1)} %get-tuple-element.31), channel_id=1, source_target_pairs={{0,24},{1,25},{2,26},{3,27},{4,28},{5,29},{6,30},{7,31},{8,16},{9,... | collective-permute-start | bytes 73736 | tf_op jit(solution)/shard_map/ppermute | solution.py:448

commit v2 on v1

v2 whole, which is shorter than its diff:
```python
import math

import jax
import jax.numpy as jnp
from jax import lax
from jax.experimental import pallas as pl
from jax.experimental.pallas import tpu as pltpu
from jax.sharding import PartitionSpec as P

BLK = 8
CITERS = 4
BRICK = (0.6, 1.0, 1.0)
MORTAR = (0.25, 0.3, 0.3)
MASS = 0.05
OMEGA = 0.8
WEIGHT_ONE = 1.0 / (1.05 - 0.95 * math.cos(math.pi / 4))
WEIGHT_TWO = 1.0 / (1.05 + 0.95 * math.cos(math.pi / 4))
SELF = 1.0 + 1.0 + 1.0 / 3.0 + MASS / 3.0
KEEP = 1.0 + WEIGHT_TWO / WEIGHT_ONE - WEIGHT_TWO

NZ, NY, NX = 16, 32, 128
CZ, CY, CX = 2, 4, 16
F32 = jnp.float32
HIGHEST = lax.Precision.HIGHEST

BULK = 7 * NY
UCOL = 40
URGENT = UCOL + NY
KROWS = 36
GROUP = NZ + 2
RROW = 3 * KROWS
YCO = 128
YPAY = YCO + 8
XPAY = 40 + 16
RLANE = 110


def iota(shape, dim):
    return lax.broadcasted_iota(jnp.int32, shape, dim)


def roll(values, shift, axis):
    size = values.shape[axis]
    shift = shift % size
    return values if shift == 0 else pltpu.roll(values, shift, axis)


def both(values, step, axis):
    return roll(values, step, axis) + roll(values, -step, axis)


def take(values, lanes):
    return jnp.take_along_axis(values, lanes, axis=1, mode="promise_in_bounds")


def pair_stiffness(own, below, above):
    k0, k1, k2 = own
    d0, d1, d2 = (a + b if a is not None else b for a, b in zip(below, above))
    part_y = 0.5 * k1 + 0.125 * (d0 + d1)
    part_yx = 0.125 * (k1 + k2) + (1.0 / 24.0) * (d0 + d1 + d2)
    part_0 = 0.5 * d0
    part_x = 0.5 * k2 + 0.125 * (d0 + d2)
    return part_0, part_y, part_x, part_yx


def first_kernel(
    r_hbm, lab_hbm, fac_hbm, bas_hbm, bix_hbm, kap_ref, rr_ref, sel_ref, urgent_ref,
    lab_ref, fac_ref, bas_ref, bix_ref, tile_ref, sum_ref, sems, more_sems
):
    gz = lax.axis_index("gz")
    halves = []
    small = [
        pltpu.make_async_copy(bas_hbm, bas_ref, sems.at[0]),
        pltpu.make_async_copy(bix_hbm, bix_ref, sems.at[1]),
    ]
    for copy in small:
        copy.start()
    for zc in range(CZ):
        planes = pl.ds(jnp.where(gz == 0, zc * BLK, (CZ - 1 - zc) * BLK), BLK)
        halves.append(
            [
                pltpu.make_async_copy(lab_hbm.at[planes], lab_ref.at[planes], more_sems.at[zc, 0]),
                pltpu.make_async_copy(fac_hbm.at[:, planes], fac_ref.at[:, planes], more_sems.at[zc, 1]),
                pltpu.make_async_copy(r_hbm.at[planes], rr_ref.at[planes], more_sems.at[zc, 2]),
            ]
        )
        for copy in halves[zc]:
            copy.start()
    sum_ref[...] = jnp.zeros(sum_ref.shape, F32)
    kap_ref[:, 0] = jnp.zeros((3, NY, NX), F32)
    for copy in small:
        copy.wait()
    tiled = lax.dot_general(
        bas_ref[...].reshape(4 * BLK * BLK, BLK),
        ((iota((BLK, NX), 1) & (BLK - 1)) == iota((BLK, NX), 0)).astype(F32),
        (((1,), (0,)), ((), ())),
        precision=HIGHEST,
        preferred_element_type=F32,
    )
    tile_ref[...] = tiled.reshape(4, BLK, BLK, NX)
    edges = [None] * 7
    spread = ((iota((CX, NX), 1) >> 3) == iota((CX, NX), 0)).astype(F32)
    for zc in range(CZ):
        index = lax.dot_general(
            bix_ref[jnp.where(gz == 0, zc, CZ - 1 - zc)].astype(F32),
            spread,
            (((1,), (0,)), ((), ())),
            precision=HIGHEST,
            preferred_element_type=F32,
        )
        index = jnp.concatenate([jnp.broadcast_to(index[y : y + 1], (BLK, NX)) for y in range(CY)], axis=0)
        for copy in halves[zc]:
            copy.wait()
        sums = [None] * 4
        for i in range(BLK):
            zp = zc * BLK + i
            z = jnp.where(gz == 0, zp, NZ - 1 - zp)
            zi = jnp.where(gz == 0, i, BLK - 1 - i)
            mortar = lab_ref[z] == 1
            b0, b1, b2, b3 = (jnp.concatenate([tile_ref[n, zi]] * CY, axis=0) for n in range(4))
            basis = jnp.where(index < 1.5, jnp.where(index < 0.5, b0, b1), jnp.where(index < 2.5, b2, b3))
            res = rr_ref[z]
            sel_ref[z] = basis
            terms = []
            for a in range(3):
                k = jnp.where(mortar, MORTAR[a], BRICK[a]) * fac_ref[a, z]
                kap_ref[a, zp + 1] = k
                terms.append(k)
                if zp >= NZ - 2:
                    plane = 2 * a + NZ - 1 - zp
                    edges[plane] = k
                    urgent_ref[plane * 4 : plane * 4 + 2] = k[0:2]
                    urgent_ref[plane * 4 + 2 : plane * 4 + 4] = k[NY - 2 : NY]
            if zp == NZ - 1:
                edges[6] = res
                urgent_ref[24:25] = res[0:1]
                urgent_ref[25:26] = res[NY - 1 : NY]
            terms.append(basis * res)
            sums = [t if s is None else s + t for s, t in zip(sums, terms)]
        for q in range(4):
            total = sums[q].reshape(CY, BLK, NX).sum(axis=1)
            sum_ref[(q * 2 + zc) * 8 : (q * 2 + zc) * 8 + CY] = total if q == 3 else total * (1.0 / BLK**3)
    bricks = lax.dot_general(
        sum_ref[...],
        ((iota((NX, NX), 0) >> 3) == (iota((NX, NX), 1) & (CX - 1))).astype(F32),
        (((1,), (0,)), ((), ())),
        precision=HIGHEST,
        preferred_element_type=F32,
    )
    group = iota((8, NX), 1) >> 4
    coarse = bricks[0:8]
    for g in range(1, 8):
        coarse = jnp.where(group == g, bricks[g * 8 : g * 8 + 8], coarse)
    urgent_ref[26:32] = jnp.zeros((6, NX), F32)
    urgent_ref[32:40] = coarse
    lane = iota((NY, NX), 1)
    columns = jnp.zeros((NY, NX), F32)
    for g, plane in enumerate(edges):
        columns = jnp.where(lane >= 4 * g, roll(plane, 4 * g + 2, 1), columns)
    urgent_ref[UCOL:URGENT] = columns


def place(zp):
    return jnp.where(lax.axis_index("gz") == 0, zp, NZ - 1 - zp)


def rows_kernel(kap_ref, rr_ref, ya_ref, yb_ref, bulk_ref):
    even = lax.axis_index("gy") % 2 == 0

    def put(at, low, high):
        ya_ref[at : at + 1] = jnp.where(even, high, low)
        yb_ref[at : at + 1] = jnp.where(even, low, high)

    for zp in range(NZ):
        for a in range(3):
            at = a * KROWS + zp
            put(at, kap_ref[a, zp + 1, 1:2], kap_ref[a, zp + 1, NY - 2 : NY - 1])
            put(at + GROUP, kap_ref[a, zp + 1, 0:1], kap_ref[a, zp + 1, NY - 1 : NY])
        put(RROW + zp, rr_ref[place(zp), 0:1], rr_ref[place(zp), NY - 1 : NY])
    for a in range(3):
        for s in range(2):
            bulk_ref[(2 * a + s) * NY : (2 * a + s + 1) * NY] = kap_ref[a, NZ - s]
    bulk_ref[6 * NY : 7 * NY] = rr_ref[place(NZ - 1)]


def rows_more_kernel(za_ref, mine_ref, ya_in, yb_in, after_ref, ya_ref, yb_ref):
    even = lax.axis_index("gy") % 2 == 0
    ya_ref[0:YCO] = ya_in[0:YCO]
    yb_ref[0:YCO] = yb_in[0:YCO]

    def put(at, low, high):
        ya_ref[at : at + low.shape[0]] = jnp.where(even, high, low)
        yb_ref[at : at + low.shape[0]] = jnp.where(even, low, high)

    for a in range(3):
        for s in range(2):
            base, at = (2 * a + s) * 4, a * KROWS + NZ + s
            put(at, za_ref[base + 1 : base + 2], za_ref[base + 2 : base + 3])
            put(at + GROUP, za_ref[base : base + 1], za_ref[base + 3 : base + 4])
    put(RROW + NZ, za_ref[24:25], za_ref[25:26])
    coarse = jnp.concatenate([mine_ref[32 : 32 + CY], za_ref[32 : 32 + CY]], axis=0)
    ya_ref[YCO : YCO + 8] = coarse
    yb_ref[YCO : YCO + 8] = coarse


def columns_kernel(kap_ref, rr_ref, urgent_ref, after_ref, left_ref, right_ref):
    lane = iota((NY, NX), 1)
    left = jnp.zeros((NY, NX), F32)
    right = jnp.zeros((NY, NX), F32)
    far = urgent_ref[UCOL:URGENT]
    for a in range(3):
        for zp in range(NZ + 2):
            at = 2 + a * KROWS + 2 * zp
            if zp < NZ:
                moved = roll(kap_ref[a, zp + 1], at, 1)
            else:
                moved = roll(far, at - 4 * (2 * a + zp - NZ) - 2, 1)
            left = jnp.where(lane >= at, moved, left)
            right = jnp.where(lane >= at - 2, moved, right)
    for zp in range(NZ + 1):
        at = RLANE + zp
        moved = roll(rr_ref[place(zp)], at, 1) if zp < NZ else roll(far, at - 26, 1)
        left = jnp.where(lane >= at, moved, left)
        right = jnp.where(lane >= at - 1, moved, right)
    left_ref[...] = left
    right_ref[...] = right


def columns_more_kernel(
    ra_ref, rb_ref, yb_ref, left_in, right_in, xa_ref, xb_ref, left_ref, right_ref, cor_ref, lo_ref, hi_ref
):
    gx, gy = lax.axis_index("gx"), lax.axis_index("gy")
    even = gy % 2 == 0
    zero = jnp.zeros((YPAY, NX), F32)
    hi = jnp.where(gy < lax.axis_size("gy") - 1, jnp.where(even, ra_ref[...], rb_ref[...]), zero)
    lo = jnp.where(gy > 0, jnp.where(even, rb_ref[...], ra_ref[...]), zero)
    hi_ref[...] = hi
    lo_ref[...] = lo

    lane, row = iota((8, NX), 1), iota((8, NX), 0)
    inner = (row == 0) | (row == 7)
    turned_hi, turned_lo = jnp.transpose(hi[:YCO]), jnp.transpose(lo[:YCO])
    part = (lane >= KROWS).astype(jnp.int32) + (lane >= 2 * KROWS).astype(jnp.int32)
    low_k = part * KROWS + ((lane - part * KROWS) >> 1)
    source = jnp.where(lane < RROW, low_k + jnp.where(inner, GROUP, 0), jnp.where(lane < YCO - 2, lane, 0))

    def column(x):
        values = jnp.where(
            row < 4,
            jnp.broadcast_to(turned_hi[x : x + 1], (8, NX)),
            jnp.broadcast_to(turned_lo[x : x + 1], (8, NX)),
        )
        return jnp.where((row < 2) | (row >= 6), take(values, source), 0.0)

    odd = (lane & 1) == 1
    more_left = jnp.where(odd & (lane < RROW), column(1), column(0))
    more_right = jnp.where(odd | (lane >= RROW), column(NX - 1), column(NX - 2))
    left_ref[0:NY] = left_in[...]
    right_ref[0:NY] = right_in[...]
    left_ref[NY : NY + 8] = roll(more_left, 2, 1)
    right_ref[NY : NY + 8] = jnp.where(lane < RROW, more_right, roll(more_right, 1, 1))
    even_x = gx % 2 == 0
    xa_ref[0:40] = jnp.where(even_x, right_ref[...], left_ref[...])
    xb_ref[0:40] = jnp.where(even_x, left_ref[...], right_ref[...])

    tiles = [lo[YCO:YPAY], yb_ref[YCO:YPAY], hi[YCO:YPAY]]
    zc, xs = lane >> 5, lane & 31
    pair = jnp.where(zc < 2, zc, 3 - zc)
    own = (xs >= 4) & (xs < 20)
    low_half, xs16 = lane < 64, iota((16, NX), 1) & 31
    sides = [jnp.zeros((16, NX), F32), jnp.zeros((16, NX), F32)]
    for q in range(4):
        at = (q * 2 + pair) * CX + jnp.clip(xs - 4, 0, CX - 1)
        below, mine, above = ((v, roll(v, 4, 0)) for v in (jnp.where(own, take(t, at), 0.0) for t in tiles))
        first = jnp.where(row < 4, jnp.where(low_half, below[0], below[1]), jnp.where(low_half, mine[1], mine[0]))
        second = jnp.where(row < 4, jnp.where(low_half, above[0], above[1]), 0.0)
        whole = jnp.concatenate([first, second], axis=0)
        cor_ref[q] = whole
        for i, start in enumerate((4, CX)):
            sides[i] = jnp.where((xs16 >= 4 * q) & (xs16 < 4 * q + 4), roll(whole, 4 * q - start, 1), sides[i])
    xa_ref[40:XPAY] = jnp.where(even_x, sides[1], sides[0])
    xb_ref[40:XPAY] = jnp.where(even_x, sides[0], sides[1])


def first_plane(to, zp, kap_ref, res, f_ref, p_ref, s1_ref, rim):
    below, k, above = ([kap_ref[a, zp + i] for a in range(3)] for i in range(3))
    part_0, part_y, part_x, part_yx = pair_stiffness(k, below, above)
    diag = SELF * (k[0] + k[1] + k[2]) + part_0 + both(part_y, 1, 0)
    inv = 1.0 / (diag + both(part_x + both(part_yx, 1, 0), 1, 1))
    f = jnp.where(rim, 0.0, WEIGHT_ONE * res * inv)
    f_ref[zp + 1] = f
    for a in range(3):
        p_ref[a, zp + 1] = k[a] * f
    if to < NZ if isinstance(to, int) else True:
        s1_ref[to] = WEIGHT_TWO * inv


def image_plane(to, zp, kap_ref, f_ref, p_ref, s1_ref, s2_ref, rim):
    k = [kap_ref[a, zp + 1] for a in range(3)]
    p = [p_ref[a, zp + 1] for a in range(3)]
    d0, d1, d2 = (p_ref[a, zp] + p_ref[a, zp + 2] for a in range(3))
    f, fz = f_ref[zp + 1], f_ref[zp] + f_ref[zp + 2]
    own_y = 0.5 * p[1] + 0.125 * (d0 + d1)
    own_yx = 0.125 * (p[1] + p[2]) + (1.0 / 24.0) * (d0 + d1 + d2)
    own_x = 0.5 * p[2] + 0.125 * (d0 + d2)
    fy, fyz = both(f, 1, 0), both(fz, 1, 0)
    t24, t8 = (1.0 / 24.0) * fyz, 0.125 * fyz
    total = 0.5 * d0 + both(own_y, 1, 0) + both(own_x + both(own_yx, 1, 0), 1, 1)
    total = total + k[0] * (0.5 * fz + t8 + both(0.125 * fz + t24, 1, 1))
    total = total + k[1] * (0.5 * fy + t8 + both(0.125 * fy + t24, 1, 1))
    total = total + k[2] * both(0.5 * f + 0.125 * (fz + fy) + t24, 1, 1)
    scaled = s1_ref[to]
    s1_ref[to] = jnp.where(rim, total, scaled)
    s2_ref[to] = jnp.where(rim, 0.0, KEEP * f + scaled * total)


def plane_rim():
    row, lane = iota((NY, NX), 0), iota((NY, NX), 1)
    return (row == 0) | (row == NY - 1) | (lane == 0) | (lane == NX - 1)


def inner_kernel(kap_ref, rr_ref, s1_ref, s2_ref, f_ref, p_ref):
    rim = plane_rim()
    f_ref[0] = jnp.zeros((NY, NX), F32)
    p_ref[:, 0] = jnp.zeros((3, NY, NX), F32)

    @pl.loop(0, 3)
    def _(i):
        for j in range(5):
            zp = i * 5 + j
            first_plane(zp, zp, kap_ref, rr_ref[place(zp)], f_ref, p_ref, s1_ref, rim)

    @pl.loop(0, 2)
    def _(i):
        for j in range(7):
            image_plane(i * 7 + j, i * 7 + j, kap_ref, f_ref, p_ref, s1_ref, s2_ref, rim)


def outer_kernel(kap_ref, rr_ref, bulk_ref, f_in, p_in, s1_in, s2_in, after_ref, s1_ref, s2_ref, k_ref, f_ref, p_ref):
    rim = plane_rim()
    for a in range(3):
        for i in range(3):
            k_ref[a, i] = kap_ref[a, NZ - 2 + i]
        for i in range(2):
            k_ref[a, 3 + i] = bulk_ref[(2 * a + i) * NY : (2 * a + i + 1) * NY]
            p_ref[a, i] = p_in[a, NZ - 2 + i]
    for i in range(2):
        f_ref[i] = f_in[NZ - 2 + i]
    first_plane(NZ - 1, 1, k_ref, rr_ref[place(NZ - 1)], f_ref, p_ref, s1_ref, rim)
    first_plane(NZ, 2, k_ref, bulk_ref[6 * NY : 7 * NY], f_ref, p_ref, s1_ref, rim)
    for i in range(2):
        image_plane(NZ - 2 + i, i, k_ref, f_ref, p_ref, s1_ref, s2_ref, rim)


def along_x(values):
    return both(values, 1, 1)


def edge_rows_kernel(ya_ref, yb_ref, lo_ref, hi_ref, s1_in, s2_in, s1_ref, s2_ref):
    even = lax.axis_index("gy") % 2 == 0
    size = 24
    row, lane = iota((size, NX), 0), iota((size, NX), 1)
    inner = (lane > 0) & (lane < NX - 1)
    near = inner & (row < NZ + 1)
    inner16 = inner[:NZ]
    for other, mine, face, second in (
        (lo_ref, jnp.where(even, yb_ref[...], ya_ref[...]), 0, 1),
        (hi_ref, jnp.where(even, ya_ref[...], yb_ref[...]), NY - 1, NY - 2),
    ):

        def group(source, at):
            return jnp.where(row < GROUP, source[at : at + size], 0.0)

        k = [[group(other, a * KROWS + s * GROUP) for a in range(3)] for s in (0, 1)]
        k += [[group(mine, a * KROWS + s * GROUP) for a in range(3)] for s in (1, 0)]
        parts = [pair_stiffness(v, (None, None, None), [both(u, 1, 0) for u in v]) for v in k]
        res = [None, other[RROW : RROW + size], mine[RROW : RROW + size]]
        f, inv = [None] * 3, [None] * 3
        for c in (1, 2):
            diag = SELF * (k[c][0] + k[c][1] + k[c][2]) + parts[c][0] + parts[c - 1][1] + parts[c + 1][1]
            inv[c] = 1.0 / (diag + along_x(parts[c][2] + parts[c - 1][3] + parts[c + 1][3]))
            f[c] = jnp.where(near, WEIGHT_ONE * res[c] * inv[c], 0.0)
        p = [None] + [[v * f[c] for v in k[c]] for c in (1, 2)]
        d = [None] + [[both(v, 1, 0) for v in p[c]] for c in (1, 2)]
        fz = [None] + [both(f[c], 1, 0) for c in (1, 2)]

        def row_parts(c):
            return (
                0.5 * p[c][1] + 0.125 * (d[c][0] + d[c][1]),
                0.125 * (p[c][1] + p[c][2]) + (1.0 / 24.0) * (d[c][0] + d[c][1] + d[c][2]),
            )

        own_y, own_yx = row_parts(1)
        own_x = 0.5 * p[2][2] + 0.125 * (d[2][0] + d[2][2])
        t24, t8 = (1.0 / 24.0) * fz[1], 0.125 * fz[1]
        total = 0.5 * d[2][0] + own_y + along_x(own_x + own_yx)
        total = total + k[2][0] * (0.5 * fz[2] + t8 + along_x(0.125 * fz[2] + t24))
        total = total + k[2][1] * (0.5 * f[1] + t8 + along_x(0.125 * f[1] + t24))
        total = total + k[2][2] * along_x(0.5 * f[2] + 0.125 * (fz[2] + f[1]) + t24)
        total = total[:NZ] + s1_ref[:, face, :]
        scaled = WEIGHT_TWO * inv[2][:NZ]
        s1_ref[:, face, :] = jnp.where(inner16, scaled, total)
        s2_ref[:, face, :] = jnp.where(inner16, KEEP * f[2][:NZ] + scaled * total, 0.0)

        own_y, own_yx = row_parts(2)
        t24, t8 = (1.0 / 24.0) * fz[2], 0.125 * fz[2]
        total = own_y + along_x(own_yx) + k[3][0] * (t8 + along_x(t24))
        total = total + k[3][1] * (0.5 * f[2] + t8 + along_x(0.125 * f[2] + t24))
        total = (total + k[3][2] * along_x(0.125 * f[2] + t24))[:NZ]
        scaled = s1_ref[:, second, :]
        s1_ref[:, second, :] = jnp.where(inner16, scaled, scaled + total)
        s2_ref[:, second, :] = s2_ref[:, second, :] + jnp.where(inner16, scaled * total, 0.0)


def slab_terms(mine, other, left):
    rows = NY + 8
    lane = iota((8, NX), 1)
    zp, c = lane >> 2, lane & 3
    real = zp < NZ + 2
    outer = c < 2 if left else c >= 2
    offset = jnp.where(outer, 0, 2) if left else jnp.where(outer, 2, 0)
    near = ((c == 1) | (c == 2)) & (zp < NZ + 1)
    offset_r = jnp.where(outer, RLANE - 1, RLANE) if left else jnp.where(outer, RLANE, RLANE - 1)
    at_r = jnp.where(near, zp + offset_r, 0)
    at_k = [jnp.where(real, a * KROWS + 2 * zp + (c & 1) + offset, 0) for a in range(3)]

    def spread(at, keep):
        pieces = []
        for i in range(0, rows, 8):
            piece = jnp.where(outer, take(other[i : i + 8], at), take(mine[i : i + 8], at))
            pieces.append(jnp.where(keep, piece, 0.0))
        return jnp.concatenate(pieces, axis=0)

    k = [spread(at, real) for at in at_k]
    res = spread(at_r, near)
    near = jnp.concatenate([near] * (rows // 8), axis=0)
    face = c == 2 if left else c == 1
    face = jnp.concatenate([face] * (rows // 8), axis=0)

    dz = [both(v, 4, 1) for v in k]
    part_0, part_y, part_x, part_yx = pair_stiffness(k, (None, None, None), dz)
    diag = SELF * (k[0] + k[1] + k[2]) + part_0 + both(part_y, 1, 0)
    diag = diag + both(part_x + both(part_yx, 1, 0), 1, 1)
    inv = 1.0 / diag
    f = jnp.where(near, WEIGHT_ONE * res * inv, 0.0)

    p = [v * f for v in k]
    d0, d1, d2 = (both(v, 4, 1) for v in p)
    own_y = 0.5 * p[1] + 0.125 * (d0 + d1)
    own_yx = 0.125 * (p[1] + p[2]) + (1.0 / 24.0) * (d0 + d1 + d2)
    own_x = 0.5 * p[2] + 0.125 * (d0 + d2)
    fz = both(f, 4, 1)
    fy, fyz = both(f, 1, 0), both(fz, 1, 0)
    t24, t8 = (1.0 / 24.0) * fyz, 0.125 * fyz
    total = 0.5 * d0 + both(own_y, 1, 0) + both(own_x + both(own_yx, 1, 0), 1, 1)
    total = total + k[0] * (0.5 * fz + t8 + both(0.125 * fz + t24, 1, 1))
    total = total + k[1] * (0.5 * fy + t8 + both(0.125 * fy + t24, 1, 1))
    total = total + k[2] * both(0.5 * f + 0.125 * (fz + fy) + t24, 1, 1)
    scaled = WEIGHT_TWO * inv
    times = jnp.where(face, scaled, total)
    plus = jnp.where(face, KEEP * f + scaled * total, 0.0)
    return times[:NY], plus[:NY]


def coarse_solve(cor_ref, lower, upper):
    xs = iota((16, NX), 1) & 31
    arrays = []
    for q in range(4):
        whole = jnp.where(xs < 4, roll(lower, -4 * q, 1), cor_ref[q])
        arrays.append(jnp.where((xs >= 20) & (xs < 24), roll(upper, 20 - 4 * q, 1), whole))
    kc, rhs = arrays[:3], arrays[3]
    lane = iota((16, NX), 1)

    def sides(values, axis):
        if axis == 0:
            return (
                jnp.where(lane >= 32, roll(values, 32, 1), 0.0),
                jnp.where(lane < 96, roll(values, -32, 1), 0.0),
            )
        if axis == 1:
            return roll(values, 1, 0), roll(values, -1, 0)
        return roll(values, 1, 1), roll(values, -1, 1)

    couple = [[0.5 * (kc[a] + v) for v in sides(kc[a], a)] for a in range(3)]
    diag = (MASS / 3.0) * (kc[0] + kc[1] + kc[2])
    for a in range(3):
        diag = diag + (couple[a][0] + couple[a][1])
    inside = kc[0] > 0.0
    scaled = jnp.where(inside, OMEGA / jnp.where(inside, diag, 1.0), 0.0)
    estimate = scaled * rhs
    for _ in range(CITERS - 1):
        off = None
        for a in range(3):
            low, high = sides(estimate, a)
            term = couple[a][0] * low + couple[a][1] * high
            off = term if off is None else off + term
        estimate = estimate + scaled * (rhs - (diag * estimate - off))
    return estimate[0:8]


def last_kernel(
    ra_ref, rb_ref, left_ref, right_ref, cor_ref, s1_ref, s2_ref, sel_ref, out_hbm, est_ref, out_ref, sems
):
    gx, gz = lax.axis_index("gx"), lax.axis_index("gz")
    even = gx % 2 == 0
    zero = jnp.zeros((XPAY, NX), F32)
    right = jnp.where(gx < lax.axis_size("gx") - 1, jnp.where(even, ra_ref[...], rb_ref[...]), zero)
    left = jnp.where(gx > 0, jnp.where(even, rb_ref[...], ra_ref[...]), zero)
    left_times, left_plus = slab_terms(left_ref[...], left[:40], True)
    right_times, right_plus = slab_terms(right_ref[...], right[:40], False)
    lane = iota((NY, NX), 1)
    low_side = (lane & 3) < 2
    times = jnp.where(low_side, right_times, left_times)
    plus = jnp.where(low_side, right_plus, left_plus)

    estimate = coarse_solve(cor_ref, left[40:XPAY], right[40:XPAY])
    lane8 = iota((8, NX), 1)
    rim = (lane < 2) | (lane >= NX - 2)
    copies = []
    step = 4
    for zc in range(CZ):
        z_out = jnp.where(gz == 0, zc, CZ - 1 - zc)
        est_ref[z_out] = roll(estimate, -(zc * 32 + 4), 1)[4:8, 0:CX]
        wide = take(estimate, zc * 32 + 4 + (lane8 >> 3))
        fine = jnp.concatenate([jnp.broadcast_to(wide[4 + y : 5 + y], (BLK, NX)) for y in range(CY)], axis=0)
        for i in range(BLK):
            zp = zc * BLK + i
            z = jnp.where(gz == 0, zp, NZ - 1 - zp)
            x_times = jnp.where(rim, roll(times, -(4 * zp + 2), 1), 0.0)
            x_plus = jnp.where(rim, roll(plus, -(4 * zp + 2), 1), 0.0)
            out_ref[z] = s2_ref[zp] + x_plus + s1_ref[zp] * x_times + sel_ref[z] * fine
            if zp % step == step - 1:
                planes = pl.ds(jnp.where(gz == 0, zp + 1 - step, NZ - 1 - zp), step)
                copies.append(pltpu.make_async_copy(out_ref.at[planes], out_hbm.at[planes], sems.at[zp // step]))
                copies[-1].start()
    for copy in copies:
        copy.wait()


def near(values):
    return pltpu.with_memory_space_constraint(values, pltpu.VMEM)


def call(kernel, inputs, outputs, scratch=(), aliases=None, us=0.1, name=None, in_space=pltpu.VMEM, out_spaces=None):
    return pl.pallas_call(
        kernel,
        out_shape=outputs,
        in_specs=[pl.BlockSpec(memory_space=in_space)] * len(inputs),
        out_specs=[pl.BlockSpec(memory_space=v) for v in out_spaces or [pltpu.VMEM] * len(outputs)],
        scratch_shapes=list(scratch),
        input_output_aliases=aliases or {},
        cost_estimate=pl.CostEstimate(flops=0, bytes_accessed=int(us * 3.6e6), transcendentals=0),
        compiler_params=pltpu.CompilerParams(vmem_limit_bytes=32 * 2**20),
        name=name,
    )(*inputs)


def vmem(*shape):
    return pltpu.VMEM(shape, F32)


def exchange(values, sizes, move):
    nx, ny, nz = sizes
    pairs = []
    for x in range(nx):
        for y in range(ny):
            for z in range(nz):
                a, b, c = move(x, y, z)
                pairs.append(((x * ny + y) * nz + z, (a * ny + b) * nz + c))
    return lax.ppermute(values, ("gx", "gy", "gz"), pairs)


def solution(mesh):
    sizes = (mesh.shape["gx"], mesh.shape["gy"], mesh.shape["gz"])
    nx, ny, nz = sizes

    def swap_z(values):
        return exchange(values, sizes, lambda x, y, z: (x, y, nz - 1 - z))

    def swap_y(values, odd):
        def move(x, y, z):
            b = y + 1 if y % 2 == odd else y - 1
            return (x, b, z) if 0 <= b < ny else (x ^ 1, y, z)

        return exchange(values, sizes, move)

    def swap_x(values, odd):
        return exchange(values, sizes, lambda x, y, z: ((x + 1 if x % 2 == odd else x - 1) % nx, y, z))

    def body(residual_in, labels, factor, basis, basis_index):
        inputs = [residual_in, labels, factor, basis, basis_index]
        kap, rr, sel, urgent = call(
            first_kernel,
            [pltpu.with_memory_space_constraint(v, pltpu.HBM) for v in inputs],
            [vmem(3, NZ + 1, NY, NX), vmem(NZ, NY, NX), vmem(NZ, NY, NX), vmem(URGENT, NX)],
            [
                pltpu.VMEM(labels.shape, jnp.int32),
                pltpu.VMEM(factor.shape, F32),
                pltpu.VMEM(basis.shape, F32),
                pltpu.VMEM(basis_index.shape, jnp.int32),
                pltpu.VMEM((4, BLK, BLK, NX), F32),
                pltpu.VMEM((64, NX), F32),
                pltpu.SemaphoreType.DMA((2,)),
                pltpu.SemaphoreType.DMA((CZ, 3)),
            ],
            us=1.8,
            name="stiffness",
            in_space=pltpu.HBM,
        )
        kap, rr, sel, urgent = near(kap), near(rr), near(sel), near(urgent)
        zu = near(swap_z(urgent))
        ya, yb, bulk = call(rows_kernel, [kap, rr], [vmem(YPAY, NX), vmem(YPAY, NX), vmem(BULK, NX)], name="rows")
        za = near(swap_z(near(bulk)))
        s1, s2, f, p = call(
            inner_kernel,
            [kap, rr],
            [vmem(NZ, NY, NX), vmem(NZ, NY, NX), vmem(NZ, NY, NX), vmem(3, NZ, NY, NX)],
            us=1.1,
            name="inner",
        )
        ya, yb = call(
            rows_more_kernel,
            [zu, urgent, near(ya), near(yb), near(s1)],
            [vmem(YPAY, NX), vmem(YPAY, NX)],
            name="rows_more",
        )
        ya, yb = near(ya), near(yb)
        ra, rb = near(swap_y(ya, 0)), near(swap_y(yb, 1))
        left, right = call(columns_kernel, [kap, rr, zu, ya], [vmem(NY, NX), vmem(NY, NX)], us=0.0, name="columns")
        xa, xb, left, right, cor, lo, hi = call(
            columns_more_kernel,
            [ra, rb, yb, near(left), near(right)],
            [vmem(XPAY, NX), vmem(XPAY, NX), vmem(40, NX), vmem(40, NX), vmem(4, 16, NX), vmem(YPAY, NX), vmem(YPAY, NX)],
            us=0.25,
            name="columns_more",
        )
        xa, xb = near(xa), near(xb)
        wb, wa = near(swap_x(xb, 1)), near(swap_x(xa, 0))
        s1, s2 = call(
            outer_kernel,
            [kap, rr, za, near(f), near(p), near(s1), near(s2), near(lo)],
            [vmem(NZ, NY, NX), vmem(NZ, NY, NX)],
            [pltpu.VMEM((3, 5, NY, NX), F32), pltpu.VMEM((4, NY, NX), F32), pltpu.VMEM((3, 4, NY, NX), F32)],
            aliases={5: 0, 6: 1},
            us=0.25,
            name="outer",
        )
        s1, s2 = call(
            edge_rows_kernel,
            [ya, yb, near(lo), near(hi), near(s1), near(s2)],
            [vmem(NZ, NY, NX), vmem(NZ, NY, NX)],
            aliases={4: 0, 5: 1},
            us=0.4,
            name="edge_rows",
        )
        out, estimate = call(
            last_kernel,
            [wa, wb, near(left), near(right), near(cor), near(s1), near(s2), sel],
            [jax.ShapeDtypeStruct((NZ, NY, NX), F32), jax.ShapeDtypeStruct((CZ, CY, CX), F32)],
            [pltpu.VMEM((NZ, NY, NX), F32), pltpu.SemaphoreType.DMA((4,))],
            us=2.0,
            name="last",
            out_spaces=[pltpu.HBM, pltpu.VMEM],
        )
        return out, estimate

    in_specs = (
        P("gz", "gy", "gx"),
        P("gz", "gy", "gx"),
        P(None, "gz", "gy", "gx"),
        P(),
        P("gz", "gy", "gx"),
    )
    out_specs = (P("gz", "gy", "gx"), P("gz", "gy", "gx"))
    return jax.shard_map(body, mesh=mesh, in_specs=in_specs, out_specs=out_specs, check_vma=False)
```

time: 23.4 us -> 19.5 us (0.83)
  local copies, waits for them, and re-layouts: 4.62 us -> 0 us
  waiting for transfers between devices: 6.87 us -> 4.26 us
  starting transfers between devices: 5.59 us -> 7.81 us
  Pallas kernels: 5.31 us -> 6.58 us
    unnamed x10 -> x0, local copies, waits for them, and re-layouts: 4.62 us -> none
    ppermute x5 -> x6, waiting for transfers between devices: 6.87 us -> 4.26 us  [exchange(): return lax.ppermute(values, ('gx', 'gy', 'gz'), pairs)]
    ppermute x5 -> x6, starting transfers between devices: 5.59 us -> 7.81 us  [exchange(): return lax.ppermute(values, ('gx', 'gy', 'gz'), pairs)]
    pallas_call x7 -> x9, Pallas kernels: 5.31 us -> 6.58 us  [call(): pl.pallas_call(kernel, out_shape=outputs, in_specs=[pl.BlockSpec(memory_s...]
  transfers between devices with their start and end apart: 5 -> 6, of which waited for: 3 -> 3; matrix products, arithmetic and copies ran while one was open for 0% -> 0% of each run, Pallas kernels for 11% -> 13%
where the time goes in v2:
time: 19.5 us; the launch traced here: 19.3 us
  starting transfers between devices  7.81 us (40%)
  Pallas kernels  6.58 us (34%)
  waiting for transfers between devices  4.26 us (22%)
  between operations  0.69 us (4%)
    ppermute x6, starting transfers between devices, exchange(): return lax.ppermute(values, ('gx', 'gy', 'gz'), pairs)  7.81 us
    pallas_call x9, Pallas kernels, call(): pl.pallas_call(kernel, out_shape=outputs, in_specs=[pl.BlockSpec(memory_s...  6.58 us
    ppermute x6, waiting for transfers between devices, exchange(): return lax.ppermute(values, ('gx', 'gy', 'gz'), pairs)  4.26 us
  transfers between devices with their start and end apart: 6, of which 3 were waited for; matrix products, arithmetic and copies ran while one was open for 0% of the time, Pallas kernels for 13%

profile of v2, /device:TPU:19, one launch (start us, length us, event | category | flops | bytes accessed | tf_op | source)
XLA Modules:
  0.0 19.3 jit_solution(5982972074373159978)
XLA Ops:
  0.6 1.9 %stiffness.1 = (f32[3,17,32,128]{3,2,1,0:T(8,128)S(1)}, f32[16,32,128]{2,1,0:T(8,128)S(1)}, f32[16,32,128]{2,1,0:T(8,128)S(1)}, f32[72,128]{1,0:T(8,128)S(1)}) custom-call(f32[16,32,128]{2,1,0:T(8,128)} %r_hbm.1, s32[16,32,128]{2,1,0:T(8,128)} %lab_hbm.1, f32[3,16,32,128]{3,2,1,0:T(8,128)} %fac_hbm.1, f32[4,8,8,8]{3,2,1,0:T(8,128)} %bas_hbm.1, ...), custom_call_target="tpu_custom_call" | custom-call | bytes 6480000 | tf_op jit(solution)/shard_map/stiffness/pallas_call | solution.py:545
  2.5 0.3 %collective-permute-start = (f32[72,128]{1,0:T(8,128)S(1)}, f32[72,128]{1,0:T(8,128)S(1)}, u32[]{:S(2)}, u32[]{:S(2)}) collective-permute-start(f32[72,128]{1,0:T(8,128)S(1)} %get-tuple-element.28.mine_ref), channel_id=1, source_target_pairs={{0,1},{1,0},{2,3},{3,2},{4,5},{5,4},{6,7},{7,6},{8,9},{9,8},{10,11... | collective-permute-start | bytes 110600 | tf_op jit(solution)/shard_map/ppermute | solution.py:570
  2.8 0.1 rows.1
  2.9 1.3 %collective-permute-start.5 = (f32[224,128]{1,0:T(8,128)S(1)}, f32[224,128]{1,0:T(8,128)S(1)}, u32[]{:S(2)}, u32[]{:S(2)}) collective-permute-start(f32[224,128]{1,0:T(8,128)S(1)} %get-tuple-element.45), channel_id=1, source_target_pairs={{0,1},{1,0},{2,3},{3,2},{4,5},{5,4},{6,7},{7,6},{8,9},{9,8},{10,11... | collective-permute-start | bytes 344072 | tf_op jit(solution)/shard_map/ppermute | solution.py:570
  4.2 1.1 %inner.1 = (f32[16,32,128]{2,1,0:T(8,128)S(1)}, f32[16,32,128]{2,1,0:T(8,128)S(1)}, f32[16,32,128]{2,1,0:T(8,128)S(1)}, f32[3,16,32,128]{3,2,1,0:T(8,128)S(1)}) custom-call(f32[3,17,32,128]{3,2,1,0:T(8,128)S(1)} %get-tuple-element.29.kap_ref, f32[16,32,128]{2,1,0:T(8,128)S(1)} %get-tuple-element.30.rr_ref), custom_call_target="tpu_custom_call" | custom-call | bytes 3960000 | tf_op jit(solution)/shard_map/inner/pallas_call | solution.py:545
  5.3 0.0 collective-permute-done.za_ref.urgent_ref
  5.4 1.4 %collective-permute-start.1 = (f32[136,128]{1,0:T(8,128)S(1)}, f32[136,128]{1,0:T(8,128)S(1)}, u32[]{:S(2)}, u32[]{:S(2)}) collective-permute-start(f32[136,128]{1,0:T(8,128)S(1)} %get-tuple-element.34.after_ref.ya_ref), channel_id=1, source_target_pairs={{0,2},{1,3},{2,0},{3,1},{4,6},{5,7},{6,4},{7,5},{8,10},{9,11},{10,... | collective-permute-start | bytes 208904 | tf_op jit(solution)/shard_map/ppermute | solution.py:570
  6.8 0.0 collective-permute-start.2
  6.8 0.4 %columns.1 = (f32[32,128]{1,0:T(8,128)S(1)}, f32[32,128]{1,0:T(8,128)S(1)}) custom-call(f32[3,17,32,128]{3,2,1,0:T(8,128)S(1)} %get-tuple-element.29.kap_ref, f32[16,32,128]{2,1,0:T(8,128)S(1)} %get-tuple-element.30.rr_ref, f32[72,128]{1,0:T(8,128)S(1)} %collective-permute-done.za_ref.urgent_ref, f32[136,128]{1,0:T(8,128)S(1)} %get-tuple-element.34.after_ref.ya_ref), custom_call_target="tpu_custom_call" | custom-call | tf_op jit(solution)/shard_map/columns/pallas_call | solution.py:545
  7.1 1.5 %collective-permute-done.1.ra_ref = f32[136,128]{1,0:T(8,128)S(1)} collective-permute-done((f32[136,128]{1,0:T(8,128)S(1)}, f32[136,128]{1,0:T(8,128)S(1)}, u32[]{:S(2)}, u32[]{:S(2)}) %collective-permute-start.1) | collective-permute-done | bytes 69664 | tf_op jit(solution)/shard_map/ppermute | solution.py:570
  8.6 1.3 %collective-permute-done.2.rb_ref = f32[136,128]{1,0:T(8,128)S(1)} collective-permute-done((f32[136,128]{1,0:T(8,128)S(1)}, f32[136,128]{1,0:T(8,128)S(1)}, u32[]{:S(2)}, u32[]{:S(2)}) %collective-permute-start.2) | collective-permute-done | bytes 69664 | tf_op jit(solution)/shard_map/ppermute | solution.py:570
  9.9 0.3 %columns_more.1 = (f32[56,128]{1,0:T(8,128)S(1)}, f32[56,128]{1,0:T(8,128)S(1)}, f32[40,128]{1,0:T(8,128)S(1)}, f32[40,128]{1,0:T(8,128)S(1)}, f32[4,16,128]{2,1...) custom-call(f32[136,128]{1,0:T(8,128)S(1)} %collective-permute-done.1.ra_ref, ...), custom_call_target="tpu_custom_call" | custom-call | bytes 900000 | tf_op jit(solution)/shard_map/columns_more/pallas_call | solution.py:545
  10.2 3.6 %collective-permute-start.3 = (f32[56,128]{1,0:T(8,128)S(1)}, f32[56,128]{1,0:T(8,128)S(1)}, u32[]{:S(2)}, u32[]{:S(2)}) collective-permute-start(f32[56,128]{1,0:T(8,128)S(1)} %get-tuple-element.38), channel_id=1, source_target_pairs={{0,8},{1,9},{2,10},{3,11},{4,12},{5,13},{6,14},{7,15},{8,0},{9,1},... | collective-permute-start | bytes 86024 | tf_op jit(solution)/shard_map/ppermute | solution.py:570
  13.8 1.2 %collective-permute-start.4 = (f32[56,128]{1,0:T(8,128)S(1)}, f32[56,128]{1,0:T(8,128)S(1)}, u32[]{:S(2)}, u32[]{:S(2)}) collective-permute-start(f32[56,128]{1,0:T(8,128)S(1)} %get-tuple-element.39), channel_id=1, source_target_pairs={{0,24},{1,25},{2,26},{3,27},{4,28},{5,29},{6,30},{7,31},{8,16},{9,... | collective-permute-start | bytes 86024 | tf_op jit(solution)/shard_map/ppermute | solution.py:570
  15.0 0.0 collective-permute-done.5.bulk_ref
  15.0 0.2 %outer.1 = (f32[16,32,128]{2,1,0:T(8,128)S(1)}, f32[16,32,128]{2,1,0:T(8,128)S(1)}) custom-call(f32[3,17,32,128]{3,2,1,0:T(8,128)S(1)} %get-tuple-element.29.kap_ref, f32[16,32,128]{2,1,0:T(8,128)S(1)} %get-tuple-element.30.rr_ref, f32[224,128]{1,0:T(8,128)S(1)} %collective-permute-done.5.bulk_ref, ...), custom_call_target="tpu_custom_call", output_to_operand_aliasing={{0}: (5, {}), {1}: (6, {})} | custom-call | bytes 900000 | tf_op jit(solution)/shard_map/outer/pallas_call | solution.py:545
  15.3 0.4 %edge_rows.1 = (f32[16,32,128]{2,1,0:T(8,128)S(1)}, f32[16,32,128]{2,1,0:T(8,128)S(1)}) custom-call(f32[136,128]{1,0:T(8,128)S(1)} %get-tuple-element.34.after_ref.ya_ref, f32[136,128]{1,0:T(8,128)S(1)} %get-tuple-element.35.yb_ref, f32[136,128]{1,0:T(8,128)S(1)} %get-tuple-element.43.after_ref.lo_ref, ...), custom_call_target="tpu_custom_call", output_to_operand_aliasing={{0}: (4, {}), {1}: (5, {})} | custom-call | bytes 1440000 | tf_op jit(solution)/shard_map/edge_rows/pallas_call | solution.py:545
  15.6 0.0 collective-permute-done.3.ra_ref
  15.7 1.5 %collective-permute-done.4.rb_ref = f32[56,128]{1,0:T(8,128)S(1)} collective-permute-done((f32[56,128]{1,0:T(8,128)S(1)}, f32[56,128]{1,0:T(8,128)S(1)}, u32[]{:S(2)}, u32[]{:S(2)}) %collective-permute-start.4) | collective-permute-done | bytes 28704 | tf_op jit(solution)/shard_map/ppermute | solution.py:570
  17.1 2.2 %last.1 = (f32[16,32,128]{2,1,0:T(8,128)}, f32[2,4,16]{2,1,0:T(4,128)}) custom-call(f32[56,128]{1,0:T(8,128)S(1)} %collective-permute-done.3.ra_ref, f32[56,128]{1,0:T(8,128)S(1)} %collective-permute-done.4.rb_ref, f32[40,128]{1,0:T(8,128)S(1)} %get-tuple-element.40.left_ref, f32[40,128]{1,0:T(8,128)S(1)} %get-tuple-element.41.right_ref, ...), custom_call_target="tpu_custom_call" | custom-call | bytes 7200000 | tf_op jit(solution)/shard_map/last/pallas_call | solution.py:545
  (1 shorter events, 0.0 us)
Async XLA Ops:
  2.5 2.9 %collective-permute-start = (f32[72,128]{1,0:T(8,128)S(1)}, f32[72,128]{1,0:T(8,128)S(1)}, u32[]{:S(2)}, u32[]{:S(2)}) collective-permute-start(f32[72,128]{1,0:T(8,128)S(1)} %get-tuple-element.28.mine_ref), channel_id=1, source_target_pairs={{0,1},{1,0},{2,3},{3,2},{4,5},{5,4},{6,7},{7,6},{8,9},{9,8},{10,11... | collective-permute-start | bytes 110600 | tf_op jit(solution)/shard_map/ppermute | solution.py:570
  2.9 12.1 %collective-permute-start.5 = (f32[224,128]{1,0:T(8,128)S(1)}, f32[224,128]{1,0:T(8,128)S(1)}, u32[]{:S(2)}, u32[]{:S(2)}) collective-permute-start(f32[224,128]{1,0:T(8,128)S(1)} %get-tuple-element.45), channel_id=1, source_target_pairs={{0,1},{1,0},{2,3},{3,2},{4,5},{5,4},{6,7},{7,6},{8,9},{9,8},{10,11... | collective-permute-start | bytes 344072 | tf_op jit(solution)/shard_map/ppermute | solution.py:570
  5.4 3.2 %collective-permute-start.1 = (f32[136,128]{1,0:T(8,128)S(1)}, f32[136,128]{1,0:T(8,128)S(1)}, u32[]{:S(2)}, u32[]{:S(2)}) collective-permute-start(f32[136,128]{1,0:T(8,128)S(1)} %get-tuple-element.34.after_ref.ya_ref), channel_id=1, source_target_pairs={{0,2},{1,3},{2,0},{3,1},{4,6},{5,7},{6,4},{7,5},{8,10},{9,11},{10,... | collective-permute-start | bytes 208904 | tf_op jit(solution)/shard_map/ppermute | solution.py:570
  6.8 3.2 %collective-permute-start.2 = (f32[136,128]{1,0:T(8,128)S(1)}, f32[136,128]{1,0:T(8,128)S(1)}, u32[]{:S(2)}, u32[]{:S(2)}) collective-permute-start(f32[136,128]{1,0:T(8,128)S(1)} %get-tuple-element.35.yb_ref), channel_id=1, source_target_pairs={{0,8},{1,9},{2,4},{3,5},{4,2},{5,3},{6,14},{7,15},{8,0},{9,1},{10,... | collective-permute-start | bytes 208904 | tf_op jit(solution)/shard_map/ppermute | solution.py:570
  10.2 5.5 %collective-permute-start.3 = (f32[56,128]{1,0:T(8,128)S(1)}, f32[56,128]{1,0:T(8,128)S(1)}, u32[]{:S(2)}, u32[]{:S(2)}) collective-permute-start(f32[56,128]{1,0:T(8,128)S(1)} %get-tuple-element.38), channel_id=1, source_target_pairs={{0,8},{1,9},{2,10},{3,11},{4,12},{5,13},{6,14},{7,15},{8,0},{9,1},... | collective-permute-start | bytes 86024 | tf_op jit(solution)/shard_map/ppermute | solution.py:570
  13.8 3.3 %collective-permute-start.4 = (f32[56,128]{1,0:T(8,128)S(1)}, f32[56,128]{1,0:T(8,128)S(1)}, u32[]{:S(2)}, u32[]{:S(2)}) collective-permute-start(f32[56,128]{1,0:T(8,128)S(1)} %get-tuple-element.39), channel_id=1, source_target_pairs={{0,24},{1,25},{2,26},{3,27},{4,28},{5,29},{6,30},{7,31},{8,16},{9,... | collective-permute-start | bytes 86024 | tf_op jit(solution)/shard_map/ppermute | solution.py:570

commit v3 on v2

--- a/solution.py
+++ b/solution.py
@@ -20,17 +20,18 @@
 
 NZ, NY, NX = 16, 32, 128
 CZ, CY, CX = 2, 4, 16
+PARTS = range(2)
 F32 = jnp.float32
 HIGHEST = lax.Precision.HIGHEST
 
 BULK = 7 * NY
-UCOL = 40
-URGENT = UCOL + NY
+URGENT = 16
+ZURGENT = 48
+ZROW = 16
 KROWS = 36
 GROUP = NZ + 2
 RROW = 3 * KROWS
-YCO = 128
-YPAY = YCO + 8
+YPAY = 128
 XPAY = 40 + 16
 RLANE = 110
 
@@ -68,23 +69,24 @@
     lab_ref, fac_ref, bas_ref, bix_ref, tile_ref, sum_ref, sems, more_sems
 ):
     gz = lax.axis_index("gz")
-    halves = []
+    parts = []
     small = [
         pltpu.make_async_copy(bas_hbm, bas_ref, sems.at[0]),
         pltpu.make_async_copy(bix_hbm, bix_ref, sems.at[1]),
     ]
     for copy in small:
         copy.start()
-    for zc in range(CZ):
-        planes = pl.ds(jnp.where(gz == 0, zc * BLK, (CZ - 1 - zc) * BLK), BLK)
-        halves.append(
+    step = NZ // len(PARTS)
+    for part in PARTS:
+        planes = pl.ds(jnp.where(gz == 0, part * step, NZ - step - part * step), step)
+        parts.append(
             [
-                pltpu.make_async_copy(lab_hbm.at[planes], lab_ref.at[planes], more_sems.at[zc, 0]),
-                pltpu.make_async_copy(fac_hbm.at[:, planes], fac_ref.at[:, planes], more_sems.at[zc, 1]),
-                pltpu.make_async_copy(r_hbm.at[planes], rr_ref.at[planes], more_sems.at[zc, 2]),
+                pltpu.make_async_copy(lab_hbm.at[planes], lab_ref.at[planes], more_sems.at[part, 0]),
+                pltpu.make_async_copy(fac_hbm.at[:, planes], fac_ref.at[:, planes], more_sems.at[part, 1]),
+                pltpu.make_async_copy(r_hbm.at[planes], rr_ref.at[planes], more_sems.at[part, 2]),
             ]
         )
-        for copy in halves[zc]:
+        for copy in parts[part]:
             copy.start()
     sum_ref[...] = jnp.zeros(sum_ref.shape, F32)
     kap_ref[:, 0] = jnp.zeros((3, NY, NX), F32)
@@ -109,11 +111,12 @@
             preferred_element_type=F32,
         )
         index = jnp.concatenate([jnp.broadcast_to(index[y : y + 1], (BLK, NX)) for y in range(CY)], axis=0)
-        for copy in halves[zc]:
-            copy.wait()
         sums = [None] * 4
         for i in range(BLK):
             zp = zc * BLK + i
+            if zp % step == 0:
+                for copy in parts[zp // step]:
+                    copy.wait()
             z = jnp.where(gz == 0, zp, NZ - 1 - zp)
             zi = jnp.where(gz == 0, i, BLK - 1 - i)
             mortar = lab_ref[z] == 1
@@ -129,12 +132,8 @@
                 if zp >= NZ - 2:
                     plane = 2 * a + NZ - 1 - zp
                     edges[plane] = k
-                    urgent_ref[plane * 4 : plane * 4 + 2] = k[0:2]
-                    urgent_ref[plane * 4 + 2 : plane * 4 + 4] = k[NY - 2 : NY]
             if zp == NZ - 1:
                 edges[6] = res
-                urgent_ref[24:25] = res[0:1]
-                urgent_ref[25:26] = res[NY - 1 : NY]
             terms.append(basis * res)
             sums = [t if s is None else s + t for s, t in zip(sums, terms)]
         for q in range(4):
@@ -151,13 +150,22 @@
     coarse = bricks[0:8]
     for g in range(1, 8):
         coarse = jnp.where(group == g, bricks[g * 8 : g * 8 + 8], coarse)
-    urgent_ref[26:32] = jnp.zeros((6, NX), F32)
-    urgent_ref[32:40] = coarse
+    urgent_ref[0:8] = coarse
     lane = iota((NY, NX), 1)
     columns = jnp.zeros((NY, NX), F32)
     for g, plane in enumerate(edges):
         columns = jnp.where(lane >= 4 * g, roll(plane, 4 * g + 2, 1), columns)
-    urgent_ref[UCOL:URGENT] = columns
+    lane = iota((8, NX), 1)
+    folded = columns[:8]
+    for i in range(1, NY // 8):
+        folded = jnp.where(lane >= 32 * i, roll(columns[8 * i : 8 * i + 8], 32 * i, 1), folded)
+    urgent_ref[8:16] = folded
+    for g, plane in enumerate(edges[:6]):
+        urgent_ref[ZROW + 4 * g : ZROW + 4 * g + 2] = plane[0:2]
+        urgent_ref[ZROW + 4 * g + 2 : ZROW + 4 * g + 4] = plane[NY - 2 : NY]
+    urgent_ref[ZROW + 24 : ZROW + 25] = edges[6][0:1]
+    urgent_ref[ZROW + 25 : ZROW + 26] = edges[6][NY - 1 : NY]
+    urgent_ref[ZROW + 26 : ZURGENT] = jnp.zeros((6, NX), F32)
 
 
 def place(zp):
@@ -183,87 +191,98 @@
     bulk_ref[6 * NY : 7 * NY] = rr_ref[place(NZ - 1)]
 
 
-def rows_more_kernel(za_ref, mine_ref, ya_in, yb_in, after_ref, ya_ref, yb_ref):
-    even = lax.axis_index("gy") % 2 == 0
-    ya_ref[0:YCO] = ya_in[0:YCO]
-    yb_ref[0:YCO] = yb_in[0:YCO]
-
-    def put(at, low, high):
-        ya_ref[at : at + low.shape[0]] = jnp.where(even, high, low)
-        yb_ref[at : at + low.shape[0]] = jnp.where(even, low, high)
-
-    for a in range(3):
-        for s in range(2):
-            base, at = (2 * a + s) * 4, a * KROWS + NZ + s
-            put(at, za_ref[base + 1 : base + 2], za_ref[base + 2 : base + 3])
-            put(at + GROUP, za_ref[base : base + 1], za_ref[base + 3 : base + 4])
-    put(RROW + NZ, za_ref[24:25], za_ref[25:26])
-    coarse = jnp.concatenate([mine_ref[32 : 32 + CY], za_ref[32 : 32 + CY]], axis=0)
-    ya_ref[YCO : YCO + 8] = coarse
-    yb_ref[YCO : YCO + 8] = coarse
-
-
-def columns_kernel(kap_ref, rr_ref, urgent_ref, after_ref, left_ref, right_ref):
+def columns_kernel(kap_ref, rr_ref, left_ref, right_ref):
     lane = iota((NY, NX), 1)
     left = jnp.zeros((NY, NX), F32)
     right = jnp.zeros((NY, NX), F32)
-    far = urgent_ref[UCOL:URGENT]
     for a in range(3):
-        for zp in range(NZ + 2):
+        for zp in range(NZ):
             at = 2 + a * KROWS + 2 * zp
-            if zp < NZ:
-                moved = roll(kap_ref[a, zp + 1], at, 1)
-            else:
-                moved = roll(far, at - 4 * (2 * a + zp - NZ) - 2, 1)
+            moved = roll(kap_ref[a, zp + 1], at, 1)
             left = jnp.where(lane >= at, moved, left)
             right = jnp.where(lane >= at - 2, moved, right)
-    for zp in range(NZ + 1):
+    for zp in range(NZ):
         at = RLANE + zp
-        moved = roll(rr_ref[place(zp)], at, 1) if zp < NZ else roll(far, at - 26, 1)
+        moved = roll(rr_ref[place(zp)], at, 1)
         left = jnp.where(lane >= at, moved, left)
         right = jnp.where(lane >= at - 1, moved, right)
     left_ref[...] = left
     right_ref[...] = right
 
 
-def columns_more_kernel(
-    ra_ref, rb_ref, yb_ref, left_in, right_in, xa_ref, xb_ref, left_ref, right_ref, cor_ref, lo_ref, hi_ref
-):
+def columns_beyond(left, right, moved):
+    lane = iota(left.shape, 1)
+    for a in range(3):
+        for s in range(2):
+            at = 2 + a * KROWS + 2 * (NZ + s)
+            values = moved(2 * a + s, at)
+            left = jnp.where((lane == at) | (lane == at + 1), values, left)
+            right = jnp.where((lane == at - 2) | (lane == at - 1), values, right)
+    at = RLANE + NZ
+    values = moved(6, at)
+    return jnp.where(lane == at, values, left), jnp.where(lane == at - 1, values, right)
+
+
+def columns_beyond_kernel(left_in, right_in, far_ref, left_ref, right_ref):
+    folded = far_ref[8:16]
+    columns = jnp.concatenate([roll(folded, -32 * i, 1) for i in range(NY // 8)], axis=0)
+    left_ref[...], right_ref[...] = columns_beyond(
+        left_in[...], right_in[...], lambda g, x0: roll(columns, x0 - 4 * g - 2, 1)
+    )
+
+
+def send_rows_kernel(far_ref, mine_ref, left_ref, right_ref, ya_in, yb_in, after_ref, ya_ref, yb_ref, ub_ref):
+    even = lax.axis_index("gy") % 2 == 0
+
+    def put(at, low, high):
+        ya_ref[at : at + 1] = jnp.where(even, high, low)
+        yb_ref[at : at + 1] = jnp.where(even, low, high)
+
+    for a in range(3):
+        for s in range(2):
+            base, at = ZROW + (2 * a + s) * 4, a * KROWS + NZ + s
+            put(at, far_ref[base + 1 : base + 2], far_ref[base + 2 : base + 3])
+            put(at + GROUP, far_ref[base : base + 1], far_ref[base + 3 : base + 4])
+    put(RROW + NZ, far_ref[ZROW + 24 : ZROW + 25], far_ref[ZROW + 25 : ZROW + 26])
+    row = iota((8, NX), 0)
+    folded = far_ref[8:16]
+    corners = jnp.where(row < 2, folded, roll(roll(folded, -96, 1), 4, 0))
+
+    def ends(ref):
+        return jnp.where(row < 2, ref[0:8], roll(ref[NY - 8 : NY], 4, 0))
+
+    left, right = columns_beyond(ends(left_ref), ends(right_ref), lambda g, x0: roll(corners, x0 - 4 * g - 2, 1))
+    low = jnp.where(row < 2, left, roll(right, 2, 0))
+    high = jnp.where(row < 2, roll(left, -2, 0), right)
+    ya_ref[YPAY + 8 :] = jnp.where(even, high, low)
+    ub_ref[8:16] = jnp.where(even, low, high)
+    coarse = jnp.concatenate([mine_ref[0:CY], far_ref[0:CY]], axis=0)
+    ya_ref[YPAY : YPAY + 8] = coarse
+    ub_ref[0:8] = coarse
+
+
+def columns_more_kernel(ra_ref, rb_ref, mine_ref, left_in, right_in, xa_ref, xb_ref, left_ref, right_ref, cor_ref):
     gx, gy = lax.axis_index("gx"), lax.axis_index("gy")
     even = gy % 2 == 0
-    zero = jnp.zeros((YPAY, NX), F32)
-    hi = jnp.where(gy < lax.axis_size("gy") - 1, jnp.where(even, ra_ref[...], rb_ref[...]), zero)
-    lo = jnp.where(gy > 0, jnp.where(even, rb_ref[...], ra_ref[...]), zero)
-    hi_ref[...] = hi
-    lo_ref[...] = lo
-
+    zero = jnp.zeros((URGENT, NX), F32)
+    ra = ra_ref[YPAY:]
+    hi = jnp.where(gy < lax.axis_size("gy") - 1, jnp.where(even, ra, rb_ref[...]), zero)
+    lo = jnp.where(gy > 0, jnp.where(even, rb_ref[...], ra), zero)
     lane, row = iota((8, NX), 1), iota((8, NX), 0)
-    inner = (row == 0) | (row == 7)
-    turned_hi, turned_lo = jnp.transpose(hi[:YCO]), jnp.transpose(lo[:YCO])
-    part = (lane >= KROWS).astype(jnp.int32) + (lane >= 2 * KROWS).astype(jnp.int32)
-    low_k = part * KROWS + ((lane - part * KROWS) >> 1)
-    source = jnp.where(lane < RROW, low_k + jnp.where(inner, GROUP, 0), jnp.where(lane < YCO - 2, lane, 0))
-
-    def column(x):
-        values = jnp.where(
-            row < 4,
-            jnp.broadcast_to(turned_hi[x : x + 1], (8, NX)),
-            jnp.broadcast_to(turned_lo[x : x + 1], (8, NX)),
-        )
-        return jnp.where((row < 2) | (row >= 6), take(values, source), 0.0)
-
-    odd = (lane & 1) == 1
-    more_left = jnp.where(odd & (lane < RROW), column(1), column(0))
-    more_right = jnp.where(odd | (lane >= RROW), column(NX - 1), column(NX - 2))
+
+    def halo(shift):
+        above, below = roll(hi[8:16], -shift, 0), roll(lo[8:16], 6 - shift, 0)
+        return jnp.where(row < 2, above, jnp.where(row >= 6, below, 0.0))
+
     left_ref[0:NY] = left_in[...]
     right_ref[0:NY] = right_in[...]
-    left_ref[NY : NY + 8] = roll(more_left, 2, 1)
-    right_ref[NY : NY + 8] = jnp.where(lane < RROW, more_right, roll(more_right, 1, 1))
+    left_ref[NY : NY + 8] = halo(0)
+    right_ref[NY : NY + 8] = halo(2)
     even_x = gx % 2 == 0
     xa_ref[0:40] = jnp.where(even_x, right_ref[...], left_ref[...])
     xb_ref[0:40] = jnp.where(even_x, left_ref[...], right_ref[...])
 
-    tiles = [lo[YCO:YPAY], yb_ref[YCO:YPAY], hi[YCO:YPAY]]
+    tiles = [lo[0:8], mine_ref[0:8], hi[0:8]]
     zc, xs = lane >> 5, lane & 31
     pair = jnp.where(zc < 2, zc, 3 - zc)
     own = (xs >= 4) & (xs < 20)
@@ -319,7 +338,7 @@
     return (row == 0) | (row == NY - 1) | (lane == 0) | (lane == NX - 1)
 
 
-def inner_kernel(kap_ref, rr_ref, s1_ref, s2_ref, f_ref, p_ref):
+def inner_first_kernel(kap_ref, rr_ref, s1_ref, f_ref, p_ref):
     rim = plane_rim()
     f_ref[0] = jnp.zeros((NY, NX), F32)
     p_ref[:, 0] = jnp.zeros((3, NY, NX), F32)
@@ -330,13 +349,17 @@
             zp = i * 5 + j
             first_plane(zp, zp, kap_ref, rr_ref[place(zp)], f_ref, p_ref, s1_ref, rim)
 
+
+def inner_image_kernel(kap_ref, f_ref, p_ref, s1_in, after_ref, s1_ref, s2_ref):
+    rim = plane_rim()
+
     @pl.loop(0, 2)
     def _(i):
         for j in range(7):
             image_plane(i * 7 + j, i * 7 + j, kap_ref, f_ref, p_ref, s1_ref, s2_ref, rim)
 
 
-def outer_kernel(kap_ref, rr_ref, bulk_ref, f_in, p_in, s1_in, s2_in, after_ref, s1_ref, s2_ref, k_ref, f_ref, p_ref):
+def outer_kernel(kap_ref, rr_ref, bulk_ref, f_in, p_in, s1_in, s2_in, s1_ref, s2_ref, k_ref, f_ref, p_ref):
     rim = plane_rim()
     for a in range(3):
         for i in range(3):
@@ -356,16 +379,21 @@
     return both(values, 1, 1)
 
 
-def edge_rows_kernel(ya_ref, yb_ref, lo_ref, hi_ref, s1_in, s2_in, s1_ref, s2_ref):
+def edge_rows_kernel(ya_ref, yb_ref, ra_ref, rb_ref, s1_in, s2_in, s1_ref, s2_ref):
     even = lax.axis_index("gy") % 2 == 0
     size = 24
     row, lane = iota((size, NX), 0), iota((size, NX), 1)
     inner = (lane > 0) & (lane < NX - 1)
     near = inner & (row < NZ + 1)
     inner16 = inner[:NZ]
+    gy = lax.axis_index("gy")
+    zero = jnp.zeros((YPAY, NX), F32)
+    ya, yb, ra, rb = ya_ref[0:YPAY], yb_ref[...], ra_ref[0:YPAY], rb_ref[...]
+    hi = jnp.where(gy < lax.axis_size("gy") - 1, jnp.where(even, ra, rb), zero)
+    lo = jnp.where(gy > 0, jnp.where(even, rb, ra), zero)
     for other, mine, face, second in (
-        (lo_ref, jnp.where(even, yb_ref[...], ya_ref[...]), 0, 1),
-        (hi_ref, jnp.where(even, ya_ref[...], yb_ref[...]), NY - 1, NY - 2),
+        (lo, jnp.where(even, yb, ya), 0, 1),
+        (hi, jnp.where(even, ya, yb), NY - 1, NY - 2),
     ):
 
         def group(source, at):
@@ -374,7 +402,7 @@
         k = [[group(other, a * KROWS + s * GROUP) for a in range(3)] for s in (0, 1)]
         k += [[group(mine, a * KROWS + s * GROUP) for a in range(3)] for s in (1, 0)]
         parts = [pair_stiffness(v, (None, None, None), [both(u, 1, 0) for u in v]) for v in k]
-        res = [None, other[RROW : RROW + size], mine[RROW : RROW + size]]
+        res = [None] + [jnp.where(row < NZ + 1, v[YPAY - size :], 0.0) for v in (roll(other, 4 - 8, 0), roll(mine, 4 - 8, 0))]
         f, inv = [None] * 3, [None] * 3
         for c in (1, 2):
             diag = SELF * (k[c][0] + k[c][1] + k[c][2]) + parts[c][0] + parts[c - 1][1] + parts[c + 1][1]
@@ -499,7 +527,7 @@
 
 
 def last_kernel(
-    ra_ref, rb_ref, left_ref, right_ref, cor_ref, s1_ref, s2_ref, sel_ref, out_hbm, est_ref, out_ref, sems
+    rb_ref, ra_ref, left_ref, right_ref, cor_ref, s1_ref, s2_ref, sel_ref, out_hbm, est_hbm, out_ref, est_ref, sems
 ):
     gx, gz = lax.axis_index("gx"), lax.axis_index("gz")
     even = gx % 2 == 0
@@ -516,11 +544,13 @@
     estimate = coarse_solve(cor_ref, left[40:XPAY], right[40:XPAY])
     lane8 = iota((8, NX), 1)
     rim = (lane < 2) | (lane >= NX - 2)
-    copies = []
     step = 4
     for zc in range(CZ):
         z_out = jnp.where(gz == 0, zc, CZ - 1 - zc)
         est_ref[z_out] = roll(estimate, -(zc * 32 + 4), 1)[4:8, 0:CX]
+    copies = [pltpu.make_async_copy(est_ref, est_hbm, sems.at[NZ // step])]
+    copies[0].start()
+    for zc in range(CZ):
         wide = take(estimate, zc * 32 + 4 + (lane8 >> 3))
         fine = jnp.concatenate([jnp.broadcast_to(wide[4 + y : 5 + y], (BLK, NX)) for y in range(CY)], axis=0)
         for i in range(BLK):
@@ -549,7 +579,7 @@
         out_specs=[pl.BlockSpec(memory_space=v) for v in out_spaces or [pltpu.VMEM] * len(outputs)],
         scratch_shapes=list(scratch),
         input_output_aliases=aliases or {},
-        cost_estimate=pl.CostEstimate(flops=0, bytes_accessed=int(us * 3.6e6), transcendentals=0),
+        cost_estimate=pl.CostEstimate(flops=int(us * 1e9), bytes_accessed=0, transcendentals=0),
         compiler_params=pltpu.CompilerParams(vmem_limit_bytes=32 * 2**20),
         name=name,
     )(*inputs)
@@ -592,7 +622,7 @@
         kap, rr, sel, urgent = call(
             first_kernel,
             [pltpu.with_memory_space_constraint(v, pltpu.HBM) for v in inputs],
-            [vmem(3, NZ + 1, NY, NX), vmem(NZ, NY, NX), vmem(NZ, NY, NX), vmem(URGENT, NX)],
+            [vmem(3, NZ + 1, NY, NX), vmem(NZ, NY, NX), vmem(NZ, NY, NX), vmem(ZURGENT, NX)],
             [
                 pltpu.VMEM(labels.shape, jnp.int32),
                 pltpu.VMEM(factor.shape, F32),
@@ -601,7 +631,7 @@
                 pltpu.VMEM((4, BLK, BLK, NX), F32),
                 pltpu.VMEM((64, NX), F32),
                 pltpu.SemaphoreType.DMA((2,)),
-                pltpu.SemaphoreType.DMA((CZ, 3)),
+                pltpu.SemaphoreType.DMA((len(PARTS), 3)),
             ],
             us=1.8,
             name="stiffness",
@@ -609,36 +639,49 @@
         )
         kap, rr, sel, urgent = near(kap), near(rr), near(sel), near(urgent)
         zu = near(swap_z(urgent))
-        ya, yb, bulk = call(rows_kernel, [kap, rr], [vmem(YPAY, NX), vmem(YPAY, NX), vmem(BULK, NX)], name="rows")
-        za = near(swap_z(near(bulk)))
-        s1, s2, f, p = call(
-            inner_kernel,
+        ya, yb, bulk = call(rows_kernel, [kap, rr], [vmem(YPAY + URGENT, NX), vmem(YPAY, NX), vmem(BULK, NX)], name="rows")
+        zb = near(swap_z(near(bulk)))
+        left, right = call(columns_kernel, [kap, rr], [vmem(NY, NX), vmem(NY, NX)], us=0.4, name="columns")
+        left, right = near(left), near(right)
+        s1, f, p = call(
+            inner_first_kernel,
             [kap, rr],
-            [vmem(NZ, NY, NX), vmem(NZ, NY, NX), vmem(NZ, NY, NX), vmem(3, NZ, NY, NX)],
-            us=1.1,
-            name="inner",
-        )
-        ya, yb = call(
-            rows_more_kernel,
-            [zu, urgent, near(ya), near(yb), near(s1)],
-            [vmem(YPAY, NX), vmem(YPAY, NX)],
-            name="rows_more",
-        )
-        ya, yb = near(ya), near(yb)
-        ra, rb = near(swap_y(ya, 0)), near(swap_y(yb, 1))
-        left, right = call(columns_kernel, [kap, rr, zu, ya], [vmem(NY, NX), vmem(NY, NX)], us=0.0, name="columns")
-        xa, xb, left, right, cor, lo, hi = call(
+            [vmem(NZ, NY, NX), vmem(NZ, NY, NX), vmem(3, NZ, NY, NX)],
+            us=0.6,
+            name="inner_first",
+        )
+        s1, f, p = near(s1), near(f), near(p)
+        ya, yb, ub = call(
+            send_rows_kernel,
+            [zu, urgent, left, right, near(ya), near(yb), f],
+            [vmem(YPAY + URGENT, NX), vmem(YPAY, NX), vmem(URGENT, NX)],
+            aliases={4: 0, 5: 1},
+            us=10.0,
+            name="send_rows",
+        )
+        ya, yb, ub = near(ya), near(yb), near(ub)
+        wa, rb, wb = near(swap_y(ya, 0)), near(swap_y(ub, 1)), near(swap_y(yb, 1))
+        left, right = call(columns_beyond_kernel, [left, right, zu], [vmem(NY, NX), vmem(NY, NX)], us=100.0, name="columns_beyond")
+        xa, xb, left, right, cor = call(
             columns_more_kernel,
-            [ra, rb, yb, near(left), near(right)],
-            [vmem(XPAY, NX), vmem(XPAY, NX), vmem(40, NX), vmem(40, NX), vmem(4, 16, NX), vmem(YPAY, NX), vmem(YPAY, NX)],
-            us=0.25,
+            [wa, rb, ub, near(left), near(right)],
+            [vmem(XPAY, NX), vmem(XPAY, NX), vmem(40, NX), vmem(40, NX), vmem(4, 16, NX)],
+            us=1.0,
             name="columns_more",
         )
         xa, xb = near(xa), near(xb)
-        wb, wa = near(swap_x(xb, 1)), near(swap_x(xa, 0))
+        vb, va = near(swap_x(xb, 1)), near(swap_x(xa, 0))
+        s1, s2 = call(
+            inner_image_kernel,
+            [kap, f, p, s1, xa],
+            [vmem(NZ, NY, NX), vmem(NZ, NY, NX)],
+            aliases={3: 0},
+            us=0.6,
+            name="inner_image",
+        )
         s1, s2 = call(
             outer_kernel,
-            [kap, rr, za, near(f), near(p), near(s1), near(s2), near(lo)],
+            [kap, rr, zb, f, p, near(s1), near(s2)],
             [vmem(NZ, NY, NX), vmem(NZ, NY, NX)],
             [pltpu.VMEM((3, 5, NY, NX), F32), pltpu.VMEM((4, NY, NX), F32), pltpu.VMEM((3, 4, NY, NX), F32)],
             aliases={5: 0, 6: 1},
@@ -647,7 +690,7 @@
         )
         s1, s2 = call(
             edge_rows_kernel,
-            [ya, yb, near(lo), near(hi), near(s1), near(s2)],
+            [ya, yb, wa, wb, near(s1), near(s2)],
             [vmem(NZ, NY, NX), vmem(NZ, NY, NX)],
             aliases={4: 0, 5: 1},
             us=0.4,
@@ -655,12 +698,12 @@
         )
         out, estimate = call(
             last_kernel,
-            [wa, wb, near(left), near(right), near(cor), near(s1), near(s2), sel],
+            [vb, va, near(left), near(right), near(cor), near(s1), near(s2), sel],
             [jax.ShapeDtypeStruct((NZ, NY, NX), F32), jax.ShapeDtypeStruct((CZ, CY, CX), F32)],
-            [pltpu.VMEM((NZ, NY, NX), F32), pltpu.SemaphoreType.DMA((4,))],
-            us=2.0,
+            [pltpu.VMEM((NZ, NY, NX), F32), pltpu.VMEM((CZ, CY, CX), F32), pltpu.SemaphoreType.DMA((5,))],
+            us=1.5,
             name="last",
-            out_spaces=[pltpu.HBM, pltpu.VMEM],
+            out_spaces=[pltpu.HBM, pltpu.HBM],
         )
         return out, estimate
 

time: 19.5 us -> 17.8 us (0.913)
  waiting for transfers between devices: 4.26 us -> 1.76 us
  starting transfers between devices: 7.81 us -> 9.06 us
  Pallas kernels: 6.58 us -> 6.16 us
    ppermute x6 -> x7, waiting for transfers between devices: 4.26 us -> 1.76 us  [exchange(): return lax.ppermute(values, ('gx', 'gy', 'gz'), pairs)]
    ppermute x6 -> x7, starting transfers between devices: 7.81 us -> 9.06 us  [exchange(): return lax.ppermute(values, ('gx', 'gy', 'gz'), pairs)]
    pallas_call x9 -> x11, Pallas kernels: 6.58 us -> 6.16 us  [call(): pl.pallas_call(kernel, out_shape=outputs, in_specs=[pl.BlockSpec(memory_s...]
  transfers between devices with their start and end apart: 6 -> 7, of which waited for: 3 -> 3; matrix products, arithmetic and copies ran while one was open for 0% -> 0% of each run, Pallas kernels for 13% -> 15%
where the time goes in v3:
time: 17.8 us; the launch traced here: 17.7 us
  starting transfers between devices  9.06 us (51%)
  Pallas kernels  6.16 us (35%)
  waiting for transfers between devices  1.76 us (10%)
  between operations  0.71 us (4%)
    ppermute x7, starting transfers between devices, exchange(): return lax.ppermute(values, ('gx', 'gy', 'gz'), pairs)  9.06 us
    pallas_call x11, Pallas kernels, call(): pl.pallas_call(kernel, out_shape=outputs, in_specs=[pl.BlockSpec(memory_s...  6.16 us
    ppermute x7, waiting for transfers between devices, exchange(): return lax.ppermute(values, ('gx', 'gy', 'gz'), pairs)  1.76 us
  transfers between devices with their start and end apart: 7, of which 3 were waited for; matrix products, arithmetic and copies ran while one was open for 0% of the time, Pallas kernels for 15%

profile of v3, /device:TPU:19, one launch (start us, length us, event | category | flops | bytes accessed | tf_op | source)
XLA Modules:
  0.0 17.7 jit_solution(10201598849866091510)
XLA Ops:
  0.6 1.8 %stiffness.1 = (f32[3,17,32,128]{3,2,1,0:T(8,128)S(1)}, f32[16,32,128]{2,1,0:T(8,128)S(1)}, f32[16,32,128]{2,1,0:T(8,128)S(1)}, f32[48,128]{1,0:T(8,128)S(1)}) custom-call(f32[16,32,128]{2,1,0:T(8,128)} %r_hbm.1, s32[16,32,128]{2,1,0:T(8,128)} %lab_hbm.1, f32[3,16,32,128]{3,2,1,0:T(8,128)} %fac_hbm.1, f32[4,8,8,8]{3,2,1,0:T(8,128)} %bas_hbm.1, ...), custom_call_target="tpu_custom_call" | custom-call | flops 1800000000 | tf_op jit(solution)/shard_map/stiffness/pallas_call | solution.py:575
  2.5 0.3 %collective-permute-start = (f32[48,128]{1,0:T(8,128)S(1)}, f32[48,128]{1,0:T(8,128)S(1)}, u32[]{:S(2)}, u32[]{:S(2)}) collective-permute-start(f32[48,128]{1,0:T(8,128)S(1)} %get-tuple-element.30.mine_ref), channel_id=1, source_target_pairs={{0,1},{1,0},{2,3},{3,2},{4,5},{5,4},{6,7},{7,6},{8,9},{9,8},{10,11... | collective-permute-start | bytes 73736 | tf_op jit(solution)/shard_map/ppermute | solution.py:600
  2.8 0.1 rows.1
  2.9 1.3 %collective-permute-start.6 = (f32[224,128]{1,0:T(8,128)S(1)}, f32[224,128]{1,0:T(8,128)S(1)}, u32[]{:S(2)}, u32[]{:S(2)}) collective-permute-start(f32[224,128]{1,0:T(8,128)S(1)} %get-tuple-element.48), channel_id=1, source_target_pairs={{0,1},{1,0},{2,3},{3,2},{4,5},{5,4},{6,7},{7,6},{8,9},{9,8},{10,11... | collective-permute-start | bytes 344072 | tf_op jit(solution)/shard_map/ppermute | solution.py:600
  4.2 0.4 %inner_first.1 = (f32[16,32,128]{2,1,0:T(8,128)S(1)}, f32[16,32,128]{2,1,0:T(8,128)S(1)}, f32[3,16,32,128]{3,2,1,0:T(8,128)S(1)}) custom-call(f32[3,17,32,128]{3,2,1,0:T(8,128)S(1)} %get-tuple-element.31.kap_ref, f32[16,32,128]{2,1,0:T(8,128)S(1)} %get-tuple-element.32.rr_ref), custom_call_target="tpu_custom_call" | custom-call | flops 600000000 | tf_op jit(solution)/shard_map/inner_first/pallas_call | solution.py:575
  4.6 0.3 %columns.1 = (f32[32,128]{1,0:T(8,128)S(1)}, f32[32,128]{1,0:T(8,128)S(1)}) custom-call(f32[3,17,32,128]{3,2,1,0:T(8,128)S(1)} %get-tuple-element.31.kap_ref, f32[16,32,128]{2,1,0:T(8,128)S(1)} %get-tuple-element.32.rr_ref), custom_call_target="tpu_custom_call" | custom-call | flops 400000000 | tf_op jit(solution)/shard_map/columns/pallas_call | solution.py:575
  5.0 0.3 %collective-permute-done.far_ref = f32[48,128]{1,0:T(8,128)S(1)} collective-permute-done((f32[48,128]{1,0:T(8,128)S(1)}, f32[48,128]{1,0:T(8,128)S(1)}, u32[]{:S(2)}, u32[]{:S(2)}) %collective-permute-start) | collective-permute-done | bytes 24608 | tf_op jit(solution)/shard_map/ppermute | solution.py:600
  5.2 0.1 send_rows.1
  5.4 1.3 %collective-permute-start.1 = (f32[144,128]{1,0:T(8,128)S(1)}, f32[144,128]{1,0:T(8,128)S(1)}, u32[]{:S(2)}, u32[]{:S(2)}) collective-permute-start(f32[144,128]{1,0:T(8,128)S(1)} %get-tuple-element.38.ya_ref), channel_id=1, source_target_pairs={{0,2},{1,3},{2,0},{3,1},{4,6},{5,7},{6,4},{7,5},{8,10},{9,11},{10,... | collective-permute-start | bytes 221192 | tf_op jit(solution)/shard_map/ppermute | solution.py:600
  6.7 0.0 collective-permute-start.2
  6.7 1.5 %collective-permute-start.5 = (f32[128,128]{1,0:T(8,128)S(1)}, f32[128,128]{1,0:T(8,128)S(1)}, u32[]{:S(2)}, u32[]{:S(2)}) collective-permute-start(f32[128,128]{1,0:T(8,128)S(1)} %get-tuple-element.47.yb_ref), channel_id=1, source_target_pairs={{0,8},{1,9},{2,4},{3,5},{4,2},{5,3},{6,14},{7,15},{8,0},{9,1},{10,... | collective-permute-start | bytes 196616 | tf_op jit(solution)/shard_map/ppermute | solution.py:600
  8.2 0.2 columns_beyond.1
  8.3 0.9 %collective-permute-done.2.rb_ref = f32[16,128]{1,0:T(8,128)S(1)} collective-permute-done((f32[16,128]{1,0:T(8,128)S(1)}, f32[16,128]{1,0:T(8,128)S(1)}, u32[]{:S(2)}, u32[]{:S(2)}) %collective-permute-start.2) | collective-permute-done | bytes 8224 | tf_op jit(solution)/shard_map/ppermute | solution.py:600
  9.2 0.2 columns_more.1
  9.4 4.7 %collective-permute-start.3 = (f32[56,128]{1,0:T(8,128)S(1)}, f32[56,128]{1,0:T(8,128)S(1)}, u32[]{:S(2)}, u32[]{:S(2)}) collective-permute-start(f32[56,128]{1,0:T(8,128)S(1)} %get-tuple-element.42), channel_id=1, source_target_pairs={{0,24},{1,25},{2,26},{3,27},{4,28},{5,29},{6,30},{7,31},{8,16},{9,... | collective-permute-start | bytes 86024 | tf_op jit(solution)/shard_map/ppermute | solution.py:600
  14.1 0.0 collective-permute-start.4
  14.1 0.7 %inner_image.1 = (f32[16,32,128]{2,1,0:T(8,128)S(1)}, f32[16,32,128]{2,1,0:T(8,128)S(1)}) custom-call(f32[3,17,32,128]{3,2,1,0:T(8,128)S(1)} %get-tuple-element.31.kap_ref, f32[16,32,128]{2,1,0:T(8,128)S(1)} %get-tuple-element.37.after_ref.f_ref.f_in, f32[3,16,32,128]{3,2,1,0:T(8,128)S(1)} %get-tuple-element.49.p_ref.p_in, ...), custom_call_target="tpu_custom_call", output_to_operand_aliasing={{0}: (3, {})} | custom-call | flops 600000000 | tf_op jit(solution)/shard_map/inner_image/pallas_call | solution.py:575
  14.7 0.0 collective-permute-done.6.bulk_ref
  14.7 0.3 %outer.1 = (f32[16,32,128]{2,1,0:T(8,128)S(1)}, f32[16,32,128]{2,1,0:T(8,128)S(1)}) custom-call(f32[3,17,32,128]{3,2,1,0:T(8,128)S(1)} %get-tuple-element.31.kap_ref, f32[16,32,128]{2,1,0:T(8,128)S(1)} %get-tuple-element.32.rr_ref, f32[224,128]{1,0:T(8,128)S(1)} %collective-permute-done.6.bulk_ref, ...), custom_call_target="tpu_custom_call", output_to_operand_aliasing={{0}: (5, {}), {1}: (6, {})} | custom-call | flops 250000000 | tf_op jit(solution)/shard_map/outer/pallas_call | solution.py:575
  15.0 0.0 collective-permute-done.5.rb_ref
  15.0 0.4 %edge_rows.1 = (f32[16,32,128]{2,1,0:T(8,128)S(1)}, f32[16,32,128]{2,1,0:T(8,128)S(1)}) custom-call(f32[144,128]{1,0:T(8,128)S(1)} %get-tuple-element.38.ya_ref, f32[128,128]{1,0:T(8,128)S(1)} %get-tuple-element.47.yb_ref, f32[144,128]{1,0:T(8,128)S(1)} %collective-permute-done.1.ra_ref, ...), custom_call_target="tpu_custom_call", output_to_operand_aliasing={{0}: (4, {}), {1}: (5, {})} | custom-call | flops 400000000 | tf_op jit(solution)/shard_map/edge_rows/pallas_call | solution.py:575
  15.4 0.6 %collective-permute-done.3.rb_ref = f32[56,128]{1,0:T(8,128)S(1)} collective-permute-done((f32[56,128]{1,0:T(8,128)S(1)}, f32[56,128]{1,0:T(8,128)S(1)}, u32[]{:S(2)}, u32[]{:S(2)}) %collective-permute-start.3) | collective-permute-done | bytes 28704 | tf_op jit(solution)/shard_map/ppermute | solution.py:600
  16.1 0.0 collective-permute-done.4.ra_ref
  16.1 1.6 %last.1 = (f32[16,32,128]{2,1,0:T(8,128)}, f32[2,4,16]{2,1,0:T(4,128)}) custom-call(f32[56,128]{1,0:T(8,128)S(1)} %collective-permute-done.3.rb_ref, f32[56,128]{1,0:T(8,128)S(1)} %collective-permute-done.4.ra_ref, f32[40,128]{1,0:T(8,128)S(1)} %get-tuple-element.44.left_ref, f32[40,128]{1,0:T(8,128)S(1)} %get-tuple-element.45.right_ref, ...), custom_call_target="tpu_custom_call" | custom-call | flops 1500000000 | tf_op jit(solution)/shard_map/last/pallas_call | solution.py:575
  (1 shorter events, 0.0 us)
Async XLA Ops:
  2.5 2.7 %collective-permute-start = (f32[48,128]{1,0:T(8,128)S(1)}, f32[48,128]{1,0:T(8,128)S(1)}, u32[]{:S(2)}, u32[]{:S(2)}) collective-permute-start(f32[48,128]{1,0:T(8,128)S(1)} %get-tuple-element.30.mine_ref), channel_id=1, source_target_pairs={{0,1},{1,0},{2,3},{3,2},{4,5},{5,4},{6,7},{7,6},{8,9},{9,8},{10,11... | collective-permute-start | bytes 73736 | tf_op jit(solution)/shard_map/ppermute | solution.py:600
  2.9 11.8 %collective-permute-start.6 = (f32[224,128]{1,0:T(8,128)S(1)}, f32[224,128]{1,0:T(8,128)S(1)}, u32[]{:S(2)}, u32[]{:S(2)}) collective-permute-start(f32[224,128]{1,0:T(8,128)S(1)} %get-tuple-element.48), channel_id=1, source_target_pairs={{0,1},{1,0},{2,3},{3,2},{4,5},{5,4},{6,7},{7,6},{8,9},{9,8},{10,11... | collective-permute-start | bytes 344072 | tf_op jit(solution)/shard_map/ppermute | solution.py:600
  5.4 3.8 %collective-permute-start.1 = (f32[144,128]{1,0:T(8,128)S(1)}, f32[144,128]{1,0:T(8,128)S(1)}, u32[]{:S(2)}, u32[]{:S(2)}) collective-permute-start(f32[144,128]{1,0:T(8,128)S(1)} %get-tuple-element.38.ya_ref), channel_id=1, source_target_pairs={{0,2},{1,3},{2,0},{3,1},{4,6},{5,7},{6,4},{7,5},{8,10},{9,11},{10,... | collective-permute-start | bytes 221192 | tf_op jit(solution)/shard_map/ppermute | solution.py:600
  6.7 2.5 %collective-permute-start.2 = (f32[16,128]{1,0:T(8,128)S(1)}, f32[16,128]{1,0:T(8,128)S(1)}, u32[]{:S(2)}, u32[]{:S(2)}) collective-permute-start(f32[16,128]{1,0:T(8,128)S(1)} %get-tuple-element.39.mine_ref), channel_id=1, source_target_pairs={{0,8},{1,9},{2,4},{3,5},{4,2},{5,3},{6,14},{7,15},{8,0},{9,1},{10,... | collective-permute-start | bytes 24584 | tf_op jit(solution)/shard_map/ppermute | solution.py:600
  6.7 8.3 %collective-permute-start.5 = (f32[128,128]{1,0:T(8,128)S(1)}, f32[128,128]{1,0:T(8,128)S(1)}, u32[]{:S(2)}, u32[]{:S(2)}) collective-permute-start(f32[128,128]{1,0:T(8,128)S(1)} %get-tuple-element.47.yb_ref), channel_id=1, source_target_pairs={{0,8},{1,9},{2,4},{3,5},{4,2},{5,3},{6,14},{7,15},{8,0},{9,1},{10,... | collective-permute-start | bytes 196616 | tf_op jit(solution)/shard_map/ppermute | solution.py:600
  9.4 6.7 %collective-permute-start.3 = (f32[56,128]{1,0:T(8,128)S(1)}, f32[56,128]{1,0:T(8,128)S(1)}, u32[]{:S(2)}, u32[]{:S(2)}) collective-permute-start(f32[56,128]{1,0:T(8,128)S(1)} %get-tuple-element.42), channel_id=1, source_target_pairs={{0,24},{1,25},{2,26},{3,27},{4,28},{5,29},{6,30},{7,31},{8,16},{9,... | collective-permute-start | bytes 86024 | tf_op jit(solution)/shard_map/ppermute | solution.py:600
  14.1 2.0 %collective-permute-start.4 = (f32[56,128]{1,0:T(8,128)S(1)}, f32[56,128]{1,0:T(8,128)S(1)}, u32[]{:S(2)}, u32[]{:S(2)}) collective-permute-start(f32[56,128]{1,0:T(8,128)S(1)} %get-tuple-element.43.after_ref), channel_id=1, source_target_pairs={{0,8},{1,9},{2,10},{3,11},{4,12},{5,13},{6,14},{7,15},{8,0},{9,1},... | collective-permute-start | bytes 86024 | tf_op jit(solution)/shard_map/ppermute | solution.py:600

commit v4 on v3

--- a/solution.py
+++ b/solution.py
@@ -440,37 +440,60 @@
         s2_ref[:, second, :] = s2_ref[:, second, :] + jnp.where(inner16, scaled * total, 0.0)
 
 
-def slab_terms(mine, other, left):
-    rows = NY + 8
+def slab_lanes(left):
     lane = iota((8, NX), 1)
     zp, c = lane >> 2, lane & 3
-    real = zp < NZ + 2
     outer = c < 2 if left else c >= 2
+    real = zp < GROUP
+    near = ((c == 1) | (c == 2)) & (zp < NZ + 1)
     offset = jnp.where(outer, 0, 2) if left else jnp.where(outer, 2, 0)
-    near = ((c == 1) | (c == 2)) & (zp < NZ + 1)
     offset_r = jnp.where(outer, RLANE - 1, RLANE) if left else jnp.where(outer, RLANE, RLANE - 1)
-    at_r = jnp.where(near, zp + offset_r, 0)
-    at_k = [jnp.where(real, a * KROWS + 2 * zp + (c & 1) + offset, 0) for a in range(3)]
-
-    def spread(at, keep):
+    sources = [jnp.where(real, a * KROWS + 2 * zp + (c & 1) + offset, 0) for a in range(3)]
+    sources.append(jnp.where(near, zp + offset_r, 0))
+    return outer, [real] * 3 + [near], sources
+
+
+def slab_kernel(left_ref, right_ref, after_ref, slab_ref):
+    for side, pack in enumerate((left_ref, right_ref)):
+        outer, keeps, sources = slab_lanes(side == 0)
+        for q in range(4):
+            for i in range(0, NY + 8, 8):
+                piece = take(pack[i : i + 8], sources[q])
+                slab_ref[side, q, i : i + 8] = jnp.where(keeps[q] & ~outer, piece, 0.0)
+
+
+def rim_kernel(s1_ref, s2_ref, rim1_ref, rim2_ref):
+    lane = iota((NY, NX), 1)
+    for source, rim in ((s1_ref, rim1_ref), (s2_ref, rim2_ref)):
+        values = jnp.zeros((NY, NX), F32)
+        for zp in range(NZ):
+            values = jnp.where(lane >= 4 * zp, roll(source[zp], 4 * zp + 2, 1), values)
+        rim[...] = values
+
+
+def slab_terms(mine, other, rim1, rim2, left):
+    rows = NY + 8
+    outer, keeps, sources = slab_lanes(left)
+
+    def spread(q):
         pieces = []
         for i in range(0, rows, 8):
-            piece = jnp.where(outer, take(other[i : i + 8], at), take(mine[i : i + 8], at))
-            pieces.append(jnp.where(keep, piece, 0.0))
+            pieces.append(jnp.where(keeps[q] & outer, take(other[i : i + 8], sources[q]), mine[q, i : i + 8]))
         return jnp.concatenate(pieces, axis=0)
 
-    k = [spread(at, real) for at in at_k]
-    res = spread(at_r, near)
-    near = jnp.concatenate([near] * (rows // 8), axis=0)
-    face = c == 2 if left else c == 1
-    face = jnp.concatenate([face] * (rows // 8), axis=0)
+    k = [spread(a) for a in range(3)]
+    res = spread(3)
+    c = iota((rows, NX), 1) & 3
+    near = jnp.concatenate([keeps[3]] * (rows // 8), axis=0)
 
     dz = [both(v, 4, 1) for v in k]
     part_0, part_y, part_x, part_yx = pair_stiffness(k, (None, None, None), dz)
     diag = SELF * (k[0] + k[1] + k[2]) + part_0 + both(part_y, 1, 0)
-    diag = diag + both(part_x + both(part_yx, 1, 0), 1, 1)
-    inv = 1.0 / diag
+    inv = 1.0 / (diag + both(part_x + both(part_yx, 1, 0), 1, 1))
     f = jnp.where(near, WEIGHT_ONE * res * inv, 0.0)
+
+    def from_outer(values):
+        return roll(values, 1 if left else -1, 1)
 
     p = [v * f for v in k]
     d0, d1, d2 = (both(v, 4, 1) for v in p)
@@ -478,16 +501,16 @@
     own_yx = 0.125 * (p[1] + p[2]) + (1.0 / 24.0) * (d0 + d1 + d2)
     own_x = 0.5 * p[2] + 0.125 * (d0 + d2)
     fz = both(f, 4, 1)
-    fy, fyz = both(f, 1, 0), both(fz, 1, 0)
+    fy, fyz = both(f, 1, 0)[:NY], both(fz, 1, 0)[:NY]
+    fc, fz = f[:NY], fz[:NY]
+    k = [v[:NY] for v in k]
     t24, t8 = (1.0 / 24.0) * fyz, 0.125 * fyz
-    total = 0.5 * d0 + both(own_y, 1, 0) + both(own_x + both(own_yx, 1, 0), 1, 1)
-    total = total + k[0] * (0.5 * fz + t8 + both(0.125 * fz + t24, 1, 1))
-    total = total + k[1] * (0.5 * fy + t8 + both(0.125 * fy + t24, 1, 1))
-    total = total + k[2] * both(0.5 * f + 0.125 * (fz + fy) + t24, 1, 1)
-    scaled = WEIGHT_TWO * inv
-    times = jnp.where(face, scaled, total)
-    plus = jnp.where(face, KEEP * f + scaled * total, 0.0)
-    return times[:NY], plus[:NY]
+    total = 0.5 * d0[:NY] + both(own_y, 1, 0)[:NY] + from_outer(own_x[:NY] + both(own_yx, 1, 0)[:NY])
+    total = total + k[0] * (0.5 * fz + t8 + from_outer(0.125 * fz + t24))
+    total = total + k[1] * (0.5 * fy + t8 + from_outer(0.125 * fy + t24))
+    total = total + k[2] * from_outer(0.5 * fc + 0.125 * (fz + fy) + t24)
+    face = (c == 2 if left else c == 1)[:NY]
+    return jnp.where(face, KEEP * fc + WEIGHT_TWO * inv[:NY] * (total + rim1), rim2 + rim1 * total)
 
 
 def coarse_solve(cor_ref, lower, upper):
@@ -501,45 +524,42 @@
 
     def sides(values, axis):
         if axis == 0:
-            return (
-                jnp.where(lane >= 32, roll(values, 32, 1), 0.0),
-                jnp.where(lane < 96, roll(values, -32, 1), 0.0),
-            )
-        if axis == 1:
-            return roll(values, 1, 0), roll(values, -1, 0)
-        return roll(values, 1, 1), roll(values, -1, 1)
-
-    couple = [[0.5 * (kc[a] + v) for v in sides(kc[a], a)] for a in range(3)]
-    diag = (MASS / 3.0) * (kc[0] + kc[1] + kc[2])
+            return roll(values, 32, 1), roll(values, -32, 1)
+        return roll(values, 1, axis - 1), roll(values, -1, axis - 1)
+
+    within = [(lane >= 32, lane < 96), (None, None), (None, None)]
+    diag = (1.0 + MASS / 3.0) * (kc[0] + kc[1] + kc[2])
+    couple = []
     for a in range(3):
-        diag = diag + (couple[a][0] + couple[a][1])
+        for v, real in zip(sides(kc[a], a), within[a]):
+            half = 0.5 * v if real is None else jnp.where(real, 0.5 * v, 0.0)
+            diag = diag + half
+            half = 0.5 * kc[a] + half
+            couple.append(half if real is None else jnp.where(real, half, 0.0))
     inside = kc[0] > 0.0
     scaled = jnp.where(inside, OMEGA / jnp.where(inside, diag, 1.0), 0.0)
-    estimate = scaled * rhs
+    couple = [scaled * v for v in couple]
+    start = scaled * rhs
+    estimate = start
     for _ in range(CITERS - 1):
-        off = None
-        for a in range(3):
-            low, high = sides(estimate, a)
-            term = couple[a][0] * low + couple[a][1] * high
-            off = term if off is None else off + term
-        estimate = estimate + scaled * (rhs - (diag * estimate - off))
+        t = [v * u for v, u in zip(couple, [u for a in range(3) for u in sides(estimate, a)])]
+        estimate = (start + (1.0 - OMEGA) * estimate) + (((t[0] + t[1]) + (t[2] + t[3])) + (t[4] + t[5]))
     return estimate[0:8]
 
 
 def last_kernel(
-    rb_ref, ra_ref, left_ref, right_ref, cor_ref, s1_ref, s2_ref, sel_ref, out_hbm, est_hbm, out_ref, est_ref, sems
+    rb_ref, ra_ref, slab_ref, cor_ref, rim1_ref, rim2_ref, s2_ref, sel_ref, out_hbm, est_hbm, out_ref, est_ref, sems
 ):
     gx, gz = lax.axis_index("gx"), lax.axis_index("gz")
     even = gx % 2 == 0
     zero = jnp.zeros((XPAY, NX), F32)
     right = jnp.where(gx < lax.axis_size("gx") - 1, jnp.where(even, ra_ref[...], rb_ref[...]), zero)
     left = jnp.where(gx > 0, jnp.where(even, rb_ref[...], ra_ref[...]), zero)
-    left_times, left_plus = slab_terms(left_ref[...], left[:40], True)
-    right_times, right_plus = slab_terms(right_ref[...], right[:40], False)
+    rim1, rim2 = rim1_ref[...], rim2_ref[...]
+    from_left = slab_terms(slab_ref[0], left[:40], rim1, rim2, True)
+    from_right = slab_terms(slab_ref[1], right[:40], rim1, rim2, False)
     lane = iota((NY, NX), 1)
-    low_side = (lane & 3) < 2
-    times = jnp.where(low_side, right_times, left_times)
-    plus = jnp.where(low_side, right_plus, left_plus)
+    faces = jnp.where((lane & 3) < 2, from_right, from_left)
 
     estimate = coarse_solve(cor_ref, left[40:XPAY], right[40:XPAY])
     lane8 = iota((8, NX), 1)
@@ -556,9 +576,7 @@
         for i in range(BLK):
             zp = zc * BLK + i
             z = jnp.where(gz == 0, zp, NZ - 1 - zp)
-            x_times = jnp.where(rim, roll(times, -(4 * zp + 2), 1), 0.0)
-            x_plus = jnp.where(rim, roll(plus, -(4 * zp + 2), 1), 0.0)
-            out_ref[z] = s2_ref[zp] + x_plus + s1_ref[zp] * x_times + sel_ref[z] * fine
+            out_ref[z] = jnp.where(rim, roll(faces, -(4 * zp + 2), 1), s2_ref[zp]) + sel_ref[z] * fine
             if zp % step == step - 1:
                 planes = pl.ds(jnp.where(gz == 0, zp + 1 - step, NZ - 1 - zp), step)
                 copies.append(pltpu.make_async_copy(out_ref.at[planes], out_hbm.at[planes], sems.at[zp // step]))
@@ -696,9 +714,11 @@
             us=0.4,
             name="edge_rows",
         )
+        (slab,) = call(slab_kernel, [near(left), near(right), xa], [vmem(2, 4, 40, NX)], us=0.1, name="slab")
+        rim1, rim2 = call(rim_kernel, [near(s1), near(s2)], [vmem(NY, NX), vmem(NY, NX)], us=0.2, name="rim")
         out, estimate = call(
             last_kernel,
-            [vb, va, near(left), near(right), near(cor), near(s1), near(s2), sel],
+            [vb, va, near(slab), near(cor), near(rim1), near(rim2), near(s2), sel],
             [jax.ShapeDtypeStruct((NZ, NY, NX), F32), jax.ShapeDtypeStruct((CZ, CY, CX), F32)],
             [pltpu.VMEM((NZ, NY, NX), F32), pltpu.VMEM((CZ, CY, CX), F32), pltpu.SemaphoreType.DMA((5,))],
             us=1.5,

time: 17.8 us -> 17.6 us (0.989)
  waiting for transfers between devices: 1.76 us -> 1.42 us
    ppermute x7, waiting for transfers between devices: 1.76 us -> 1.42 us  [exchange(): return lax.ppermute(values, ('gx', 'gy', 'gz'), pairs)]
    pallas_call x11 -> x13, Pallas kernels: 6.16 us -> 6.25 us  [call(): pl.pallas_call(kernel, out_shape=outputs, in_specs=[pl.BlockSpec(memory_s...]
  transfers between devices with their start and end apart: 7 -> 7, of which waited for: 3 -> 3; matrix products, arithmetic and copies ran while one was open for 0% -> 0% of each run, Pallas kernels for 15% -> 17%
where the time goes in v4:
time: 17.6 us; the launch traced here: 17.4 us
  starting transfers between devices  9.06 us (51%)
  Pallas kernels  6.25 us (36%)
  waiting for transfers between devices  1.42 us (8%)
  between operations  0.72 us (4%)
    ppermute x7, starting transfers between devices, exchange(): return lax.ppermute(values, ('gx', 'gy', 'gz'), pairs)  9.06 us
    pallas_call x13, Pallas kernels, call(): pl.pallas_call(kernel, out_shape=outputs, in_specs=[pl.BlockSpec(memory_s...  6.25 us
    ppermute x7, waiting for transfers between devices, exchange(): return lax.ppermute(values, ('gx', 'gy', 'gz'), pairs)  1.42 us
  transfers between devices with their start and end apart: 7, of which 3 were waited for; matrix products, arithmetic and copies ran while one was open for 0% of the time, Pallas kernels for 17%

profile of v4, /device:TPU:19, one launch (start us, length us, event | category | flops | bytes accessed | tf_op | source)
XLA Modules:
  0.0 17.4 jit_solution(8636718223575993820)
XLA Ops:
  0.6 1.8 %stiffness.1 = (f32[3,17,32,128]{3,2,1,0:T(8,128)S(1)}, f32[16,32,128]{2,1,0:T(8,128)S(1)}, f32[16,32,128]{2,1,0:T(8,128)S(1)}, f32[48,128]{1,0:T(8,128)S(1)}) custom-call(f32[16,32,128]{2,1,0:T(8,128)} %r_hbm.1, s32[16,32,128]{2,1,0:T(8,128)} %lab_hbm.1, f32[3,16,32,128]{3,2,1,0:T(8,128)} %fac_hbm.1, f32[4,8,8,8]{3,2,1,0:T(8,128)} %bas_hbm.1, ...), custom_call_target="tpu_custom_call" | custom-call | flops 1800000000 | tf_op jit(solution)/shard_map/stiffness/pallas_call | solution.py:593
  2.5 0.3 %collective-permute-start = (f32[48,128]{1,0:T(8,128)S(1)}, f32[48,128]{1,0:T(8,128)S(1)}, u32[]{:S(2)}, u32[]{:S(2)}) collective-permute-start(f32[48,128]{1,0:T(8,128)S(1)} %get-tuple-element.32.mine_ref), channel_id=1, source_target_pairs={{0,1},{1,0},{2,3},{3,2},{4,5},{5,4},{6,7},{7,6},{8,9},{9,8},{10,11... | collective-permute-start | bytes 73736 | tf_op jit(solution)/shard_map/ppermute | solution.py:618
  2.8 0.1 rows.1
  2.9 1.3 %collective-permute-start.6 = (f32[224,128]{1,0:T(8,128)S(1)}, f32[224,128]{1,0:T(8,128)S(1)}, u32[]{:S(2)}, u32[]{:S(2)}) collective-permute-start(f32[224,128]{1,0:T(8,128)S(1)} %get-tuple-element.50), channel_id=1, source_target_pairs={{0,1},{1,0},{2,3},{3,2},{4,5},{5,4},{6,7},{7,6},{8,9},{9,8},{10,11... | collective-permute-start | bytes 344072 | tf_op jit(solution)/shard_map/ppermute | solution.py:618
  4.2 0.4 %inner_first.1 = (f32[16,32,128]{2,1,0:T(8,128)S(1)}, f32[16,32,128]{2,1,0:T(8,128)S(1)}, f32[3,16,32,128]{3,2,1,0:T(8,128)S(1)}) custom-call(f32[3,17,32,128]{3,2,1,0:T(8,128)S(1)} %get-tuple-element.33.kap_ref, f32[16,32,128]{2,1,0:T(8,128)S(1)} %get-tuple-element.34.rr_ref), custom_call_target="tpu_custom_call" | custom-call | flops 600000000 | tf_op jit(solution)/shard_map/inner_first/pallas_call | solution.py:593
  4.6 0.3 %columns.1 = (f32[32,128]{1,0:T(8,128)S(1)}, f32[32,128]{1,0:T(8,128)S(1)}) custom-call(f32[3,17,32,128]{3,2,1,0:T(8,128)S(1)} %get-tuple-element.33.kap_ref, f32[16,32,128]{2,1,0:T(8,128)S(1)} %get-tuple-element.34.rr_ref), custom_call_target="tpu_custom_call" | custom-call | flops 400000000 | tf_op jit(solution)/shard_map/columns/pallas_call | solution.py:593
  5.0 0.3 %collective-permute-done.far_ref = f32[48,128]{1,0:T(8,128)S(1)} collective-permute-done((f32[48,128]{1,0:T(8,128)S(1)}, f32[48,128]{1,0:T(8,128)S(1)}, u32[]{:S(2)}, u32[]{:S(2)}) %collective-permute-start) | collective-permute-done | bytes 24608 | tf_op jit(solution)/shard_map/ppermute | solution.py:618
  5.2 0.1 send_rows.1
  5.4 1.3 %collective-permute-start.1 = (f32[144,128]{1,0:T(8,128)S(1)}, f32[144,128]{1,0:T(8,128)S(1)}, u32[]{:S(2)}, u32[]{:S(2)}) collective-permute-start(f32[144,128]{1,0:T(8,128)S(1)} %get-tuple-element.40.ya_ref), channel_id=1, source_target_pairs={{0,2},{1,3},{2,0},{3,1},{4,6},{5,7},{6,4},{7,5},{8,10},{9,11},{10,... | collective-permute-start | bytes 221192 | tf_op jit(solution)/shard_map/ppermute | solution.py:618
  6.7 0.0 collective-permute-start.2
  6.7 1.5 %collective-permute-start.5 = (f32[128,128]{1,0:T(8,128)S(1)}, f32[128,128]{1,0:T(8,128)S(1)}, u32[]{:S(2)}, u32[]{:S(2)}) collective-permute-start(f32[128,128]{1,0:T(8,128)S(1)} %get-tuple-element.49.yb_ref), channel_id=1, source_target_pairs={{0,8},{1,9},{2,4},{3,5},{4,2},{5,3},{6,14},{7,15},{8,0},{9,1},{10,... | collective-permute-start | bytes 196616 | tf_op jit(solution)/shard_map/ppermute | solution.py:618
  8.2 0.2 columns_beyond.1
  8.3 0.9 %collective-permute-done.2.rb_ref = f32[16,128]{1,0:T(8,128)S(1)} collective-permute-done((f32[16,128]{1,0:T(8,128)S(1)}, f32[16,128]{1,0:T(8,128)S(1)}, u32[]{:S(2)}, u32[]{:S(2)}) %collective-permute-start.2) | collective-permute-done | bytes 8224 | tf_op jit(solution)/shard_map/ppermute | solution.py:618
  9.2 0.2 %columns_more.1 = (f32[56,128]{1,0:T(8,128)S(1)}, f32[56,128]{1,0:T(8,128)S(1)}, f32[40,128]{1,0:T(8,128)S(1)}, f32[40,128]{1,0:T(8,128)S(1)}, f32[4,16,128]{2,1,0:T(8,128)S(1)}) custom-call(f32[144,128]{1,0:T(8,128)S(1)} %collective-permute-done.1.ra_ref, f32[16,128]{1,0:T(8,128)S(1)} %collective-permute-done.2.rb_ref, ...), custom_call_target="tpu_custom_call" | custom-call | flops 1000000000 | tf_op jit(solution)/shard_map/columns_more/pallas_call | solution.py:593
  9.4 4.7 %collective-permute-start.3 = (f32[56,128]{1,0:T(8,128)S(1)}, f32[56,128]{1,0:T(8,128)S(1)}, u32[]{:S(2)}, u32[]{:S(2)}) collective-permute-start(f32[56,128]{1,0:T(8,128)S(1)} %get-tuple-element.44), channel_id=1, source_target_pairs={{0,24},{1,25},{2,26},{3,27},{4,28},{5,29},{6,30},{7,31},{8,16},{9,... | collective-permute-start | bytes 86024 | tf_op jit(solution)/shard_map/ppermute | solution.py:618
  14.1 0.0 collective-permute-start.4
  14.1 0.1 slab.1.slab_ref
  14.2 0.7 %inner_image.1 = (f32[16,32,128]{2,1,0:T(8,128)S(1)}, f32[16,32,128]{2,1,0:T(8,128)S(1)}) custom-call(f32[3,17,32,128]{3,2,1,0:T(8,128)S(1)} %get-tuple-element.33.kap_ref, f32[16,32,128]{2,1,0:T(8,128)S(1)} %get-tuple-element.39.after_ref.f_ref.f_in, f32[3,16,32,128]{3,2,1,0:T(8,128)S(1)} %get-tuple-element.51.p_ref.p_in, ...), custom_call_target="tpu_custom_call", output_to_operand_aliasing={{0}: (3, {})} | custom-call | flops 600000000 | tf_op jit(solution)/shard_map/inner_image/pallas_call | solution.py:593
  14.9 0.0 collective-permute-done.6.bulk_ref
  14.9 0.3 %outer.1 = (f32[16,32,128]{2,1,0:T(8,128)S(1)}, f32[16,32,128]{2,1,0:T(8,128)S(1)}) custom-call(f32[3,17,32,128]{3,2,1,0:T(8,128)S(1)} %get-tuple-element.33.kap_ref, f32[16,32,128]{2,1,0:T(8,128)S(1)} %get-tuple-element.34.rr_ref, f32[224,128]{1,0:T(8,128)S(1)} %collective-permute-done.6.bulk_ref, ...), custom_call_target="tpu_custom_call", output_to_operand_aliasing={{0}: (5, {}), {1}: (6, {})} | custom-call | flops 250000000 | tf_op jit(solution)/shard_map/outer/pallas_call | solution.py:593
  15.2 0.4 %edge_rows.1 = (f32[16,32,128]{2,1,0:T(8,128)S(1)}, f32[16,32,128]{2,1,0:T(8,128)S(1)}) custom-call(f32[144,128]{1,0:T(8,128)S(1)} %get-tuple-element.40.ya_ref, f32[128,128]{1,0:T(8,128)S(1)} %get-tuple-element.49.yb_ref, f32[144,128]{1,0:T(8,128)S(1)} %collective-permute-done.1.ra_ref, ...), custom_call_target="tpu_custom_call", output_to_operand_aliasing={{0}: (4, {}), {1}: (5, {})} | custom-call | flops 400000000 | tf_op jit(solution)/shard_map/edge_rows/pallas_call | solution.py:593
  15.6 0.2 %rim.1 = (f32[32,128]{1,0:T(8,128)S(1)}, f32[32,128]{1,0:T(8,128)S(1)}) custom-call(f32[16,32,128]{2,1,0:T(8,128)S(1)} %get-tuple-element.57.s1_ref, f32[16,32,128]{2,1,0:T(8,128)S(1)} %get-tuple-element.58.s2_ref), custom_call_target="tpu_custom_call" | custom-call | flops 200000000 | tf_op jit(solution)/shard_map/rim/pallas_call | solution.py:593
  15.8 0.3 %collective-permute-done.3.rb_ref = f32[56,128]{1,0:T(8,128)S(1)} collective-permute-done((f32[56,128]{1,0:T(8,128)S(1)}, f32[56,128]{1,0:T(8,128)S(1)}, u32[]{:S(2)}, u32[]{:S(2)}) %collective-permute-start.3) | collective-permute-done | bytes 28704 | tf_op jit(solution)/shard_map/ppermute | solution.py:618
  16.1 1.4 %last.1 = (f32[16,32,128]{2,1,0:T(8,128)}, f32[2,4,16]{2,1,0:T(4,128)}) custom-call(f32[56,128]{1,0:T(8,128)S(1)} %collective-permute-done.3.rb_ref, f32[56,128]{1,0:T(8,128)S(1)} %collective-permute-done.4.ra_ref, f32[2,4,40,128]{3,2,1,0:T(8,128)S(1)} %slab.1.slab_ref, f32[4,16,128]{2,1,0:T(8,128)S(1)} %get-tuple-element.48.cor_ref, ...), custom_call_target="tpu_custom_call" | custom-call | flops 1500000000 | tf_op jit(solution)/shard_map/last/pallas_call | solution.py:593
  (3 shorter events, 0.0 us)
Async XLA Ops:
  2.5 2.7 %collective-permute-start = (f32[48,128]{1,0:T(8,128)S(1)}, f32[48,128]{1,0:T(8,128)S(1)}, u32[]{:S(2)}, u32[]{:S(2)}) collective-permute-start(f32[48,128]{1,0:T(8,128)S(1)} %get-tuple-element.32.mine_ref), channel_id=1, source_target_pairs={{0,1},{1,0},{2,3},{3,2},{4,5},{5,4},{6,7},{7,6},{8,9},{9,8},{10,11... | collective-permute-start | bytes 73736 | tf_op jit(solution)/shard_map/ppermute | solution.py:618
  2.9 12.0 %collective-permute-start.6 = (f32[224,128]{1,0:T(8,128)S(1)}, f32[224,128]{1,0:T(8,128)S(1)}, u32[]{:S(2)}, u32[]{:S(2)}) collective-permute-start(f32[224,128]{1,0:T(8,128)S(1)} %get-tuple-element.50), channel_id=1, source_target_pairs={{0,1},{1,0},{2,3},{3,2},{4,5},{5,4},{6,7},{7,6},{8,9},{9,8},{10,11... | collective-permute-start | bytes 344072 | tf_op jit(solution)/shard_map/ppermute | solution.py:618
  5.4 3.8 %collective-permute-start.1 = (f32[144,128]{1,0:T(8,128)S(1)}, f32[144,128]{1,0:T(8,128)S(1)}, u32[]{:S(2)}, u32[]{:S(2)}) collective-permute-start(f32[144,128]{1,0:T(8,128)S(1)} %get-tuple-element.40.ya_ref), channel_id=1, source_target_pairs={{0,2},{1,3},{2,0},{3,1},{4,6},{5,7},{6,4},{7,5},{8,10},{9,11},{10,... | collective-permute-start | bytes 221192 | tf_op jit(solution)/shard_map/ppermute | solution.py:618
  6.7 2.5 %collective-permute-start.2 = (f32[16,128]{1,0:T(8,128)S(1)}, f32[16,128]{1,0:T(8,128)S(1)}, u32[]{:S(2)}, u32[]{:S(2)}) collective-permute-start(f32[16,128]{1,0:T(8,128)S(1)} %get-tuple-element.41.mine_ref), channel_id=1, source_target_pairs={{0,8},{1,9},{2,4},{3,5},{4,2},{5,3},{6,14},{7,15},{8,0},{9,1},{10,... | collective-permute-start | bytes 24584 | tf_op jit(solution)/shard_map/ppermute | solution.py:618
  6.7 8.4 %collective-permute-start.5 = (f32[128,128]{1,0:T(8,128)S(1)}, f32[128,128]{1,0:T(8,128)S(1)}, u32[]{:S(2)}, u32[]{:S(2)}) collective-permute-start(f32[128,128]{1,0:T(8,128)S(1)} %get-tuple-element.49.yb_ref), channel_id=1, source_target_pairs={{0,8},{1,9},{2,4},{3,5},{4,2},{5,3},{6,14},{7,15},{8,0},{9,1},{10,... | collective-permute-start | bytes 196616 | tf_op jit(solution)/shard_map/ppermute | solution.py:618
  9.4 6.7 %collective-permute-start.3 = (f32[56,128]{1,0:T(8,128)S(1)}, f32[56,128]{1,0:T(8,128)S(1)}, u32[]{:S(2)}, u32[]{:S(2)}) collective-permute-start(f32[56,128]{1,0:T(8,128)S(1)} %get-tuple-element.44), channel_id=1, source_target_pairs={{0,24},{1,25},{2,26},{3,27},{4,28},{5,29},{6,30},{7,31},{8,16},{9,... | collective-permute-start | bytes 86024 | tf_op jit(solution)/shard_map/ppermute | solution.py:618
  14.1 2.0 %collective-permute-start.4 = (f32[56,128]{1,0:T(8,128)S(1)}, f32[56,128]{1,0:T(8,128)S(1)}, u32[]{:S(2)}, u32[]{:S(2)}) collective-permute-start(f32[56,128]{1,0:T(8,128)S(1)} %get-tuple-element.45.after_ref), channel_id=1, source_target_pairs={{0,8},{1,9},{2,10},{3,11},{4,12},{5,13},{6,14},{7,15},{8,0},{9,1},... | collective-permute-start | bytes 86024 | tf_op jit(solution)/shard_map/ppermute | solution.py:618

commit v5 on v4

--- a/solution.py
+++ b/solution.py
@@ -24,10 +24,10 @@
 F32 = jnp.float32
 HIGHEST = lax.Precision.HIGHEST
 
-BULK = 7 * NY
+BULK = 7 * NY + 24
+BCOL, BROW = 7 * NY, 7 * NY + 8
 URGENT = 16
-ZURGENT = 48
-ZROW = 16
+ZURGENT = 32
 KROWS = 36
 GROUP = NZ + 2
 RROW = 3 * KROWS
@@ -88,7 +88,6 @@
         )
         for copy in parts[part]:
             copy.start()
-    sum_ref[...] = jnp.zeros(sum_ref.shape, F32)
     kap_ref[:, 0] = jnp.zeros((3, NY, NX), F32)
     for copy in small:
         copy.wait()
@@ -102,6 +101,7 @@
     tile_ref[...] = tiled.reshape(4, BLK, BLK, NX)
     edges = [None] * 7
     spread = ((iota((CX, NX), 1) >> 3) == iota((CX, NX), 0)).astype(F32)
+    indices = []
     for zc in range(CZ):
         index = lax.dot_general(
             bix_ref[jnp.where(gz == 0, zc, CZ - 1 - zc)].astype(F32),
@@ -110,7 +110,9 @@
             precision=HIGHEST,
             preferred_element_type=F32,
         )
-        index = jnp.concatenate([jnp.broadcast_to(index[y : y + 1], (BLK, NX)) for y in range(CY)], axis=0)
+        indices.append(jnp.concatenate([jnp.broadcast_to(index[y : y + 1], (BLK, NX)) for y in range(CY)], axis=0))
+    for zc in range(CZ):
+        index = indices[zc]
         sums = [None] * 4
         for i in range(BLK):
             zp = zc * BLK + i
@@ -138,34 +140,46 @@
             sums = [t if s is None else s + t for s, t in zip(sums, terms)]
         for q in range(4):
             total = sums[q].reshape(CY, BLK, NX).sum(axis=1)
-            sum_ref[(q * 2 + zc) * 8 : (q * 2 + zc) * 8 + CY] = total if q == 3 else total * (1.0 / BLK**3)
-    bricks = lax.dot_general(
-        sum_ref[...],
-        ((iota((NX, NX), 0) >> 3) == (iota((NX, NX), 1) & (CX - 1))).astype(F32),
-        (((1,), (0,)), ((), ())),
-        precision=HIGHEST,
-        preferred_element_type=F32,
-    )
+            total = total if q == 3 else total * (1.0 / BLK**3)
+            at = (q * 2 + zc) * 8
+            sum_ref[at : at + CY] = total
+            sum_ref[at + CY : at + 8] = total
+    gather = ((iota((NX, NX), 0) >> 3) == (iota((NX, NX), 1) & (CX - 1))).astype(jnp.bfloat16)
+    rest, bricks = sum_ref[...], None
+    for _ in range(3):
+        part = rest.astype(jnp.bfloat16)
+        rest = rest - part.astype(F32)
+        term = lax.dot_general(part, gather, (((1,), (0,)), ((), ())), preferred_element_type=F32)
+        bricks = term if bricks is None else bricks + term
     group = iota((8, NX), 1) >> 4
     coarse = bricks[0:8]
     for g in range(1, 8):
         coarse = jnp.where(group == g, bricks[g * 8 : g * 8 + 8], coarse)
     urgent_ref[0:8] = coarse
-    lane = iota((NY, NX), 1)
-    columns = jnp.zeros((NY, NX), F32)
+    even = lax.axis_index("gy") % 2 == 0
+    row = iota((8, NX), 0)
+
+    def ends(plane):
+        return jnp.where(row < 4, plane[:8], plane[NY - 8 :])
+
+    left, right = columns_beyond(
+        jnp.zeros((8, NX), F32), jnp.zeros((8, NX), F32), lambda g, x0: roll(ends(edges[g]), x0, 1)
+    )
+    urgent_ref[8:16] = end_tile(left, right)
     for g, plane in enumerate(edges):
-        columns = jnp.where(lane >= 4 * g, roll(plane, 4 * g + 2, 1), columns)
-    lane = iota((8, NX), 1)
-    folded = columns[:8]
-    for i in range(1, NY // 8):
-        folded = jnp.where(lane >= 32 * i, roll(columns[8 * i : 8 * i + 8], 32 * i, 1), folded)
-    urgent_ref[8:16] = folded
-    for g, plane in enumerate(edges[:6]):
-        urgent_ref[ZROW + 4 * g : ZROW + 4 * g + 2] = plane[0:2]
-        urgent_ref[ZROW + 4 * g + 2 : ZROW + 4 * g + 4] = plane[NY - 2 : NY]
-    urgent_ref[ZROW + 24 : ZROW + 25] = edges[6][0:1]
-    urgent_ref[ZROW + 25 : ZROW + 26] = edges[6][NY - 1 : NY]
-    urgent_ref[ZROW + 26 : ZURGENT] = jnp.zeros((6, NX), F32)
+        a, beyond = divmod(g, 2)
+        for inner in range(2) if g < 6 else (1,):
+            at = 12 if g == 6 else 4 * a + 2 * inner + beyond
+            low = plane[0:1] if inner else plane[1:2]
+            high = plane[NY - 1 : NY] if inner else plane[NY - 2 : NY - 1]
+            urgent_ref[16 + at : 17 + at] = jnp.where(even, high, low)
+
+
+def end_tile(left, right):
+    row = iota((8, NX), 0)
+    low = jnp.where(row < 2, left, roll(right, 2, 0))
+    high = jnp.where(row < 6, roll(left, -2, 0), right)
+    return jnp.where(row < 4, low, high)
 
 
 def place(zp):
@@ -189,9 +203,27 @@
         for s in range(2):
             bulk_ref[(2 * a + s) * NY : (2 * a + s + 1) * NY] = kap_ref[a, NZ - s]
     bulk_ref[6 * NY : 7 * NY] = rr_ref[place(NZ - 1)]
-
-
-def columns_kernel(kap_ref, rr_ref, left_ref, right_ref):
+    planes = [kap_ref[a, NZ - s] for a in range(3) for s in range(2)] + [rr_ref[place(NZ - 1)]]
+    lane = iota((NY, NX), 1)
+    columns = jnp.zeros((NY, NX), F32)
+    for g, plane in enumerate(planes):
+        columns = jnp.where(lane >= 4 * g, roll(plane, 4 * g + 2, 1), columns)
+    lane = iota((8, NX), 1)
+    folded = columns[:8]
+    for i in range(1, NY // 8):
+        folded = jnp.where(lane >= 32 * i, roll(columns[8 * i : 8 * i + 8], 32 * i, 1), folded)
+    bulk_ref[BCOL:BROW] = folded
+    bulk_ref[BROW:BULK] = jnp.zeros((16, NX), F32)
+    for g, plane in enumerate(planes):
+        a, beyond = divmod(g, 2)
+        for inner in range(2) if g < 6 else (1,):
+            at = BROW + (12 if g == 6 else 4 * a + 2 * inner + beyond)
+            low = plane[0:1] if inner else plane[1:2]
+            high = plane[NY - 1 : NY] if inner else plane[NY - 2 : NY - 1]
+            bulk_ref[at : at + 1] = jnp.where(even, low, high)
+
+
+def columns_kernel(kap_ref, rr_ref, left_ref, right_ref, ends_ref):
     lane = iota((NY, NX), 1)
     left = jnp.zeros((NY, NX), F32)
     right = jnp.zeros((NY, NX), F32)
@@ -208,6 +240,8 @@
         right = jnp.where(lane >= at - 1, moved, right)
     left_ref[...] = left
     right_ref[...] = right
+    row = iota((8, NX), 0)
+    ends_ref[...] = end_tile(*(jnp.where(row < 4, v[:8], v[NY - 8 :]) for v in (left, right)))
 
 
 def columns_beyond(left, right, moved):
@@ -223,40 +257,35 @@
     return jnp.where(lane == at, values, left), jnp.where(lane == at - 1, values, right)
 
 
-def columns_beyond_kernel(left_in, right_in, far_ref, left_ref, right_ref):
-    folded = far_ref[8:16]
+def insert_rows(y_ref, far_ref, at):
+    for i in range(6):
+        y_ref[i * GROUP + NZ : (i + 1) * GROUP] = far_ref[at + 2 * i : at + 2 * i + 2]
+    y_ref[RROW + NZ : RROW + NZ + 1] = far_ref[at + 12 : at + 13]
+
+
+def columns_beyond_kernel(left_in, right_in, bulk_ref, yb_in, after_ref, left_ref, right_ref, yb_ref):
+    folded = bulk_ref[BCOL:BROW]
     columns = jnp.concatenate([roll(folded, -32 * i, 1) for i in range(NY // 8)], axis=0)
     left_ref[...], right_ref[...] = columns_beyond(
         left_in[...], right_in[...], lambda g, x0: roll(columns, x0 - 4 * g - 2, 1)
     )
-
-
-def send_rows_kernel(far_ref, mine_ref, left_ref, right_ref, ya_in, yb_in, after_ref, ya_ref, yb_ref, ub_ref):
+    insert_rows(yb_ref, bulk_ref, BROW)
+
+
+def send_rows_kernel(far_ref, mine_ref, ends_ref, ya_in, after_ref, ya_ref, ub_ref):
     even = lax.axis_index("gy") % 2 == 0
-
-    def put(at, low, high):
-        ya_ref[at : at + 1] = jnp.where(even, high, low)
-        yb_ref[at : at + 1] = jnp.where(even, low, high)
-
-    for a in range(3):
-        for s in range(2):
-            base, at = ZROW + (2 * a + s) * 4, a * KROWS + NZ + s
-            put(at, far_ref[base + 1 : base + 2], far_ref[base + 2 : base + 3])
-            put(at + GROUP, far_ref[base : base + 1], far_ref[base + 3 : base + 4])
-    put(RROW + NZ, far_ref[ZROW + 24 : ZROW + 25], far_ref[ZROW + 25 : ZROW + 26])
-    row = iota((8, NX), 0)
-    folded = far_ref[8:16]
-    corners = jnp.where(row < 2, folded, roll(roll(folded, -96, 1), 4, 0))
-
-    def ends(ref):
-        return jnp.where(row < 2, ref[0:8], roll(ref[NY - 8 : NY], 4, 0))
-
-    left, right = columns_beyond(ends(left_ref), ends(right_ref), lambda g, x0: roll(corners, x0 - 4 * g - 2, 1))
-    low = jnp.where(row < 2, left, roll(right, 2, 0))
-    high = jnp.where(row < 2, roll(left, -2, 0), right)
-    ya_ref[YPAY + 8 :] = jnp.where(even, high, low)
-    ub_ref[8:16] = jnp.where(even, low, high)
-    coarse = jnp.concatenate([mine_ref[0:CY], far_ref[0:CY]], axis=0)
+    row, lane = iota((8, NX), 0), iota((8, NX), 1)
+    insert_rows(ya_ref, far_ref, 16)
+    is_right = ((row >> 1) & 1) == 1
+    at = lane - jnp.where(is_right, 0, 2)
+    within = at - jnp.where(at >= 2 * KROWS, 2 * KROWS, jnp.where(at >= KROWS, KROWS, 0))
+    beyond = (at < RROW) & (within >= 2 * NZ)
+    beyond = beyond | (lane == RLANE + NZ - is_right.astype(jnp.int32))
+    tile = jnp.where(beyond, far_ref[8:16], ends_ref[...])
+    turned = roll(tile, 4, 0)
+    ya_ref[YPAY + 8 :] = jnp.where(even, turned, tile)
+    ub_ref[8:16] = jnp.where(even, tile, turned)
+    coarse = jnp.where(row < CY, mine_ref[0:8], far_ref[0:8])
     ya_ref[YPAY : YPAY + 8] = coarse
     ub_ref[0:8] = coarse
 
@@ -659,8 +688,9 @@
         zu = near(swap_z(urgent))
         ya, yb, bulk = call(rows_kernel, [kap, rr], [vmem(YPAY + URGENT, NX), vmem(YPAY, NX), vmem(BULK, NX)], name="rows")
         zb = near(swap_z(near(bulk)))
-        left, right = call(columns_kernel, [kap, rr], [vmem(NY, NX), vmem(NY, NX)], us=0.4, name="columns")
-        left, right = near(left), near(right)
+        left, right, ends = call(
+            columns_kernel, [kap, rr], [vmem(NY, NX), vmem(NY, NX), vmem(8, NX)], us=0.4, name="columns"
+        )
         s1, f, p = call(
             inner_first_kernel,
             [kap, rr],
@@ -669,17 +699,26 @@
             name="inner_first",
         )
         s1, f, p = near(s1), near(f), near(p)
-        ya, yb, ub = call(
+        ya, ub = call(
             send_rows_kernel,
-            [zu, urgent, left, right, near(ya), near(yb), f],
-            [vmem(YPAY + URGENT, NX), vmem(YPAY, NX), vmem(URGENT, NX)],
-            aliases={4: 0, 5: 1},
+            [zu, urgent, near(ends), near(ya), f],
+            [vmem(YPAY + URGENT, NX), vmem(URGENT, NX)],
+            aliases={3: 0},
             us=10.0,
             name="send_rows",
         )
-        ya, yb, ub = near(ya), near(yb), near(ub)
-        wa, rb, wb = near(swap_y(ya, 0)), near(swap_y(ub, 1)), near(swap_y(yb, 1))
-        left, right = call(columns_beyond_kernel, [left, right, zu], [vmem(NY, NX), vmem(NY, NX)], us=100.0, name="columns_beyond")
+        ya, ub = near(ya), near(ub)
+        wa, rb = near(swap_y(ya, 0)), near(swap_y(ub, 1))
+        left, right, yb = call(
+            columns_beyond_kernel,
+            [near(left), near(right), zb, near(yb), ub],
+            [vmem(NY, NX), vmem(NY, NX), vmem(YPAY, NX)],
+            aliases={0: 0, 1: 1, 3: 2},
+            us=100.0,
+            name="columns_beyond",
+        )
+        yb = near(yb)
+        wb = near(swap_y(yb, 1))
         xa, xb, left, right, cor = call(
             columns_more_kernel,
             [wa, rb, ub, near(left), near(right)],

time: 17.6 us -> 17.2 us (0.977)
  starting transfers between devices: 9.06 us -> 8.17 us
  waiting for transfers between devices: 1.42 us -> 1.98 us
    ppermute x7, starting transfers between devices: 9.06 us -> 8.17 us  [exchange(): return lax.ppermute(values, ('gx', 'gy', 'gz'), pairs)]
    ppermute x7, waiting for transfers between devices: 1.42 us -> 1.98 us  [exchange(): return lax.ppermute(values, ('gx', 'gy', 'gz'), pairs)]
  transfers between devices with their start and end apart: 7 -> 7, of which waited for: 3 -> 4; matrix products, arithmetic and copies ran while one was open for 0% -> 0% of each run, Pallas kernels for 17% -> 18%
where the time goes in v5:
time: 17.2 us; the launch traced here: 17 us
  starting transfers between devices  8.17 us (48%)
  Pallas kernels  6.17 us (36%)
  waiting for transfers between devices  1.98 us (12%)
  between operations  0.72 us (4%)
    ppermute x7, starting transfers between devices, exchange(): return lax.ppermute(values, ('gx', 'gy', 'gz'), pairs)  8.17 us
    pallas_call x13, Pallas kernels, call(): pl.pallas_call(kernel, out_shape=outputs, in_specs=[pl.BlockSpec(memory_s...  6.17 us
    ppermute x7, waiting for transfers between devices, exchange(): return lax.ppermute(values, ('gx', 'gy', 'gz'), pairs)  1.98 us
  transfers between devices with their start and end apart: 7, of which 4 were waited for; matrix products, arithmetic and copies ran while one was open for 0% of the time, Pallas kernels for 18%

profile of v5, /device:TPU:19, one launch (start us, length us, event | category | flops | bytes accessed | tf_op | source)
XLA Modules:
  0.0 17.0 jit_solution(6876091437596423900)
XLA Ops:
  0.6 1.7 %stiffness.1 = (f32[3,17,32,128]{3,2,1,0:T(8,128)S(1)}, f32[16,32,128]{2,1,0:T(8,128)S(1)}, f32[16,32,128]{2,1,0:T(8,128)S(1)}, f32[32,128]{1,0:T(8,128)S(1)}) custom-call(f32[16,32,128]{2,1,0:T(8,128)} %r_hbm.1, s32[16,32,128]{2,1,0:T(8,128)} %lab_hbm.1, f32[3,16,32,128]{3,2,1,0:T(8,128)} %fac_hbm.1, f32[4,8,8,8]{3,2,1,0:T(8,128)} %bas_hbm.1, ...), custom_call_target="tpu_custom_call" | custom-call | flops 1800000000 | tf_op jit(solution)/shard_map/stiffness/pallas_call | solution.py:622
  2.3 0.3 %collective-permute-start = (f32[32,128]{1,0:T(8,128)S(1)}, f32[32,128]{1,0:T(8,128)S(1)}, u32[]{:S(2)}, u32[]{:S(2)}) collective-permute-start(f32[32,128]{1,0:T(8,128)S(1)} %get-tuple-element.33.mine_ref), channel_id=1, source_target_pairs={{0,1},{1,0},{2,3},{3,2},{4,5},{5,4},{6,7},{7,6},{8,9},{9,8},{10,11... | collective-permute-start | bytes 49160 | tf_op jit(solution)/shard_map/ppermute | solution.py:647
  2.7 0.2 %rows.1 = (f32[144,128]{1,0:T(8,128)S(1)}, f32[128,128]{1,0:T(8,128)S(1)}, f32[248,128]{1,0:T(8,128)S(1)}) custom-call(f32[3,17,32,128]{3,2,1,0:T(8,128)S(1)} %get-tuple-element.34.kap_ref, f32[16,32,128]{2,1,0:T(8,128)S(1)} %get-tuple-element.35.rr_ref), custom_call_target="tpu_custom_call" | custom-call | flops 100000000 | tf_op jit(solution)/shard_map/rows/pallas_call | solution.py:622
  2.9 1.2 %collective-permute-start.3 = (f32[248,128]{1,0:T(8,128)S(1)}, f32[248,128]{1,0:T(8,128)S(1)}, u32[]{:S(2)}, u32[]{:S(2)}) collective-permute-start(f32[248,128]{1,0:T(8,128)S(1)} %get-tuple-element.43), channel_id=1, source_target_pairs={{0,1},{1,0},{2,3},{3,2},{4,5},{5,4},{6,7},{7,6},{8,9},{9,8},{10,11... | collective-permute-start | bytes 380936 | tf_op jit(solution)/shard_map/ppermute | solution.py:647
  4.1 0.5 %inner_first.1 = (f32[16,32,128]{2,1,0:T(8,128)S(1)}, f32[16,32,128]{2,1,0:T(8,128)S(1)}, f32[3,16,32,128]{3,2,1,0:T(8,128)S(1)}) custom-call(f32[3,17,32,128]{3,2,1,0:T(8,128)S(1)} %get-tuple-element.34.kap_ref, f32[16,32,128]{2,1,0:T(8,128)S(1)} %get-tuple-element.35.rr_ref), custom_call_target="tpu_custom_call" | custom-call | flops 600000000 | tf_op jit(solution)/shard_map/inner_first/pallas_call | solution.py:622
  4.6 0.3 %columns.1 = (f32[32,128]{1,0:T(8,128)S(1)}, f32[32,128]{1,0:T(8,128)S(1)}, f32[8,128]{1,0:T(8,128)S(1)}) custom-call(f32[3,17,32,128]{3,2,1,0:T(8,128)S(1)} %get-tuple-element.34.kap_ref, f32[16,32,128]{2,1,0:T(8,128)S(1)} %get-tuple-element.35.rr_ref), custom_call_target="tpu_custom_call" | custom-call | flops 400000000 | tf_op jit(solution)/shard_map/columns/pallas_call | solution.py:622
  4.9 0.1 collective-permute-done.far_ref
  5.0 1.4 %collective-permute-start.1 = (f32[144,128]{1,0:T(8,128)S(1)}, f32[144,128]{1,0:T(8,128)S(1)}, u32[]{:S(2)}, u32[]{:S(2)}) collective-permute-start(f32[144,128]{1,0:T(8,128)S(1)} %get-tuple-element.39.ya_ref), channel_id=1, source_target_pairs={{0,2},{1,3},{2,0},{3,1},{4,6},{5,7},{6,4},{7,5},{8,10},{9,11},{10,... | collective-permute-start | bytes 221192 | tf_op jit(solution)/shard_map/ppermute | solution.py:647
  6.4 0.0 collective-permute-start.2
  6.4 0.8 %collective-permute-done.3.bulk_ref = f32[248,128]{1,0:T(8,128)S(1)} collective-permute-done((f32[248,128]{1,0:T(8,128)S(1)}, f32[248,128]{1,0:T(8,128)S(1)}, u32[]{:S(2)}, u32[]{:S(2)}) %collective-permute-start.3) | collective-permute-done | bytes 127008 | tf_op jit(solution)/shard_map/ppermute | solution.py:647
  7.2 0.2 columns_beyond.1
  7.4 0.7 %collective-permute-start.6 = (f32[128,128]{1,0:T(8,128)S(1)}, f32[128,128]{1,0:T(8,128)S(1)}, u32[]{:S(2)}, u32[]{:S(2)}) collective-permute-start(f32[128,128]{1,0:T(8,128)S(1)} %get-tuple-element.52.yb_ref), channel_id=1, source_target_pairs={{0,8},{1,9},{2,4},{3,5},{4,2},{5,3},{6,14},{7,15},{8,0},{9,1},{10,... | collective-permute-start | bytes 196616 | tf_op jit(solution)/shard_map/ppermute | solution.py:647
  8.1 0.8 %collective-permute-done.2.rb_ref = f32[16,128]{1,0:T(8,128)S(1)} collective-permute-done((f32[16,128]{1,0:T(8,128)S(1)}, f32[16,128]{1,0:T(8,128)S(1)}, u32[]{:S(2)}, u32[]{:S(2)}) %collective-permute-start.2) | collective-permute-done | bytes 8224 | tf_op jit(solution)/shard_map/ppermute | solution.py:647
  8.9 0.2 %columns_more.1 = (f32[56,128]{1,0:T(8,128)S(1)}, f32[56,128]{1,0:T(8,128)S(1)}, f32[40,128]{1,0:T(8,128)S(1)}, f32[40,128]{1,0:T(8,128)S(1)}, f32[4,16,128]{2,1,0:T(8,128)S(1)}) custom-call(f32[144,128]{1,0:T(8,128)S(1)} %collective-permute-done.1.ra_ref, f32[16,128]{1,0:T(8,128)S(1)} %collective-permute-done.2.rb_ref, ...), custom_call_target="tpu_custom_call" | custom-call | flops 1000000000 | tf_op jit(solution)/shard_map/columns_more/pallas_call | solution.py:622
  9.1 4.6 %collective-permute-start.4 = (f32[56,128]{1,0:T(8,128)S(1)}, f32[56,128]{1,0:T(8,128)S(1)}, u32[]{:S(2)}, u32[]{:S(2)}) collective-permute-start(f32[56,128]{1,0:T(8,128)S(1)} %get-tuple-element.47), channel_id=1, source_target_pairs={{0,24},{1,25},{2,26},{3,27},{4,28},{5,29},{6,30},{7,31},{8,16},{9,... | collective-permute-start | bytes 86024 | tf_op jit(solution)/shard_map/ppermute | solution.py:647
  13.6 0.1 slab.1.slab_ref
  13.8 0.7 %inner_image.1 = (f32[16,32,128]{2,1,0:T(8,128)S(1)}, f32[16,32,128]{2,1,0:T(8,128)S(1)}) custom-call(f32[3,17,32,128]{3,2,1,0:T(8,128)S(1)} %get-tuple-element.34.kap_ref, f32[16,32,128]{2,1,0:T(8,128)S(1)} %get-tuple-element.38.after_ref.f_ref.f_in, f32[3,16,32,128]{3,2,1,0:T(8,128)S(1)} %get-tuple-element.53.p_ref.p_in, ...), custom_call_target="tpu_custom_call", output_to_operand_aliasing={{0}: (3, {})} | custom-call | flops 600000000 | tf_op jit(solution)/shard_map/inner_image/pallas_call | solution.py:622
  14.5 0.3 %outer.1 = (f32[16,32,128]{2,1,0:T(8,128)S(1)}, f32[16,32,128]{2,1,0:T(8,128)S(1)}) custom-call(f32[3,17,32,128]{3,2,1,0:T(8,128)S(1)} %get-tuple-element.34.kap_ref, f32[16,32,128]{2,1,0:T(8,128)S(1)} %get-tuple-element.35.rr_ref, f32[248,128]{1,0:T(8,128)S(1)} %collective-permute-done.3.bulk_ref, ...), custom_call_target="tpu_custom_call", output_to_operand_aliasing={{0}: (5, {}), {1}: (6, {})} | custom-call | flops 250000000 | tf_op jit(solution)/shard_map/outer/pallas_call | solution.py:622
  14.7 0.0 collective-permute-done.6.rb_ref
  14.8 0.4 %edge_rows.1 = (f32[16,32,128]{2,1,0:T(8,128)S(1)}, f32[16,32,128]{2,1,0:T(8,128)S(1)}) custom-call(f32[144,128]{1,0:T(8,128)S(1)} %get-tuple-element.39.ya_ref, f32[128,128]{1,0:T(8,128)S(1)} %get-tuple-element.52.yb_ref, f32[144,128]{1,0:T(8,128)S(1)} %collective-permute-done.1.ra_ref, ...), custom_call_target="tpu_custom_call", output_to_operand_aliasing={{0}: (4, {}), {1}: (5, {})} | custom-call | flops 400000000 | tf_op jit(solution)/shard_map/edge_rows/pallas_call | solution.py:622
  15.2 0.2 %rim.1 = (f32[32,128]{1,0:T(8,128)S(1)}, f32[32,128]{1,0:T(8,128)S(1)}) custom-call(f32[16,32,128]{2,1,0:T(8,128)S(1)} %get-tuple-element.59.s1_ref, f32[16,32,128]{2,1,0:T(8,128)S(1)} %get-tuple-element.60.s2_ref), custom_call_target="tpu_custom_call" | custom-call | flops 200000000 | tf_op jit(solution)/shard_map/rim/pallas_call | solution.py:622
  15.4 0.3 %collective-permute-done.4.rb_ref = f32[56,128]{1,0:T(8,128)S(1)} collective-permute-done((f32[56,128]{1,0:T(8,128)S(1)}, f32[56,128]{1,0:T(8,128)S(1)}, u32[]{:S(2)}, u32[]{:S(2)}) %collective-permute-start.4) | collective-permute-done | bytes 28704 | tf_op jit(solution)/shard_map/ppermute | solution.py:647
  15.6 0.0 collective-permute-done.5.ra_ref
  15.6 1.4 %last.1 = (f32[16,32,128]{2,1,0:T(8,128)}, f32[2,4,16]{2,1,0:T(4,128)}) custom-call(f32[56,128]{1,0:T(8,128)S(1)} %collective-permute-done.4.rb_ref, f32[56,128]{1,0:T(8,128)S(1)} %collective-permute-done.5.ra_ref, f32[2,4,40,128]{3,2,1,0:T(8,128)S(1)} %slab.1.slab_ref, f32[4,16,128]{2,1,0:T(8,128)S(1)} %get-tuple-element.51.cor_ref, ...), custom_call_target="tpu_custom_call" | custom-call | flops 1500000000 | tf_op jit(solution)/shard_map/last/pallas_call | solution.py:622
  (3 shorter events, 0.0 us)
Async XLA Ops:
  2.3 2.7 %collective-permute-start = (f32[32,128]{1,0:T(8,128)S(1)}, f32[32,128]{1,0:T(8,128)S(1)}, u32[]{:S(2)}, u32[]{:S(2)}) collective-permute-start(f32[32,128]{1,0:T(8,128)S(1)} %get-tuple-element.33.mine_ref), channel_id=1, source_target_pairs={{0,1},{1,0},{2,3},{3,2},{4,5},{5,4},{6,7},{7,6},{8,9},{9,8},{10,11... | collective-permute-start | bytes 49160 | tf_op jit(solution)/shard_map/ppermute | solution.py:647
  2.9 4.3 %collective-permute-start.3 = (f32[248,128]{1,0:T(8,128)S(1)}, f32[248,128]{1,0:T(8,128)S(1)}, u32[]{:S(2)}, u32[]{:S(2)}) collective-permute-start(f32[248,128]{1,0:T(8,128)S(1)} %get-tuple-element.43), channel_id=1, source_target_pairs={{0,1},{1,0},{2,3},{3,2},{4,5},{5,4},{6,7},{7,6},{8,9},{9,8},{10,11... | collective-permute-start | bytes 380936 | tf_op jit(solution)/shard_map/ppermute | solution.py:647
  5.0 3.9 %collective-permute-start.1 = (f32[144,128]{1,0:T(8,128)S(1)}, f32[144,128]{1,0:T(8,128)S(1)}, u32[]{:S(2)}, u32[]{:S(2)}) collective-permute-start(f32[144,128]{1,0:T(8,128)S(1)} %get-tuple-element.39.ya_ref), channel_id=1, source_target_pairs={{0,2},{1,3},{2,0},{3,1},{4,6},{5,7},{6,4},{7,5},{8,10},{9,11},{10,... | collective-permute-start | bytes 221192 | tf_op jit(solution)/shard_map/ppermute | solution.py:647
  6.4 2.5 %collective-permute-start.2 = (f32[16,128]{1,0:T(8,128)S(1)}, f32[16,128]{1,0:T(8,128)S(1)}, u32[]{:S(2)}, u32[]{:S(2)}) collective-permute-start(f32[16,128]{1,0:T(8,128)S(1)} %get-tuple-element.40.after_ref.mine_ref), channel_id=1, source_target_pairs={{0,8},{1,9},{2,4},{3,5},{4,2},{5,3},{6,14},{7,15},{8,0},{9,1},{10,... | collective-permute-start | bytes 24584 | tf_op jit(solution)/shard_map/ppermute | solution.py:647
  7.4 7.4 %collective-permute-start.6 = (f32[128,128]{1,0:T(8,128)S(1)}, f32[128,128]{1,0:T(8,128)S(1)}, u32[]{:S(2)}, u32[]{:S(2)}) collective-permute-start(f32[128,128]{1,0:T(8,128)S(1)} %get-tuple-element.52.yb_ref), channel_id=1, source_target_pairs={{0,8},{1,9},{2,4},{3,5},{4,2},{5,3},{6,14},{7,15},{8,0},{9,1},{10,... | collective-permute-start | bytes 196616 | tf_op jit(solution)/shard_map/ppermute | solution.py:647
  9.1 6.6 %collective-permute-start.4 = (f32[56,128]{1,0:T(8,128)S(1)}, f32[56,128]{1,0:T(8,128)S(1)}, u32[]{:S(2)}, u32[]{:S(2)}) collective-permute-start(f32[56,128]{1,0:T(8,128)S(1)} %get-tuple-element.47), channel_id=1, source_target_pairs={{0,24},{1,25},{2,26},{3,27},{4,28},{5,29},{6,30},{7,31},{8,16},{9,... | collective-permute-start | bytes 86024 | tf_op jit(solution)/shard_map/ppermute | solution.py:647
  13.6 2.0 %collective-permute-start.5 = (f32[56,128]{1,0:T(8,128)S(1)}, f32[56,128]{1,0:T(8,128)S(1)}, u32[]{:S(2)}, u32[]{:S(2)}) collective-permute-start(f32[56,128]{1,0:T(8,128)S(1)} %get-tuple-element.48.after_ref), channel_id=1, source_target_pairs={{0,8},{1,9},{2,10},{3,11},{4,12},{5,13},{6,14},{7,15},{8,0},{9,1},... | collective-permute-start | bytes 86024 | tf_op jit(solution)/shard_map/ppermute | solution.py:647

commit v6 on v5

--- a/solution.py
+++ b/solution.py
@@ -24,10 +24,10 @@
 F32 = jnp.float32
 HIGHEST = lax.Precision.HIGHEST
 
-BULK = 7 * NY + 24
-BCOL, BROW = 7 * NY, 7 * NY + 8
+BULK = 7 * NY + 8
+BCOL = 7 * NY
 URGENT = 16
-ZURGENT = 32
+ZURGENT = 48
 KROWS = 36
 GROUP = NZ + 2
 RROW = 3 * KROWS
@@ -156,7 +156,6 @@
     for g in range(1, 8):
         coarse = jnp.where(group == g, bricks[g * 8 : g * 8 + 8], coarse)
     urgent_ref[0:8] = coarse
-    even = lax.axis_index("gy") % 2 == 0
     row = iota((8, NX), 0)
 
     def ends(plane):
@@ -170,9 +169,8 @@
         a, beyond = divmod(g, 2)
         for inner in range(2) if g < 6 else (1,):
             at = 12 if g == 6 else 4 * a + 2 * inner + beyond
-            low = plane[0:1] if inner else plane[1:2]
-            high = plane[NY - 1 : NY] if inner else plane[NY - 2 : NY - 1]
-            urgent_ref[16 + at : 17 + at] = jnp.where(even, high, low)
+            urgent_ref[16 + at : 17 + at] = plane[0:1] if inner else plane[1:2]
+            urgent_ref[32 + at : 33 + at] = plane[NY - 1 : NY] if inner else plane[NY - 2 : NY - 1]
 
 
 def end_tile(left, right):
@@ -186,12 +184,12 @@
     return jnp.where(lax.axis_index("gz") == 0, zp, NZ - 1 - zp)
 
 
-def rows_kernel(kap_ref, rr_ref, ya_ref, yb_ref, bulk_ref):
-    even = lax.axis_index("gy") % 2 == 0
+def rows_kernel(kap_ref, rr_ref, y0_ref, y1_ref, y2_ref, bulk_ref):
+    phase = lax.rem(lax.axis_index("gy"), 3)
 
     def put(at, low, high):
-        ya_ref[at : at + 1] = jnp.where(even, high, low)
-        yb_ref[at : at + 1] = jnp.where(even, low, high)
+        for slot, ref in enumerate((y0_ref, y1_ref, y2_ref)):
+            ref[at : at + 1] = jnp.where(phase == slot, high, low)
 
     for zp in range(NZ):
         for a in range(3):
@@ -212,15 +210,7 @@
     folded = columns[:8]
     for i in range(1, NY // 8):
         folded = jnp.where(lane >= 32 * i, roll(columns[8 * i : 8 * i + 8], 32 * i, 1), folded)
-    bulk_ref[BCOL:BROW] = folded
-    bulk_ref[BROW:BULK] = jnp.zeros((16, NX), F32)
-    for g, plane in enumerate(planes):
-        a, beyond = divmod(g, 2)
-        for inner in range(2) if g < 6 else (1,):
-            at = BROW + (12 if g == 6 else 4 * a + 2 * inner + beyond)
-            low = plane[0:1] if inner else plane[1:2]
-            high = plane[NY - 1 : NY] if inner else plane[NY - 2 : NY - 1]
-            bulk_ref[at : at + 1] = jnp.where(even, low, high)
+    bulk_ref[BCOL:BULK] = folded
 
 
 def columns_kernel(kap_ref, rr_ref, left_ref, right_ref, ends_ref):
@@ -257,25 +247,23 @@
     return jnp.where(lane == at, values, left), jnp.where(lane == at - 1, values, right)
 
 
-def insert_rows(y_ref, far_ref, at):
-    for i in range(6):
-        y_ref[i * GROUP + NZ : (i + 1) * GROUP] = far_ref[at + 2 * i : at + 2 * i + 2]
-    y_ref[RROW + NZ : RROW + NZ + 1] = far_ref[at + 12 : at + 13]
-
-
-def columns_beyond_kernel(left_in, right_in, bulk_ref, yb_in, after_ref, left_ref, right_ref, yb_ref):
-    folded = bulk_ref[BCOL:BROW]
+def columns_beyond_kernel(left_in, right_in, bulk_ref, after_ref, left_ref, right_ref):
+    folded = bulk_ref[BCOL:BULK]
     columns = jnp.concatenate([roll(folded, -32 * i, 1) for i in range(NY // 8)], axis=0)
     left_ref[...], right_ref[...] = columns_beyond(
         left_in[...], right_in[...], lambda g, x0: roll(columns, x0 - 4 * g - 2, 1)
     )
-    insert_rows(yb_ref, bulk_ref, BROW)
-
-
-def send_rows_kernel(far_ref, mine_ref, ends_ref, ya_in, after_ref, ya_ref, ub_ref):
-    even = lax.axis_index("gy") % 2 == 0
+
+
+def send_rows_kernel(far_ref, mine_ref, ends_ref, y0_in, y1_in, y2_in, after_ref, y0_ref, y1_ref, y2_ref, u2_ref):
+    phase = lax.rem(lax.axis_index("gy"), 3)
     row, lane = iota((8, NX), 0), iota((8, NX), 1)
-    insert_rows(ya_ref, far_ref, 16)
+    low, high = far_ref[16:32], far_ref[32:48]
+    for slot, ref in enumerate((y0_ref, y1_ref, y2_ref)):
+        rows = jnp.where(phase == slot, high, low)
+        for i in range(6):
+            ref[i * GROUP + NZ : (i + 1) * GROUP] = rows[2 * i : 2 * i + 2]
+        ref[RROW + NZ : RROW + NZ + 1] = rows[12:13]
     is_right = ((row >> 1) & 1) == 1
     at = lane - jnp.where(is_right, 0, 2)
     within = at - jnp.where(at >= 2 * KROWS, 2 * KROWS, jnp.where(at >= KROWS, KROWS, 0))
@@ -283,20 +271,24 @@
     beyond = beyond | (lane == RLANE + NZ - is_right.astype(jnp.int32))
     tile = jnp.where(beyond, far_ref[8:16], ends_ref[...])
     turned = roll(tile, 4, 0)
-    ya_ref[YPAY + 8 :] = jnp.where(even, turned, tile)
-    ub_ref[8:16] = jnp.where(even, tile, turned)
     coarse = jnp.where(row < CY, mine_ref[0:8], far_ref[0:8])
-    ya_ref[YPAY : YPAY + 8] = coarse
-    ub_ref[0:8] = coarse
-
-
-def columns_more_kernel(ra_ref, rb_ref, mine_ref, left_in, right_in, xa_ref, xb_ref, left_ref, right_ref, cor_ref):
-    gx, gy = lax.axis_index("gx"), lax.axis_index("gy")
-    even = gy % 2 == 0
-    zero = jnp.zeros((URGENT, NX), F32)
-    ra = ra_ref[YPAY:]
-    hi = jnp.where(gy < lax.axis_size("gy") - 1, jnp.where(even, ra, rb_ref[...]), zero)
-    lo = jnp.where(gy > 0, jnp.where(even, rb_ref[...], ra), zero)
+    for slot, (ref, at) in enumerate(((y0_ref, YPAY), (y1_ref, YPAY), (u2_ref, 0))):
+        ref[at : at + 8] = coarse
+        ref[at + 8 : at + 16] = jnp.where(phase == slot, turned, tile)
+
+
+def neighbours(slots):
+    gy = lax.axis_index("gy")
+    phase = lax.rem(gy, 3)
+    zero = jnp.zeros(slots[0].shape, F32)
+    hi = jnp.where(phase == 0, slots[0], jnp.where(phase == 1, slots[1], slots[2]))
+    lo = jnp.where(phase == 0, slots[2], jnp.where(phase == 1, slots[0], slots[1]))
+    return jnp.where(gy > 0, lo, zero), jnp.where(gy < lax.axis_size("gy") - 1, hi, zero)
+
+
+def columns_more_kernel(r0_ref, r1_ref, r2_ref, mine_ref, left_in, right_in, xa_ref, xb_ref, left_ref, right_ref, cor_ref):
+    gx = lax.axis_index("gx")
+    lo, hi = neighbours([r0_ref[YPAY:], r1_ref[YPAY:], r2_ref[...]])
     lane, row = iota((8, NX), 1), iota((8, NX), 0)
 
     def halo(shift):
@@ -388,7 +380,7 @@
             image_plane(i * 7 + j, i * 7 + j, kap_ref, f_ref, p_ref, s1_ref, s2_ref, rim)
 
 
-def outer_kernel(kap_ref, rr_ref, bulk_ref, f_in, p_in, s1_in, s2_in, s1_ref, s2_ref, k_ref, f_ref, p_ref):
+def outer_kernel(kap_ref, rr_ref, bulk_ref, f_in, p_in, s1_in, s2_in, after_ref, s1_ref, s2_ref, k_ref, f_ref, p_ref):
     rim = plane_rim()
     for a in range(3):
         for i in range(3):
@@ -408,21 +400,20 @@
     return both(values, 1, 1)
 
 
-def edge_rows_kernel(ya_ref, yb_ref, ra_ref, rb_ref, s1_in, s2_in, s1_ref, s2_ref):
-    even = lax.axis_index("gy") % 2 == 0
+def edge_rows_kernel(y0_ref, y1_ref, y2_ref, r0_ref, r1_ref, r2_ref, s1_in, s2_in, s1_ref, s2_ref):
     size = 24
     row, lane = iota((size, NX), 0), iota((size, NX), 1)
     inner = (lane > 0) & (lane < NX - 1)
     near = inner & (row < NZ + 1)
     inner16 = inner[:NZ]
-    gy = lax.axis_index("gy")
-    zero = jnp.zeros((YPAY, NX), F32)
-    ya, yb, ra, rb = ya_ref[0:YPAY], yb_ref[...], ra_ref[0:YPAY], rb_ref[...]
-    hi = jnp.where(gy < lax.axis_size("gy") - 1, jnp.where(even, ra, rb), zero)
-    lo = jnp.where(gy > 0, jnp.where(even, rb, ra), zero)
+    sent = [y0_ref[0:YPAY], y1_ref[0:YPAY], y2_ref[...]]
+    phase = lax.rem(lax.axis_index("gy"), 3)
+    high = jnp.where(phase == 0, sent[0], jnp.where(phase == 1, sent[1], sent[2]))
+    low = jnp.where(phase == 0, sent[2], jnp.where(phase == 1, sent[0], sent[1]))
+    lo, hi = neighbours([r0_ref[0:YPAY], r1_ref[0:YPAY], r2_ref[...]])
     for other, mine, face, second in (
-        (lo, jnp.where(even, yb, ya), 0, 1),
-        (hi, jnp.where(even, ya, yb), NY - 1, NY - 2),
+        (lo, low, 0, 1),
+        (hi, high, NY - 1, NY - 2),
     ):
 
         def group(source, at):
@@ -654,9 +645,9 @@
     def swap_z(values):
         return exchange(values, sizes, lambda x, y, z: (x, y, nz - 1 - z))
 
-    def swap_y(values, odd):
+    def swap_y(values, slot):
         def move(x, y, z):
-            b = y + 1 if y % 2 == odd else y - 1
+            b = y + 1 if y % 3 == slot else y - 1 if (y + 2) % 3 == slot else -1
             return (x, b, z) if 0 <= b < ny else (x ^ 1, y, z)
 
         return exchange(values, sizes, move)
@@ -686,7 +677,8 @@
         )
         kap, rr, sel, urgent = near(kap), near(rr), near(sel), near(urgent)
         zu = near(swap_z(urgent))
-        ya, yb, bulk = call(rows_kernel, [kap, rr], [vmem(YPAY + URGENT, NX), vmem(YPAY, NX), vmem(BULK, NX)], name="rows")
+        payloads = [vmem(YPAY + URGENT, NX), vmem(YPAY + URGENT, NX), vmem(YPAY, NX)]
+        y0, y1, y2, bulk = call(rows_kernel, [kap, rr], payloads + [vmem(BULK, NX)], name="rows")
         zb = near(swap_z(near(bulk)))
         left, right, ends = call(
             columns_kernel, [kap, rr], [vmem(NY, NX), vmem(NY, NX), vmem(8, NX)], us=0.4, name="columns"
@@ -699,29 +691,36 @@
             name="inner_first",
         )
         s1, f, p = near(s1), near(f), near(p)
-        ya, ub = call(
+        y0, y1, y2, u2 = call(
             send_rows_kernel,
-            [zu, urgent, near(ends), near(ya), f],
-            [vmem(YPAY + URGENT, NX), vmem(URGENT, NX)],
-            aliases={3: 0},
+            [zu, urgent, near(ends), near(y0), near(y1), near(y2), f],
+            payloads + [vmem(URGENT, NX)],
+            aliases={3: 0, 4: 1, 5: 2},
             us=10.0,
             name="send_rows",
         )
-        ya, ub = near(ya), near(ub)
-        wa, rb = near(swap_y(ya, 0)), near(swap_y(ub, 1))
-        left, right, yb = call(
+        y0, y1, y2, u2 = near(y0), near(y1), near(y2), near(u2)
+        r0, r1, t2, r2 = near(swap_y(y0, 0)), near(swap_y(y1, 1)), near(swap_y(u2, 2)), near(swap_y(y2, 2))
+        s1, s2 = call(
+            inner_image_kernel,
+            [kap, f, p, s1, u2],
+            [vmem(NZ, NY, NX), vmem(NZ, NY, NX)],
+            aliases={3: 0},
+            us=0.7,
+            name="inner_image",
+        )
+        s1, s2 = near(s1), near(s2)
+        left, right = call(
             columns_beyond_kernel,
-            [near(left), near(right), zb, near(yb), ub],
-            [vmem(NY, NX), vmem(NY, NX), vmem(YPAY, NX)],
-            aliases={0: 0, 1: 1, 3: 2},
+            [near(left), near(right), zb, s2],
+            [vmem(NY, NX), vmem(NY, NX)],
+            aliases={0: 0, 1: 1},
             us=100.0,
             name="columns_beyond",
         )
-        yb = near(yb)
-        wb = near(swap_y(yb, 1))
         xa, xb, left, right, cor = call(
             columns_more_kernel,
-            [wa, rb, ub, near(left), near(right)],
+            [r0, r1, t2, u2, near(left), near(right)],
             [vmem(XPAY, NX), vmem(XPAY, NX), vmem(40, NX), vmem(40, NX), vmem(4, 16, NX)],
             us=1.0,
             name="columns_more",
@@ -729,16 +728,8 @@
         xa, xb = near(xa), near(xb)
         vb, va = near(swap_x(xb, 1)), near(swap_x(xa, 0))
         s1, s2 = call(
-            inner_image_kernel,
-            [kap, f, p, s1, xa],
-            [vmem(NZ, NY, NX), vmem(NZ, NY, NX)],
-            aliases={3: 0},
-            us=0.6,
-            name="inner_image",
-        )
-        s1, s2 = call(
             outer_kernel,
-            [kap, rr, zb, f, p, near(s1), near(s2)],
+            [kap, rr, zb, f, p, s1, s2, xa],
             [vmem(NZ, NY, NX), vmem(NZ, NY, NX)],
             [pltpu.VMEM((3, 5, NY, NX), F32), pltpu.VMEM((4, NY, NX), F32), pltpu.VMEM((3, 4, NY, NX), F32)],
             aliases={5: 0, 6: 1},
@@ -747,9 +738,9 @@
         )
         s1, s2 = call(
             edge_rows_kernel,
-            [ya, yb, wa, wb, near(s1), near(s2)],
+            [y0, y1, y2, r0, r1, r2, near(s1), near(s2)],
             [vmem(NZ, NY, NX), vmem(NZ, NY, NX)],
-            aliases={4: 0, 5: 1},
+            aliases={6: 0, 7: 1},
             us=0.4,
             name="edge_rows",
         )

time: 17.2 us -> 17.1 us (level)
  the two profiles are of different devices: /device:TPU:19 before, /device:TPU:11 now
where the time goes in v6:
time: 17.1 us; the launch traced here: 16.9 us
  starting transfers between devices  8.12 us (47%)
  Pallas kernels  6.14 us (36%)
  waiting for transfers between devices  1.92 us (11%)
  between operations  0.74 us (4%)
    ppermute x8, starting transfers between devices, exchange(): return lax.ppermute(values, ('gx', 'gy', 'gz'), pairs)  8.12 us
    pallas_call x13, Pallas kernels, call(): pl.pallas_call(kernel, out_shape=outputs, in_specs=[pl.BlockSpec(memory_s...  6.14 us
    ppermute x8, waiting for transfers between devices, exchange(): return lax.ppermute(values, ('gx', 'gy', 'gz'), pairs)  1.92 us
  transfers between devices with their start and end apart: 8, of which 3 were waited for; matrix products, arithmetic and copies ran while one was open for 0% of the time, Pallas kernels for 18%

profile of v6, /device:TPU:11, one launch (start us, length us, event | category | flops | bytes accessed | tf_op | source)
XLA Modules:
  0.0 16.9 jit_solution(15896742545287337460)
XLA Ops:
  0.6 1.7 %stiffness.1 = (f32[3,17,32,128]{3,2,1,0:T(8,128)S(1)}, f32[16,32,128]{2,1,0:T(8,128)S(1)}, f32[16,32,128]{2,1,0:T(8,128)S(1)}, f32[48,128]{1,0:T(8,128)S(1)}) custom-call(f32[16,32,128]{2,1,0:T(8,128)} %r_hbm.1, s32[16,32,128]{2,1,0:T(8,128)} %lab_hbm.1, f32[3,16,32,128]{3,2,1,0:T(8,128)} %fac_hbm.1, f32[4,8,8,8]{3,2,1,0:T(8,128)} %bas_hbm.1, ...), custom_call_target="tpu_custom_call" | custom-call | flops 1800000000 | tf_op jit(solution)/shard_map/stiffness/pallas_call | solution.py:613
  2.3 0.3 %collective-permute-start = (f32[48,128]{1,0:T(8,128)S(1)}, f32[48,128]{1,0:T(8,128)S(1)}, u32[]{:S(2)}, u32[]{:S(2)}) collective-permute-start(f32[48,128]{1,0:T(8,128)S(1)} %get-tuple-element.35.mine_ref), channel_id=1, source_target_pairs={{0,1},{1,0},{2,3},{3,2},{4,5},{5,4},{6,7},{7,6},{8,9},{9,8},{10,11... | collective-permute-start | bytes 73736 | tf_op jit(solution)/shard_map/ppermute | solution.py:638
  2.7 0.2 %rows.1 = (f32[144,128]{1,0:T(8,128)S(1)}, f32[144,128]{1,0:T(8,128)S(1)}, f32[128,128]{1,0:T(8,128)S(1)}, f32[232,128]{1,0:T(8,128)S(1)}) custom-call(f32[3,17,32,128]{3,2,1,0:T(8,128)S(1)} %get-tuple-element.36.kap_ref, f32[16,32,128]{2,1,0:T(8,128)S(1)} %get-tuple-element.37.rr_ref), custom_call_target="tpu_custom_call" | custom-call | flops 100000000 | tf_op jit(solution)/shard_map/rows/pallas_call | solution.py:613
  2.9 1.2 %collective-permute-start.4 = (f32[232,128]{1,0:T(8,128)S(1)}, f32[232,128]{1,0:T(8,128)S(1)}, u32[]{:S(2)}, u32[]{:S(2)}) collective-permute-start(f32[232,128]{1,0:T(8,128)S(1)} %get-tuple-element.48), channel_id=1, source_target_pairs={{0,1},{1,0},{2,3},{3,2},{4,5},{5,4},{6,7},{7,6},{8,9},{9,8},{10,11... | collective-permute-start | bytes 356360 | tf_op jit(solution)/shard_map/ppermute | solution.py:638
  4.1 0.4 %inner_first.1 = (f32[16,32,128]{2,1,0:T(8,128)S(1)}, f32[16,32,128]{2,1,0:T(8,128)S(1)}, f32[3,16,32,128]{3,2,1,0:T(8,128)S(1)}) custom-call(f32[3,17,32,128]{3,2,1,0:T(8,128)S(1)} %get-tuple-element.36.kap_ref, f32[16,32,128]{2,1,0:T(8,128)S(1)} %get-tuple-element.37.rr_ref), custom_call_target="tpu_custom_call" | custom-call | flops 600000000 | tf_op jit(solution)/shard_map/inner_first/pallas_call | solution.py:613
  4.6 0.3 %columns.1 = (f32[32,128]{1,0:T(8,128)S(1)}, f32[32,128]{1,0:T(8,128)S(1)}, f32[8,128]{1,0:T(8,128)S(1)}) custom-call(f32[3,17,32,128]{3,2,1,0:T(8,128)S(1)} %get-tuple-element.36.kap_ref, f32[16,32,128]{2,1,0:T(8,128)S(1)} %get-tuple-element.37.rr_ref), custom_call_target="tpu_custom_call" | custom-call | flops 400000000 | tf_op jit(solution)/shard_map/columns/pallas_call | solution.py:613
  4.9 0.2 collective-permute-done.far_ref
  5.1 0.2 %collective-permute-start.1 = (f32[144,128]{1,0:T(8,128)S(1)}, f32[144,128]{1,0:T(8,128)S(1)}, u32[]{:S(2)}, u32[]{:S(2)}) collective-permute-start(f32[144,128]{1,0:T(8,128)S(1)} %get-tuple-element.43.y0_ref), channel_id=1, source_target_pairs={{0,2},{1,3},{2,0},{3,1},{4,12},{5,13},{6,14},{7,15},{8,10},{9,11},... | collective-permute-start | bytes 221192 | tf_op jit(solution)/shard_map/ppermute | solution.py:638
  5.3 3.2 %collective-permute-start.2 = (f32[144,128]{1,0:T(8,128)S(1)}, f32[144,128]{1,0:T(8,128)S(1)}, u32[]{:S(2)}, u32[]{:S(2)}) collective-permute-start(f32[144,128]{1,0:T(8,128)S(1)} %get-tuple-element.44.y1_ref), channel_id=1, source_target_pairs={{0,8},{1,9},{2,4},{3,5},{4,2},{5,3},{6,14},{7,15},{8,0},{9,1},{10,... | collective-permute-start | bytes 221192 | tf_op jit(solution)/shard_map/ppermute | solution.py:638
  8.5 0.3 %collective-permute-start.3 = (f32[16,128]{1,0:T(8,128)S(1)}, f32[16,128]{1,0:T(8,128)S(1)}, u32[]{:S(2)}, u32[]{:S(2)}) collective-permute-start(f32[16,128]{1,0:T(8,128)S(1)} %get-tuple-element.45.after_ref.mine_ref), channel_id=1, source_target_pairs={{0,8},{1,9},{2,10},{3,11},{4,6},{5,7},{6,4},{7,5},{8,0},{9,1},{10,... | collective-permute-start | bytes 24584 | tf_op jit(solution)/shard_map/ppermute | solution.py:638
  8.9 0.2 collective-permute-start.7
  9.0 0.7 %inner_image.1 = (f32[16,32,128]{2,1,0:T(8,128)S(1)}, f32[16,32,128]{2,1,0:T(8,128)S(1)}) custom-call(f32[3,17,32,128]{3,2,1,0:T(8,128)S(1)} %get-tuple-element.36.kap_ref, f32[16,32,128]{2,1,0:T(8,128)S(1)} %get-tuple-element.42.after_ref.f_ref.f_in, f32[3,16,32,128]{3,2,1,0:T(8,128)S(1)} %get-tuple-element.49.p_ref.p_in, ...), custom_call_target="tpu_custom_call", output_to_operand_aliasing={{0}: (3, {})} | custom-call | flops 700000000 | tf_op jit(solution)/shard_map/inner_image/pallas_call | solution.py:613
  9.7 0.2 columns_beyond.1
  9.9 0.0 collective-permute-done.1.r0_ref
  9.9 0.6 %collective-permute-done.2.r1_ref = f32[144,128]{1,0:T(8,128)S(1)} collective-permute-done((f32[144,128]{1,0:T(8,128)S(1)}, f32[144,128]{1,0:T(8,128)S(1)}, u32[]{:S(2)}, u32[]{:S(2)}) %collective-permute-start.2) | collective-permute-done | bytes 73760 | tf_op jit(solution)/shard_map/ppermute | solution.py:638
  10.5 0.2 %columns_more.1 = (f32[56,128]{1,0:T(8,128)S(1)}, f32[56,128]{1,0:T(8,128)S(1)}, f32[40,128]{1,0:T(8,128)S(1)}, f32[40,128]{1,0:T(8,128)S(1)}, f32[4,16,128]{2,1,0:T(8,128)S(1)}) custom-call(f32[144,128]{1,0:T(8,128)S(1)} %collective-permute-done.1.r0_ref, f32[144,128]{1,0:T(8,128)S(1)} %collective-permute-done.2.r1_ref, ...), custom_call_target="tpu_custom_call" | custom-call | flops 1000000000 | tf_op jit(solution)/shard_map/columns_more/pallas_call | solution.py:613
  10.7 2.7 %collective-permute-start.5 = (f32[56,128]{1,0:T(8,128)S(1)}, f32[56,128]{1,0:T(8,128)S(1)}, u32[]{:S(2)}, u32[]{:S(2)}) collective-permute-start(f32[56,128]{1,0:T(8,128)S(1)} %get-tuple-element.54), channel_id=1, source_target_pairs={{0,24},{1,25},{2,26},{3,27},{4,28},{5,29},{6,30},{7,31},{8,16},{9,... | collective-permute-start | bytes 86024 | tf_op jit(solution)/shard_map/ppermute | solution.py:638
  13.4 0.0 collective-permute-start.6
  13.4 0.2 %outer.1 = (f32[16,32,128]{2,1,0:T(8,128)S(1)}, f32[16,32,128]{2,1,0:T(8,128)S(1)}) custom-call(f32[3,17,32,128]{3,2,1,0:T(8,128)S(1)} %get-tuple-element.36.kap_ref, f32[16,32,128]{2,1,0:T(8,128)S(1)} %get-tuple-element.37.rr_ref, f32[232,128]{1,0:T(8,128)S(1)} %collective-permute-done.4.bulk_ref, ...), custom_call_target="tpu_custom_call", output_to_operand_aliasing={{0}: (5, {}), {1}: (6, {})} | custom-call | flops 250000000 | tf_op jit(solution)/shard_map/outer/pallas_call | solution.py:613
  13.7 0.4 %edge_rows.1 = (f32[16,32,128]{2,1,0:T(8,128)S(1)}, f32[16,32,128]{2,1,0:T(8,128)S(1)}) custom-call(f32[144,128]{1,0:T(8,128)S(1)} %get-tuple-element.43.y0_ref, f32[144,128]{1,0:T(8,128)S(1)} %get-tuple-element.44.y1_ref, f32[128,128]{1,0:T(8,128)S(1)} %get-tuple-element.59.y2_ref, ...), custom_call_target="tpu_custom_call", output_to_operand_aliasing={{0}: (6, {}), {1}: (7, {})} | custom-call | flops 400000000 | tf_op jit(solution)/shard_map/edge_rows/pallas_call | solution.py:613
  14.1 0.1 slab.1.slab_ref
  14.2 0.2 %rim.1 = (f32[32,128]{1,0:T(8,128)S(1)}, f32[32,128]{1,0:T(8,128)S(1)}) custom-call(f32[16,32,128]{2,1,0:T(8,128)S(1)} %get-tuple-element.63.s1_ref, f32[16,32,128]{2,1,0:T(8,128)S(1)} %get-tuple-element.64.s2_ref), custom_call_target="tpu_custom_call" | custom-call | flops 200000000 | tf_op jit(solution)/shard_map/rim/pallas_call | solution.py:613
  14.4 1.1 %collective-permute-done.5.rb_ref = f32[56,128]{1,0:T(8,128)S(1)} collective-permute-done((f32[56,128]{1,0:T(8,128)S(1)}, f32[56,128]{1,0:T(8,128)S(1)}, u32[]{:S(2)}, u32[]{:S(2)}) %collective-permute-start.5) | collective-permute-done | bytes 28704 | tf_op jit(solution)/shard_map/ppermute | solution.py:638
  15.5 1.4 %last.1 = (f32[16,32,128]{2,1,0:T(8,128)}, f32[2,4,16]{2,1,0:T(4,128)}) custom-call(f32[56,128]{1,0:T(8,128)S(1)} %collective-permute-done.5.rb_ref, f32[56,128]{1,0:T(8,128)S(1)} %collective-permute-done.6.ra_ref, f32[2,4,40,128]{3,2,1,0:T(8,128)S(1)} %slab.1.slab_ref, f32[4,16,128]{2,1,0:T(8,128)S(1)} %get-tuple-element.58.cor_ref, ...), custom_call_target="tpu_custom_call" | custom-call | flops 1500000000 | tf_op jit(solution)/shard_map/last/pallas_call | solution.py:613
  (5 shorter events, 0.0 us)
Async XLA Ops:
  2.3 2.7 %collective-permute-start = (f32[48,128]{1,0:T(8,128)S(1)}, f32[48,128]{1,0:T(8,128)S(1)}, u32[]{:S(2)}, u32[]{:S(2)}) collective-permute-start(f32[48,128]{1,0:T(8,128)S(1)} %get-tuple-element.35.mine_ref), channel_id=1, source_target_pairs={{0,1},{1,0},{2,3},{3,2},{4,5},{5,4},{6,7},{7,6},{8,9},{9,8},{10,11... | collective-permute-start | bytes 73736 | tf_op jit(solution)/shard_map/ppermute | solution.py:638
  2.9 6.8 %collective-permute-start.4 = (f32[232,128]{1,0:T(8,128)S(1)}, f32[232,128]{1,0:T(8,128)S(1)}, u32[]{:S(2)}, u32[]{:S(2)}) collective-permute-start(f32[232,128]{1,0:T(8,128)S(1)} %get-tuple-element.48), channel_id=1, source_target_pairs={{0,1},{1,0},{2,3},{3,2},{4,5},{5,4},{6,7},{7,6},{8,9},{9,8},{10,11... | collective-permute-start | bytes 356360 | tf_op jit(solution)/shard_map/ppermute | solution.py:638
  5.1 4.8 %collective-permute-start.1 = (f32[144,128]{1,0:T(8,128)S(1)}, f32[144,128]{1,0:T(8,128)S(1)}, u32[]{:S(2)}, u32[]{:S(2)}) collective-permute-start(f32[144,128]{1,0:T(8,128)S(1)} %get-tuple-element.43.y0_ref), channel_id=1, source_target_pairs={{0,2},{1,3},{2,0},{3,1},{4,12},{5,13},{6,14},{7,15},{8,10},{9,11},... | collective-permute-start | bytes 221192 | tf_op jit(solution)/shard_map/ppermute | solution.py:638
  5.3 5.2 %collective-permute-start.2 = (f32[144,128]{1,0:T(8,128)S(1)}, f32[144,128]{1,0:T(8,128)S(1)}, u32[]{:S(2)}, u32[]{:S(2)}) collective-permute-start(f32[144,128]{1,0:T(8,128)S(1)} %get-tuple-element.44.y1_ref), channel_id=1, source_target_pairs={{0,8},{1,9},{2,4},{3,5},{4,2},{5,3},{6,14},{7,15},{8,0},{9,1},{10,... | collective-permute-start | bytes 221192 | tf_op jit(solution)/shard_map/ppermute | solution.py:638
  8.5 1.4 %collective-permute-start.3 = (f32[16,128]{1,0:T(8,128)S(1)}, f32[16,128]{1,0:T(8,128)S(1)}, u32[]{:S(2)}, u32[]{:S(2)}) collective-permute-start(f32[16,128]{1,0:T(8,128)S(1)} %get-tuple-element.45.after_ref.mine_ref), channel_id=1, source_target_pairs={{0,8},{1,9},{2,10},{3,11},{4,6},{5,7},{6,4},{7,5},{8,0},{9,1},{10,... | collective-permute-start | bytes 24584 | tf_op jit(solution)/shard_map/ppermute | solution.py:638
  8.9 4.8 %collective-permute-start.7 = (f32[128,128]{1,0:T(8,128)S(1)}, f32[128,128]{1,0:T(8,128)S(1)}, u32[]{:S(2)}, u32[]{:S(2)}) collective-permute-start(f32[128,128]{1,0:T(8,128)S(1)} %get-tuple-element.59.y2_ref), channel_id=1, source_target_pairs={{0,8},{1,9},{2,10},{3,11},{4,6},{5,7},{6,4},{7,5},{8,0},{9,1},{10,... | collective-permute-start | bytes 196616 | tf_op jit(solution)/shard_map/ppermute | solution.py:638
  10.7 4.8 %collective-permute-start.5 = (f32[56,128]{1,0:T(8,128)S(1)}, f32[56,128]{1,0:T(8,128)S(1)}, u32[]{:S(2)}, u32[]{:S(2)}) collective-permute-start(f32[56,128]{1,0:T(8,128)S(1)} %get-tuple-element.54), channel_id=1, source_target_pairs={{0,24},{1,25},{2,26},{3,27},{4,28},{5,29},{6,30},{7,31},{8,16},{9,... | collective-permute-start | bytes 86024 | tf_op jit(solution)/shard_map/ppermute | solution.py:638
  13.4 2.2 %collective-permute-start.6 = (f32[56,128]{1,0:T(8,128)S(1)}, f32[56,128]{1,0:T(8,128)S(1)}, u32[]{:S(2)}, u32[]{:S(2)}) collective-permute-start(f32[56,128]{1,0:T(8,128)S(1)} %get-tuple-element.55.after_ref), channel_id=1, source_target_pairs={{0,8},{1,9},{2,10},{3,11},{4,12},{5,13},{6,14},{7,15},{8,0},{9,1},... | collective-permute-start | bytes 86024 | tf_op jit(solution)/shard_map/ppermute | solution.py:638

commit v7 on v6

--- a/solution.py
+++ b/solution.py
@@ -184,12 +184,12 @@
     return jnp.where(lax.axis_index("gz") == 0, zp, NZ - 1 - zp)
 
 
-def rows_kernel(kap_ref, rr_ref, y0_ref, y1_ref, y2_ref, bulk_ref):
-    phase = lax.rem(lax.axis_index("gy"), 3)
+def rows_kernel(kap_ref, rr_ref, ya_ref, yb_ref, bulk_ref):
+    even = lax.rem(lax.axis_index("gy"), 2) == 0
 
     def put(at, low, high):
-        for slot, ref in enumerate((y0_ref, y1_ref, y2_ref)):
-            ref[at : at + 1] = jnp.where(phase == slot, high, low)
+        ya_ref[at : at + 1] = jnp.where(even, high, low)
+        yb_ref[at : at + 1] = jnp.where(even, low, high)
 
     for zp in range(NZ):
         for a in range(3):
@@ -255,12 +255,12 @@
     )
 
 
-def send_rows_kernel(far_ref, mine_ref, ends_ref, y0_in, y1_in, y2_in, after_ref, y0_ref, y1_ref, y2_ref, u2_ref):
+def send_rows_kernel(far_ref, mine_ref, ends_ref, ya_in, yb_in, after_ref, ya_ref, yb_ref, u0_ref, u1_ref, u2_ref):
     phase = lax.rem(lax.axis_index("gy"), 3)
     row, lane = iota((8, NX), 0), iota((8, NX), 1)
     low, high = far_ref[16:32], far_ref[32:48]
-    for slot, ref in enumerate((y0_ref, y1_ref, y2_ref)):
-        rows = jnp.where(phase == slot, high, low)
+    even = lax.rem(lax.axis_index("gy"), 2) == 0
+    for ref, rows in ((ya_ref, jnp.where(even, high, low)), (yb_ref, jnp.where(even, low, high))):
         for i in range(6):
             ref[i * GROUP + NZ : (i + 1) * GROUP] = rows[2 * i : 2 * i + 2]
         ref[RROW + NZ : RROW + NZ + 1] = rows[12:13]
@@ -272,9 +272,9 @@
     tile = jnp.where(beyond, far_ref[8:16], ends_ref[...])
     turned = roll(tile, 4, 0)
     coarse = jnp.where(row < CY, mine_ref[0:8], far_ref[0:8])
-    for slot, (ref, at) in enumerate(((y0_ref, YPAY), (y1_ref, YPAY), (u2_ref, 0))):
-        ref[at : at + 8] = coarse
-        ref[at + 8 : at + 16] = jnp.where(phase == slot, turned, tile)
+    for slot, ref in enumerate((u0_ref, u1_ref, u2_ref)):
+        ref[0:8] = coarse
+        ref[8:16] = jnp.where(phase == slot, turned, tile)
 
 
 def neighbours(slots):
@@ -288,7 +288,7 @@
 
 def columns_more_kernel(r0_ref, r1_ref, r2_ref, mine_ref, left_in, right_in, xa_ref, xb_ref, left_ref, right_ref, cor_ref):
     gx = lax.axis_index("gx")
-    lo, hi = neighbours([r0_ref[YPAY:], r1_ref[YPAY:], r2_ref[...]])
+    lo, hi = neighbours([r0_ref[...], r1_ref[...], r2_ref[...]])
     lane, row = iota((8, NX), 1), iota((8, NX), 0)
 
     def halo(shift):
@@ -371,7 +371,7 @@
             first_plane(zp, zp, kap_ref, rr_ref[place(zp)], f_ref, p_ref, s1_ref, rim)
 
 
-def inner_image_kernel(kap_ref, f_ref, p_ref, s1_in, after_ref, s1_ref, s2_ref):
+def inner_image_kernel(kap_ref, f_ref, p_ref, s1_in, s1_ref, s2_ref):
     rim = plane_rim()
 
     @pl.loop(0, 2)
@@ -400,17 +400,19 @@
     return both(values, 1, 1)
 
 
-def edge_rows_kernel(y0_ref, y1_ref, y2_ref, r0_ref, r1_ref, r2_ref, s1_in, s2_in, s1_ref, s2_ref):
+def edge_rows_kernel(ya_ref, yb_ref, ra_ref, rb_ref, s1_in, s2_in, s1_ref, s2_ref):
     size = 24
     row, lane = iota((size, NX), 0), iota((size, NX), 1)
     inner = (lane > 0) & (lane < NX - 1)
     near = inner & (row < NZ + 1)
     inner16 = inner[:NZ]
-    sent = [y0_ref[0:YPAY], y1_ref[0:YPAY], y2_ref[...]]
-    phase = lax.rem(lax.axis_index("gy"), 3)
-    high = jnp.where(phase == 0, sent[0], jnp.where(phase == 1, sent[1], sent[2]))
-    low = jnp.where(phase == 0, sent[2], jnp.where(phase == 1, sent[0], sent[1]))
-    lo, hi = neighbours([r0_ref[0:YPAY], r1_ref[0:YPAY], r2_ref[...]])
+    gy = lax.axis_index("gy")
+    even = lax.rem(gy, 2) == 0
+    ya, yb, ra, rb = ya_ref[...], yb_ref[...], ra_ref[...], rb_ref[...]
+    low, high = jnp.where(even, yb, ya), jnp.where(even, ya, yb)
+    zero = jnp.zeros((YPAY, NX), F32)
+    lo = jnp.where(gy > 0, jnp.where(even, rb, ra), zero)
+    hi = jnp.where(gy < lax.axis_size("gy") - 1, jnp.where(even, ra, rb), zero)
     for other, mine, face, second in (
         (lo, low, 0, 1),
         (hi, high, NY - 1, NY - 2),
@@ -645,9 +647,9 @@
     def swap_z(values):
         return exchange(values, sizes, lambda x, y, z: (x, y, nz - 1 - z))
 
-    def swap_y(values, slot):
+    def swap_y(values, slots, slot):
         def move(x, y, z):
-            b = y + 1 if y % 3 == slot else y - 1 if (y + 2) % 3 == slot else -1
+            b = y + 1 if y % slots == slot else y - 1 if (y - 1) % slots == slot else -1
             return (x, b, z) if 0 <= b < ny else (x ^ 1, y, z)
 
         return exchange(values, sizes, move)
@@ -677,8 +679,8 @@
         )
         kap, rr, sel, urgent = near(kap), near(rr), near(sel), near(urgent)
         zu = near(swap_z(urgent))
-        payloads = [vmem(YPAY + URGENT, NX), vmem(YPAY + URGENT, NX), vmem(YPAY, NX)]
-        y0, y1, y2, bulk = call(rows_kernel, [kap, rr], payloads + [vmem(BULK, NX)], name="rows")
+        payloads = [vmem(YPAY, NX)] * 2
+        ya, yb, bulk = call(rows_kernel, [kap, rr], payloads + [vmem(BULK, NX)], name="rows")
         zb = near(swap_z(near(bulk)))
         left, right, ends = call(
             columns_kernel, [kap, rr], [vmem(NY, NX), vmem(NY, NX), vmem(8, NX)], us=0.4, name="columns"
@@ -691,28 +693,30 @@
             name="inner_first",
         )
         s1, f, p = near(s1), near(f), near(p)
-        y0, y1, y2, u2 = call(
-            send_rows_kernel,
-            [zu, urgent, near(ends), near(y0), near(y1), near(y2), f],
-            payloads + [vmem(URGENT, NX)],
-            aliases={3: 0, 4: 1, 5: 2},
-            us=10.0,
-            name="send_rows",
-        )
-        y0, y1, y2, u2 = near(y0), near(y1), near(y2), near(u2)
-        r0, r1, t2, r2 = near(swap_y(y0, 0)), near(swap_y(y1, 1)), near(swap_y(u2, 2)), near(swap_y(y2, 2))
         s1, s2 = call(
             inner_image_kernel,
-            [kap, f, p, s1, u2],
+            [kap, f, p, s1],
             [vmem(NZ, NY, NX), vmem(NZ, NY, NX)],
             aliases={3: 0},
             us=0.7,
             name="inner_image",
         )
         s1, s2 = near(s1), near(s2)
+        sent = call(
+            send_rows_kernel,
+            [zu, urgent, near(ends), near(ya), near(yb), s2],
+            payloads + [vmem(URGENT, NX)] * 3,
+            aliases={3: 0, 4: 1},
+            us=10.0,
+            name="send_rows",
+        )
+        sent = [near(v) for v in sent]
+        first, last = sent[2:], sent[:2]
+        first_in = [near(swap_y(v, 3, slot)) for slot, v in enumerate(first)]
+        last_in = [near(swap_y(v, 2, slot)) for slot, v in enumerate(last)]
         left, right = call(
             columns_beyond_kernel,
-            [near(left), near(right), zb, s2],
+            [near(left), near(right), zb, first[2]],
             [vmem(NY, NX), vmem(NY, NX)],
             aliases={0: 0, 1: 1},
             us=100.0,
@@ -720,7 +724,7 @@
         )
         xa, xb, left, right, cor = call(
             columns_more_kernel,
-            [r0, r1, t2, u2, near(left), near(right)],
+            first_in + [first[2], near(left), near(right)],
             [vmem(XPAY, NX), vmem(XPAY, NX), vmem(40, NX), vmem(40, NX), vmem(4, 16, NX)],
             us=1.0,
             name="columns_more",
@@ -738,9 +742,9 @@
         )
         s1, s2 = call(
             edge_rows_kernel,
-            [y0, y1, y2, r0, r1, r2, near(s1), near(s2)],
+            last + last_in + [near(s1), near(s2)],
             [vmem(NZ, NY, NX), vmem(NZ, NY, NX)],
-            aliases={6: 0, 7: 1},
+            aliases={4: 0, 5: 1},
             us=0.4,
             name="edge_rows",
         )

time: 17.1 us -> 17 us (level)
  the two profiles are of different devices: /device:TPU:11 before, /device:TPU:19 now
where the time goes in v7:
time: 17 us; the launch traced here: 16.7 us
  starting transfers between devices  8.32 us (49%)
  Pallas kernels  6.13 us (36%)
  waiting for transfers between devices  1.56 us (9%)
  between operations  0.74 us (4%)
    ppermute x9, starting transfers between devices, exchange(): return lax.ppermute(values, ('gx', 'gy', 'gz'), pairs)  8.32 us
    pallas_call x13, Pallas kernels, call(): pl.pallas_call(kernel, out_shape=outputs, in_specs=[pl.BlockSpec(memory_s...  6.13 us
    ppermute x9, waiting for transfers between devices, exchange(): return lax.ppermute(values, ('gx', 'gy', 'gz'), pairs)  1.56 us
  transfers between devices with their start and end apart: 9, of which 2 were waited for; matrix products, arithmetic and copies ran while one was open for 0% of the time, Pallas kernels for 18%

profile of v7, /device:TPU:19, one launch (start us, length us, event | category | flops | bytes accessed | tf_op | source)
XLA Modules:
  0.0 16.7 jit_solution(13905050436676400483)
XLA Ops:
  0.6 1.7 %stiffness.1 = (f32[3,17,32,128]{3,2,1,0:T(8,128)S(1)}, f32[16,32,128]{2,1,0:T(8,128)S(1)}, f32[16,32,128]{2,1,0:T(8,128)S(1)}, f32[48,128]{1,0:T(8,128)S(1)}) custom-call(f32[16,32,128]{2,1,0:T(8,128)} %r_hbm.1, s32[16,32,128]{2,1,0:T(8,128)} %lab_hbm.1, f32[3,16,32,128]{3,2,1,0:T(8,128)} %fac_hbm.1, f32[4,8,8,8]{3,2,1,0:T(8,128)} %bas_hbm.1, ...), custom_call_target="tpu_custom_call" | custom-call | flops 1800000000 | tf_op jit(solution)/shard_map/stiffness/pallas_call | solution.py:615
  2.3 0.3 %collective-permute-start = (f32[48,128]{1,0:T(8,128)S(1)}, f32[48,128]{1,0:T(8,128)S(1)}, u32[]{:S(2)}, u32[]{:S(2)}) collective-permute-start(f32[48,128]{1,0:T(8,128)S(1)} %get-tuple-element.35.mine_ref), channel_id=1, source_target_pairs={{0,1},{1,0},{2,3},{3,2},{4,5},{5,4},{6,7},{7,6},{8,9},{9,8},{10,11... | collective-permute-start | bytes 73736 | tf_op jit(solution)/shard_map/ppermute | solution.py:640
  2.7 0.2 %rows.1 = (f32[128,128]{1,0:T(8,128)S(1)}, f32[128,128]{1,0:T(8,128)S(1)}, f32[232,128]{1,0:T(8,128)S(1)}) custom-call(f32[3,17,32,128]{3,2,1,0:T(8,128)S(1)} %get-tuple-element.36.kap_ref, f32[16,32,128]{2,1,0:T(8,128)S(1)} %get-tuple-element.37.rr_ref), custom_call_target="tpu_custom_call" | custom-call | flops 100000000 | tf_op jit(solution)/shard_map/rows/pallas_call | solution.py:615
  2.9 1.2 %collective-permute-start.4 = (f32[232,128]{1,0:T(8,128)S(1)}, f32[232,128]{1,0:T(8,128)S(1)}, u32[]{:S(2)}, u32[]{:S(2)}) collective-permute-start(f32[232,128]{1,0:T(8,128)S(1)} %get-tuple-element.50), channel_id=1, source_target_pairs={{0,1},{1,0},{2,3},{3,2},{4,5},{5,4},{6,7},{7,6},{8,9},{9,8},{10,11... | collective-permute-start | bytes 356360 | tf_op jit(solution)/shard_map/ppermute | solution.py:640
  4.1 0.4 %inner_first.1 = (f32[16,32,128]{2,1,0:T(8,128)S(1)}, f32[16,32,128]{2,1,0:T(8,128)S(1)}, f32[3,16,32,128]{3,2,1,0:T(8,128)S(1)}) custom-call(f32[3,17,32,128]{3,2,1,0:T(8,128)S(1)} %get-tuple-element.36.kap_ref, f32[16,32,128]{2,1,0:T(8,128)S(1)} %get-tuple-element.37.rr_ref), custom_call_target="tpu_custom_call" | custom-call | flops 600000000 | tf_op jit(solution)/shard_map/inner_first/pallas_call | solution.py:615
  4.6 0.7 %inner_image.1 = (f32[16,32,128]{2,1,0:T(8,128)S(1)}, f32[16,32,128]{2,1,0:T(8,128)S(1)}) custom-call(f32[3,17,32,128]{3,2,1,0:T(8,128)S(1)} %get-tuple-element.36.kap_ref, f32[16,32,128]{2,1,0:T(8,128)S(1)} %get-tuple-element.41.f_ref.f_in, f32[3,16,32,128]{3,2,1,0:T(8,128)S(1)} %get-tuple-element.42.p_ref.p_in, ...), custom_call_target="tpu_custom_call", output_to_operand_aliasing={{0}: (3, {})} | custom-call | flops 700000000 | tf_op jit(solution)/shard_map/inner_image/pallas_call | solution.py:615
  5.3 0.3 %columns.1 = (f32[32,128]{1,0:T(8,128)S(1)}, f32[32,128]{1,0:T(8,128)S(1)}, f32[8,128]{1,0:T(8,128)S(1)}) custom-call(f32[3,17,32,128]{3,2,1,0:T(8,128)S(1)} %get-tuple-element.36.kap_ref, f32[16,32,128]{2,1,0:T(8,128)S(1)} %get-tuple-element.37.rr_ref), custom_call_target="tpu_custom_call" | custom-call | flops 400000000 | tf_op jit(solution)/shard_map/columns/pallas_call | solution.py:615
  5.6 1.6 %collective-permute-start.1 = (f32[16,128]{1,0:T(8,128)S(1)}, f32[16,128]{1,0:T(8,128)S(1)}, u32[]{:S(2)}, u32[]{:S(2)}) collective-permute-start(f32[16,128]{1,0:T(8,128)S(1)} %get-tuple-element.45), channel_id=1, source_target_pairs={{0,2},{1,3},{2,0},{3,1},{4,12},{5,13},{6,14},{7,15},{8,10},{9,11},... | collective-permute-start | bytes 24584 | tf_op jit(solution)/shard_map/ppermute | solution.py:640
  7.2 1.4 %collective-permute-start.3 = (f32[16,128]{1,0:T(8,128)S(1)}, f32[16,128]{1,0:T(8,128)S(1)}, u32[]{:S(2)}, u32[]{:S(2)}) collective-permute-start(f32[16,128]{1,0:T(8,128)S(1)} %get-tuple-element.47.after_ref.mine_ref), channel_id=1, source_target_pairs={{0,8},{1,9},{2,10},{3,11},{4,6},{5,7},{6,4},{7,5},{8,0},{9,1},{10,... | collective-permute-start | bytes 24584 | tf_op jit(solution)/shard_map/ppermute | solution.py:640
  8.6 0.1 collective-permute-start.7
  8.7 0.5 %collective-permute-start.8 = (f32[128,128]{1,0:T(8,128)S(1)}, f32[128,128]{1,0:T(8,128)S(1)}, u32[]{:S(2)}, u32[]{:S(2)}) collective-permute-start(f32[128,128]{1,0:T(8,128)S(1)} %get-tuple-element.59.yb_ref), channel_id=1, source_target_pairs={{0,8},{1,9},{2,4},{3,5},{4,2},{5,3},{6,14},{7,15},{8,0},{9,1},{10,... | collective-permute-start | bytes 196616 | tf_op jit(solution)/shard_map/ppermute | solution.py:640
  9.1 0.2 columns_beyond.1
  9.3 0.0 collective-permute-done.1.r0_ref
  9.3 0.4 %collective-permute-done.2.r1_ref = f32[16,128]{1,0:T(8,128)S(1)} collective-permute-done((f32[16,128]{1,0:T(8,128)S(1)}, f32[16,128]{1,0:T(8,128)S(1)}, u32[]{:S(2)}, u32[]{:S(2)}) %collective-permute-start.2) | collective-permute-done | bytes 8224 | tf_op jit(solution)/shard_map/ppermute | solution.py:640
  9.7 0.0 collective-permute-done.3.r2_ref
  9.7 0.2 %columns_more.1 = (f32[56,128]{1,0:T(8,128)S(1)}, f32[56,128]{1,0:T(8,128)S(1)}, f32[40,128]{1,0:T(8,128)S(1)}, f32[40,128]{1,0:T(8,128)S(1)}, f32[4,16,128]{2,1,0:T(8,128)S(1)}) custom-call(f32[16,128]{1,0:T(8,128)S(1)} %collective-permute-done.1.r0_ref, f32[16,128]{1,0:T(8,128)S(1)} %collective-permute-done.2.r1_ref, ...), custom_call_target="tpu_custom_call" | custom-call | flops 1000000000 | tf_op jit(solution)/shard_map/columns_more/pallas_call | solution.py:615
  9.9 3.3 %collective-permute-start.5 = (f32[56,128]{1,0:T(8,128)S(1)}, f32[56,128]{1,0:T(8,128)S(1)}, u32[]{:S(2)}, u32[]{:S(2)}) collective-permute-start(f32[56,128]{1,0:T(8,128)S(1)} %get-tuple-element.53), channel_id=1, source_target_pairs={{0,24},{1,25},{2,26},{3,27},{4,28},{5,29},{6,30},{7,31},{8,16},{9,... | collective-permute-start | bytes 86024 | tf_op jit(solution)/shard_map/ppermute | solution.py:640
  13.2 0.2 %outer.1 = (f32[16,32,128]{2,1,0:T(8,128)S(1)}, f32[16,32,128]{2,1,0:T(8,128)S(1)}) custom-call(f32[3,17,32,128]{3,2,1,0:T(8,128)S(1)} %get-tuple-element.36.kap_ref, f32[16,32,128]{2,1,0:T(8,128)S(1)} %get-tuple-element.37.rr_ref, f32[232,128]{1,0:T(8,128)S(1)} %collective-permute-done.4.bulk_ref, ...), custom_call_target="tpu_custom_call", output_to_operand_aliasing={{0}: (5, {}), {1}: (6, {})} | custom-call | flops 250000000 | tf_op jit(solution)/shard_map/outer/pallas_call | solution.py:615
  13.5 0.0 collective-permute-done.7.ra_ref
  13.5 0.4 %edge_rows.1 = (f32[16,32,128]{2,1,0:T(8,128)S(1)}, f32[16,32,128]{2,1,0:T(8,128)S(1)}) custom-call(f32[128,128]{1,0:T(8,128)S(1)} %get-tuple-element.58.ya_ref, f32[128,128]{1,0:T(8,128)S(1)} %get-tuple-element.59.yb_ref, f32[128,128]{1,0:T(8,128)S(1)} %collective-permute-done.7.ra_ref, ...), custom_call_target="tpu_custom_call", output_to_operand_aliasing={{0}: (4, {}), {1}: (5, {})} | custom-call | flops 400000000 | tf_op jit(solution)/shard_map/edge_rows/pallas_call | solution.py:615
  13.9 0.1 slab.1.slab_ref
  14.0 0.2 %rim.1 = (f32[32,128]{1,0:T(8,128)S(1)}, f32[32,128]{1,0:T(8,128)S(1)}) custom-call(f32[16,32,128]{2,1,0:T(8,128)S(1)} %get-tuple-element.63.s1_ref, f32[16,32,128]{2,1,0:T(8,128)S(1)} %get-tuple-element.64.s2_ref), custom_call_target="tpu_custom_call" | custom-call | flops 200000000 | tf_op jit(solution)/shard_map/rim/pallas_call | solution.py:615
  14.2 1.1 %collective-permute-done.5.rb_ref = f32[56,128]{1,0:T(8,128)S(1)} collective-permute-done((f32[56,128]{1,0:T(8,128)S(1)}, f32[56,128]{1,0:T(8,128)S(1)}, u32[]{:S(2)}, u32[]{:S(2)}) %collective-permute-start.5) | collective-permute-done | bytes 28704 | tf_op jit(solution)/shard_map/ppermute | solution.py:640
  15.3 1.4 %last.1 = (f32[16,32,128]{2,1,0:T(8,128)}, f32[2,4,16]{2,1,0:T(4,128)}) custom-call(f32[56,128]{1,0:T(8,128)S(1)} %collective-permute-done.5.rb_ref, f32[56,128]{1,0:T(8,128)S(1)} %collective-permute-done.6.ra_ref, f32[2,4,40,128]{3,2,1,0:T(8,128)S(1)} %slab.1.slab_ref, f32[4,16,128]{2,1,0:T(8,128)S(1)} %get-tuple-element.57.cor_ref, ...), custom_call_target="tpu_custom_call" | custom-call | flops 1500000000 | tf_op jit(solution)/shard_map/last/pallas_call | solution.py:615
  (7 shorter events, 0.0 us)
Async XLA Ops:
  2.3 3.3 %collective-permute-start = (f32[48,128]{1,0:T(8,128)S(1)}, f32[48,128]{1,0:T(8,128)S(1)}, u32[]{:S(2)}, u32[]{:S(2)}) collective-permute-start(f32[48,128]{1,0:T(8,128)S(1)} %get-tuple-element.35.mine_ref), channel_id=1, source_target_pairs={{0,1},{1,0},{2,3},{3,2},{4,5},{5,4},{6,7},{7,6},{8,9},{9,8},{10,11... | collective-permute-start | bytes 73736 | tf_op jit(solution)/shard_map/ppermute | solution.py:640
  2.9 5.8 %collective-permute-start.4 = (f32[232,128]{1,0:T(8,128)S(1)}, f32[232,128]{1,0:T(8,128)S(1)}, u32[]{:S(2)}, u32[]{:S(2)}) collective-permute-start(f32[232,128]{1,0:T(8,128)S(1)} %get-tuple-element.50), channel_id=1, source_target_pairs={{0,1},{1,0},{2,3},{3,2},{4,5},{5,4},{6,7},{7,6},{8,9},{9,8},{10,11... | collective-permute-start | bytes 356360 | tf_op jit(solution)/shard_map/ppermute | solution.py:640
  5.6 3.7 %collective-permute-start.1 = (f32[16,128]{1,0:T(8,128)S(1)}, f32[16,128]{1,0:T(8,128)S(1)}, u32[]{:S(2)}, u32[]{:S(2)}) collective-permute-start(f32[16,128]{1,0:T(8,128)S(1)} %get-tuple-element.45), channel_id=1, source_target_pairs={{0,2},{1,3},{2,0},{3,1},{4,12},{5,13},{6,14},{7,15},{8,10},{9,11},... | collective-permute-start | bytes 24584 | tf_op jit(solution)/shard_map/ppermute | solution.py:640
  7.2 2.5 %collective-permute-start.2 = (f32[16,128]{1,0:T(8,128)S(1)}, f32[16,128]{1,0:T(8,128)S(1)}, u32[]{:S(2)}, u32[]{:S(2)}) collective-permute-start(f32[16,128]{1,0:T(8,128)S(1)} %get-tuple-element.46), channel_id=1, source_target_pairs={{0,8},{1,9},{2,4},{3,5},{4,2},{5,3},{6,14},{7,15},{8,0},{9,1},{10,... | collective-permute-start | bytes 24584 | tf_op jit(solution)/shard_map/ppermute | solution.py:640
  7.2 2.5 %collective-permute-start.3 = (f32[16,128]{1,0:T(8,128)S(1)}, f32[16,128]{1,0:T(8,128)S(1)}, u32[]{:S(2)}, u32[]{:S(2)}) collective-permute-start(f32[16,128]{1,0:T(8,128)S(1)} %get-tuple-element.47.after_ref.mine_ref), channel_id=1, source_target_pairs={{0,8},{1,9},{2,10},{3,11},{4,6},{5,7},{6,4},{7,5},{8,0},{9,1},{10,... | collective-permute-start | bytes 24584 | tf_op jit(solution)/shard_map/ppermute | solution.py:640
  8.6 4.9 %collective-permute-start.7 = (f32[128,128]{1,0:T(8,128)S(1)}, f32[128,128]{1,0:T(8,128)S(1)}, u32[]{:S(2)}, u32[]{:S(2)}) collective-permute-start(f32[128,128]{1,0:T(8,128)S(1)} %get-tuple-element.58.ya_ref), channel_id=1, source_target_pairs={{0,2},{1,3},{2,0},{3,1},{4,6},{5,7},{6,4},{7,5},{8,10},{9,11},{10,... | collective-permute-start | bytes 196616 | tf_op jit(solution)/shard_map/ppermute | solution.py:640
  8.7 4.8 %collective-permute-start.8 = (f32[128,128]{1,0:T(8,128)S(1)}, f32[128,128]{1,0:T(8,128)S(1)}, u32[]{:S(2)}, u32[]{:S(2)}) collective-permute-start(f32[128,128]{1,0:T(8,128)S(1)} %get-tuple-element.59.yb_ref), channel_id=1, source_target_pairs={{0,8},{1,9},{2,4},{3,5},{4,2},{5,3},{6,14},{7,15},{8,0},{9,1},{10,... | collective-permute-start | bytes 196616 | tf_op jit(solution)/shard_map/ppermute | solution.py:640
  9.9 5.4 %collective-permute-start.5 = (f32[56,128]{1,0:T(8,128)S(1)}, f32[56,128]{1,0:T(8,128)S(1)}, u32[]{:S(2)}, u32[]{:S(2)}) collective-permute-start(f32[56,128]{1,0:T(8,128)S(1)} %get-tuple-element.53), channel_id=1, source_target_pairs={{0,24},{1,25},{2,26},{3,27},{4,28},{5,29},{6,30},{7,31},{8,16},{9,... | collective-permute-start | bytes 86024 | tf_op jit(solution)/shard_map/ppermute | solution.py:640
  13.2 2.1 %collective-permute-start.6 = (f32[56,128]{1,0:T(8,128)S(1)}, f32[56,128]{1,0:T(8,128)S(1)}, u32[]{:S(2)}, u32[]{:S(2)}) collective-permute-start(f32[56,128]{1,0:T(8,128)S(1)} %get-tuple-element.54.after_ref), channel_id=1, source_target_pairs={{0,8},{1,9},{2,10},{3,11},{4,12},{5,13},{6,14},{7,15},{8,0},{9,1},... | collective-permute-start | bytes 86024 | tf_op jit(solution)/shard_map/ppermute | solution.py:640

commit v8 on v7

--- a/solution.py
+++ b/solution.py
@@ -32,7 +32,7 @@
 GROUP = NZ + 2
 RROW = 3 * KROWS
 YPAY = 128
-XPAY = 40 + 16
+XPAY = 40 + 8
 RLANE = 110
 
 
@@ -307,8 +307,8 @@
     zc, xs = lane >> 5, lane & 31
     pair = jnp.where(zc < 2, zc, 3 - zc)
     own = (xs >= 4) & (xs < 20)
-    low_half, xs16 = lane < 64, iota((16, NX), 1) & 31
-    sides = [jnp.zeros((16, NX), F32), jnp.zeros((16, NX), F32)]
+    low_half = lane < 64
+    sides = [jnp.zeros((8, NX), F32), jnp.zeros((8, NX), F32)]
     for q in range(4):
         at = (q * 2 + pair) * CX + jnp.clip(xs - 4, 0, CX - 1)
         below, mine, above = ((v, roll(v, 4, 0)) for v in (jnp.where(own, take(t, at), 0.0) for t in tiles))
@@ -317,7 +317,8 @@
         whole = jnp.concatenate([first, second], axis=0)
         cor_ref[q] = whole
         for i, start in enumerate((4, CX)):
-            sides[i] = jnp.where((xs16 >= 4 * q) & (xs16 < 4 * q + 4), roll(whole, 4 * q - start, 1), sides[i])
+            for half, to in ((first, 4 * q), (second, 4 * q + 16)):
+                sides[i] = jnp.where((xs >= to) & (xs < to + 4), roll(half, to - start, 1), sides[i])
     xa_ref[40:XPAY] = jnp.where(even_x, sides[1], sides[0])
     xb_ref[40:XPAY] = jnp.where(even_x, sides[0], sides[1])
 
@@ -536,11 +537,14 @@
 
 
 def coarse_solve(cor_ref, lower, upper):
-    xs = iota((16, NX), 1) & 31
+    xs = iota((8, NX), 1) & 31
     arrays = []
     for q in range(4):
-        whole = jnp.where(xs < 4, roll(lower, -4 * q, 1), cor_ref[q])
-        arrays.append(jnp.where((xs >= 20) & (xs < 24), roll(upper, 20 - 4 * q, 1), whole))
+        halves = []
+        for i, from_ in enumerate((4 * q, 4 * q + 16)):
+            half = jnp.where(xs < 4, roll(lower, -from_, 1), cor_ref[q, 8 * i : 8 * i + 8])
+            halves.append(jnp.where((xs >= 20) & (xs < 24), roll(upper, 20 - from_, 1), half))
+        arrays.append(jnp.concatenate(halves, axis=0))
     kc, rhs = arrays[:3], arrays[3]
     lane = iota((16, NX), 1)
 

time: 17 us -> 16.9 us (level)
  no operation moved by 1% of the time
where the time goes in v8:
time: 16.9 us; the launch traced here: 16.7 us
  starting transfers between devices  8.28 us (49%)
  Pallas kernels  6.17 us (37%)
  waiting for transfers between devices  1.46 us (9%)
  between operations  0.74 us (4%)
    ppermute x9, starting transfers between devices, exchange(): return lax.ppermute(values, ('gx', 'gy', 'gz'), pairs)  8.28 us
    pallas_call x13, Pallas kernels, call(): pl.pallas_call(kernel, out_shape=outputs, in_specs=[pl.BlockSpec(memory_s...  6.17 us
    ppermute x9, waiting for transfers between devices, exchange(): return lax.ppermute(values, ('gx', 'gy', 'gz'), pairs)  1.46 us
  transfers between devices with their start and end apart: 9, of which 2 were waited for; matrix products, arithmetic and copies ran while one was open for 0% of the time, Pallas kernels for 18%

profile of v8, /device:TPU:19, one launch (start us, length us, event | category | flops | bytes accessed | tf_op | source)
XLA Modules:
  0.0 16.7 jit_solution(10796106917163929815)
XLA Ops:
  0.6 1.7 %stiffness.1 = (f32[3,17,32,128]{3,2,1,0:T(8,128)S(1)}, f32[16,32,128]{2,1,0:T(8,128)S(1)}, f32[16,32,128]{2,1,0:T(8,128)S(1)}, f32[48,128]{1,0:T(8,128)S(1)}) custom-call(f32[16,32,128]{2,1,0:T(8,128)} %r_hbm.1, s32[16,32,128]{2,1,0:T(8,128)} %lab_hbm.1, f32[3,16,32,128]{3,2,1,0:T(8,128)} %fac_hbm.1, f32[4,8,8,8]{3,2,1,0:T(8,128)} %bas_hbm.1, ...), custom_call_target="tpu_custom_call" | custom-call | flops 1800000000 | tf_op jit(solution)/shard_map/stiffness/pallas_call | solution.py:619
  2.3 0.3 %collective-permute-start = (f32[48,128]{1,0:T(8,128)S(1)}, f32[48,128]{1,0:T(8,128)S(1)}, u32[]{:S(2)}, u32[]{:S(2)}) collective-permute-start(f32[48,128]{1,0:T(8,128)S(1)} %get-tuple-element.35.mine_ref), channel_id=1, source_target_pairs={{0,1},{1,0},{2,3},{3,2},{4,5},{5,4},{6,7},{7,6},{8,9},{9,8},{10,11... | collective-permute-start | bytes 73736 | tf_op jit(solution)/shard_map/ppermute | solution.py:644
  2.7 0.2 %rows.1 = (f32[128,128]{1,0:T(8,128)S(1)}, f32[128,128]{1,0:T(8,128)S(1)}, f32[232,128]{1,0:T(8,128)S(1)}) custom-call(f32[3,17,32,128]{3,2,1,0:T(8,128)S(1)} %get-tuple-element.36.kap_ref, f32[16,32,128]{2,1,0:T(8,128)S(1)} %get-tuple-element.37.rr_ref), custom_call_target="tpu_custom_call" | custom-call | flops 100000000 | tf_op jit(solution)/shard_map/rows/pallas_call | solution.py:619
  2.9 1.2 %collective-permute-start.4 = (f32[232,128]{1,0:T(8,128)S(1)}, f32[232,128]{1,0:T(8,128)S(1)}, u32[]{:S(2)}, u32[]{:S(2)}) collective-permute-start(f32[232,128]{1,0:T(8,128)S(1)} %get-tuple-element.50), channel_id=1, source_target_pairs={{0,1},{1,0},{2,3},{3,2},{4,5},{5,4},{6,7},{7,6},{8,9},{9,8},{10,11... | collective-permute-start | bytes 356360 | tf_op jit(solution)/shard_map/ppermute | solution.py:644
  4.1 0.5 %inner_first.1 = (f32[16,32,128]{2,1,0:T(8,128)S(1)}, f32[16,32,128]{2,1,0:T(8,128)S(1)}, f32[3,16,32,128]{3,2,1,0:T(8,128)S(1)}) custom-call(f32[3,17,32,128]{3,2,1,0:T(8,128)S(1)} %get-tuple-element.36.kap_ref, f32[16,32,128]{2,1,0:T(8,128)S(1)} %get-tuple-element.37.rr_ref), custom_call_target="tpu_custom_call" | custom-call | flops 600000000 | tf_op jit(solution)/shard_map/inner_first/pallas_call | solution.py:619
  4.6 0.7 %inner_image.1 = (f32[16,32,128]{2,1,0:T(8,128)S(1)}, f32[16,32,128]{2,1,0:T(8,128)S(1)}) custom-call(f32[3,17,32,128]{3,2,1,0:T(8,128)S(1)} %get-tuple-element.36.kap_ref, f32[16,32,128]{2,1,0:T(8,128)S(1)} %get-tuple-element.41.f_ref.f_in, f32[3,16,32,128]{3,2,1,0:T(8,128)S(1)} %get-tuple-element.42.p_ref.p_in, ...), custom_call_target="tpu_custom_call", output_to_operand_aliasing={{0}: (3, {})} | custom-call | flops 700000000 | tf_op jit(solution)/shard_map/inner_image/pallas_call | solution.py:619
  5.3 0.3 %columns.1 = (f32[32,128]{1,0:T(8,128)S(1)}, f32[32,128]{1,0:T(8,128)S(1)}, f32[8,128]{1,0:T(8,128)S(1)}) custom-call(f32[3,17,32,128]{3,2,1,0:T(8,128)S(1)} %get-tuple-element.36.kap_ref, f32[16,32,128]{2,1,0:T(8,128)S(1)} %get-tuple-element.37.rr_ref), custom_call_target="tpu_custom_call" | custom-call | flops 400000000 | tf_op jit(solution)/shard_map/columns/pallas_call | solution.py:619
  5.7 1.5 %collective-permute-start.1 = (f32[16,128]{1,0:T(8,128)S(1)}, f32[16,128]{1,0:T(8,128)S(1)}, u32[]{:S(2)}, u32[]{:S(2)}) collective-permute-start(f32[16,128]{1,0:T(8,128)S(1)} %get-tuple-element.45), channel_id=1, source_target_pairs={{0,2},{1,3},{2,0},{3,1},{4,12},{5,13},{6,14},{7,15},{8,10},{9,11},... | collective-permute-start | bytes 24584 | tf_op jit(solution)/shard_map/ppermute | solution.py:644
  7.2 0.0 collective-permute-start.2
  7.2 1.4 %collective-permute-start.3 = (f32[16,128]{1,0:T(8,128)S(1)}, f32[16,128]{1,0:T(8,128)S(1)}, u32[]{:S(2)}, u32[]{:S(2)}) collective-permute-start(f32[16,128]{1,0:T(8,128)S(1)} %get-tuple-element.47.after_ref.mine_ref), channel_id=1, source_target_pairs={{0,8},{1,9},{2,10},{3,11},{4,6},{5,7},{6,4},{7,5},{8,0},{9,1},{10,... | collective-permute-start | bytes 24584 | tf_op jit(solution)/shard_map/ppermute | solution.py:644
  8.6 0.1 collective-permute-start.7
  8.7 0.0 collective-permute-done.4.bulk_ref
  8.7 0.5 %collective-permute-start.8 = (f32[128,128]{1,0:T(8,128)S(1)}, f32[128,128]{1,0:T(8,128)S(1)}, u32[]{:S(2)}, u32[]{:S(2)}) collective-permute-start(f32[128,128]{1,0:T(8,128)S(1)} %get-tuple-element.59.yb_ref), channel_id=1, source_target_pairs={{0,8},{1,9},{2,4},{3,5},{4,2},{5,3},{6,14},{7,15},{8,0},{9,1},{10,... | collective-permute-start | bytes 196616 | tf_op jit(solution)/shard_map/ppermute | solution.py:644
  9.1 0.2 columns_beyond.1
  9.3 0.4 %collective-permute-done.2.r1_ref = f32[16,128]{1,0:T(8,128)S(1)} collective-permute-done((f32[16,128]{1,0:T(8,128)S(1)}, f32[16,128]{1,0:T(8,128)S(1)}, u32[]{:S(2)}, u32[]{:S(2)}) %collective-permute-start.2) | collective-permute-done | bytes 8224 | tf_op jit(solution)/shard_map/ppermute | solution.py:644
  9.7 0.0 collective-permute-done.3.r2_ref
  9.7 0.2 %columns_more.1 = (f32[48,128]{1,0:T(8,128)S(1)}, f32[48,128]{1,0:T(8,128)S(1)}, f32[40,128]{1,0:T(8,128)S(1)}, f32[40,128]{1,0:T(8,128)S(1)}, f32[4,16,128]{2,1,0:T(8,128)S(1)}) custom-call(f32[16,128]{1,0:T(8,128)S(1)} %collective-permute-done.1.r0_ref, f32[16,128]{1,0:T(8,128)S(1)} %collective-permute-done.2.r1_ref, ...), custom_call_target="tpu_custom_call" | custom-call | flops 1000000000 | tf_op jit(solution)/shard_map/columns_more/pallas_call | solution.py:619
  9.9 3.3 %collective-permute-start.5 = (f32[48,128]{1,0:T(8,128)S(1)}, f32[48,128]{1,0:T(8,128)S(1)}, u32[]{:S(2)}, u32[]{:S(2)}) collective-permute-start(f32[48,128]{1,0:T(8,128)S(1)} %get-tuple-element.53), channel_id=1, source_target_pairs={{0,24},{1,25},{2,26},{3,27},{4,28},{5,29},{6,30},{7,31},{8,16},{9,... | collective-permute-start | bytes 73736 | tf_op jit(solution)/shard_map/ppermute | solution.py:644
  13.2 0.2 %outer.1 = (f32[16,32,128]{2,1,0:T(8,128)S(1)}, f32[16,32,128]{2,1,0:T(8,128)S(1)}) custom-call(f32[3,17,32,128]{3,2,1,0:T(8,128)S(1)} %get-tuple-element.36.kap_ref, f32[16,32,128]{2,1,0:T(8,128)S(1)} %get-tuple-element.37.rr_ref, f32[232,128]{1,0:T(8,128)S(1)} %collective-permute-done.4.bulk_ref, ...), custom_call_target="tpu_custom_call", output_to_operand_aliasing={{0}: (5, {}), {1}: (6, {})} | custom-call | flops 250000000 | tf_op jit(solution)/shard_map/outer/pallas_call | solution.py:619
  13.5 0.4 %edge_rows.1 = (f32[16,32,128]{2,1,0:T(8,128)S(1)}, f32[16,32,128]{2,1,0:T(8,128)S(1)}) custom-call(f32[128,128]{1,0:T(8,128)S(1)} %get-tuple-element.58.ya_ref, f32[128,128]{1,0:T(8,128)S(1)} %get-tuple-element.59.yb_ref, f32[128,128]{1,0:T(8,128)S(1)} %collective-permute-done.7.ra_ref, ...), custom_call_target="tpu_custom_call", output_to_operand_aliasing={{0}: (4, {}), {1}: (5, {})} | custom-call | flops 400000000 | tf_op jit(solution)/shard_map/edge_rows/pallas_call | solution.py:619
  13.9 0.1 slab.1.slab_ref
  14.0 0.2 %rim.1 = (f32[32,128]{1,0:T(8,128)S(1)}, f32[32,128]{1,0:T(8,128)S(1)}) custom-call(f32[16,32,128]{2,1,0:T(8,128)S(1)} %get-tuple-element.63.s1_ref, f32[16,32,128]{2,1,0:T(8,128)S(1)} %get-tuple-element.64.s2_ref), custom_call_target="tpu_custom_call" | custom-call | flops 200000000 | tf_op jit(solution)/shard_map/rim/pallas_call | solution.py:619
  14.2 1.0 %collective-permute-done.5.rb_ref = f32[48,128]{1,0:T(8,128)S(1)} collective-permute-done((f32[48,128]{1,0:T(8,128)S(1)}, f32[48,128]{1,0:T(8,128)S(1)}, u32[]{:S(2)}, u32[]{:S(2)}) %collective-permute-start.5) | collective-permute-done | bytes 24608 | tf_op jit(solution)/shard_map/ppermute | solution.py:644
  15.3 1.4 %last.1 = (f32[16,32,128]{2,1,0:T(8,128)}, f32[2,4,16]{2,1,0:T(4,128)}) custom-call(f32[48,128]{1,0:T(8,128)S(1)} %collective-permute-done.5.rb_ref, f32[48,128]{1,0:T(8,128)S(1)} %collective-permute-done.6.ra_ref, f32[2,4,40,128]{3,2,1,0:T(8,128)S(1)} %slab.1.slab_ref, f32[4,16,128]{2,1,0:T(8,128)S(1)} %get-tuple-element.57.cor_ref, ...), custom_call_target="tpu_custom_call" | custom-call | flops 1500000000 | tf_op jit(solution)/shard_map/last/pallas_call | solution.py:619
  (7 shorter events, 0.0 us)
Async XLA Ops:
  2.3 3.3 %collective-permute-start = (f32[48,128]{1,0:T(8,128)S(1)}, f32[48,128]{1,0:T(8,128)S(1)}, u32[]{:S(2)}, u32[]{:S(2)}) collective-permute-start(f32[48,128]{1,0:T(8,128)S(1)} %get-tuple-element.35.mine_ref), channel_id=1, source_target_pairs={{0,1},{1,0},{2,3},{3,2},{4,5},{5,4},{6,7},{7,6},{8,9},{9,8},{10,11... | collective-permute-start | bytes 73736 | tf_op jit(solution)/shard_map/ppermute | solution.py:644
  2.9 5.8 %collective-permute-start.4 = (f32[232,128]{1,0:T(8,128)S(1)}, f32[232,128]{1,0:T(8,128)S(1)}, u32[]{:S(2)}, u32[]{:S(2)}) collective-permute-start(f32[232,128]{1,0:T(8,128)S(1)} %get-tuple-element.50), channel_id=1, source_target_pairs={{0,1},{1,0},{2,3},{3,2},{4,5},{5,4},{6,7},{7,6},{8,9},{9,8},{10,11... | collective-permute-start | bytes 356360 | tf_op jit(solution)/shard_map/ppermute | solution.py:644
  5.7 3.6 %collective-permute-start.1 = (f32[16,128]{1,0:T(8,128)S(1)}, f32[16,128]{1,0:T(8,128)S(1)}, u32[]{:S(2)}, u32[]{:S(2)}) collective-permute-start(f32[16,128]{1,0:T(8,128)S(1)} %get-tuple-element.45), channel_id=1, source_target_pairs={{0,2},{1,3},{2,0},{3,1},{4,12},{5,13},{6,14},{7,15},{8,10},{9,11},... | collective-permute-start | bytes 24584 | tf_op jit(solution)/shard_map/ppermute | solution.py:644
  7.2 2.5 %collective-permute-start.2 = (f32[16,128]{1,0:T(8,128)S(1)}, f32[16,128]{1,0:T(8,128)S(1)}, u32[]{:S(2)}, u32[]{:S(2)}) collective-permute-start(f32[16,128]{1,0:T(8,128)S(1)} %get-tuple-element.46), channel_id=1, source_target_pairs={{0,8},{1,9},{2,4},{3,5},{4,2},{5,3},{6,14},{7,15},{8,0},{9,1},{10,... | collective-permute-start | bytes 24584 | tf_op jit(solution)/shard_map/ppermute | solution.py:644
  7.2 2.5 %collective-permute-start.3 = (f32[16,128]{1,0:T(8,128)S(1)}, f32[16,128]{1,0:T(8,128)S(1)}, u32[]{:S(2)}, u32[]{:S(2)}) collective-permute-start(f32[16,128]{1,0:T(8,128)S(1)} %get-tuple-element.47.after_ref.mine_ref), channel_id=1, source_target_pairs={{0,8},{1,9},{2,10},{3,11},{4,6},{5,7},{6,4},{7,5},{8,0},{9,1},{10,... | collective-permute-start | bytes 24584 | tf_op jit(solution)/shard_map/ppermute | solution.py:644
  8.6 4.9 %collective-permute-start.7 = (f32[128,128]{1,0:T(8,128)S(1)}, f32[128,128]{1,0:T(8,128)S(1)}, u32[]{:S(2)}, u32[]{:S(2)}) collective-permute-start(f32[128,128]{1,0:T(8,128)S(1)} %get-tuple-element.58.ya_ref), channel_id=1, source_target_pairs={{0,2},{1,3},{2,0},{3,1},{4,6},{5,7},{6,4},{7,5},{8,10},{9,11},{10,... | collective-permute-start | bytes 196616 | tf_op jit(solution)/shard_map/ppermute | solution.py:644
  8.7 4.8 %collective-permute-start.8 = (f32[128,128]{1,0:T(8,128)S(1)}, f32[128,128]{1,0:T(8,128)S(1)}, u32[]{:S(2)}, u32[]{:S(2)}) collective-permute-start(f32[128,128]{1,0:T(8,128)S(1)} %get-tuple-element.59.yb_ref), channel_id=1, source_target_pairs={{0,8},{1,9},{2,4},{3,5},{4,2},{5,3},{6,14},{7,15},{8,0},{9,1},{10,... | collective-permute-start | bytes 196616 | tf_op jit(solution)/shard_map/ppermute | solution.py:644
  9.9 5.3 %collective-permute-start.5 = (f32[48,128]{1,0:T(8,128)S(1)}, f32[48,128]{1,0:T(8,128)S(1)}, u32[]{:S(2)}, u32[]{:S(2)}) collective-permute-start(f32[48,128]{1,0:T(8,128)S(1)} %get-tuple-element.53), channel_id=1, source_target_pairs={{0,24},{1,25},{2,26},{3,27},{4,28},{5,29},{6,30},{7,31},{8,16},{9,... | collective-permute-start | bytes 73736 | tf_op jit(solution)/shard_map/ppermute | solution.py:644
  13.2 2.1 %collective-permute-start.6 = (f32[48,128]{1,0:T(8,128)S(1)}, f32[48,128]{1,0:T(8,128)S(1)}, u32[]{:S(2)}, u32[]{:S(2)}) collective-permute-start(f32[48,128]{1,0:T(8,128)S(1)} %get-tuple-element.54.after_ref), channel_id=1, source_target_pairs={{0,8},{1,9},{2,10},{3,11},{4,12},{5,13},{6,14},{7,15},{8,0},{9,1},... | collective-permute-start | bytes 73736 | tf_op jit(solution)/shard_map/ppermute | solution.py:644

commit v9 on v8

--- a/solution.py
+++ b/solution.py
@@ -24,8 +24,8 @@
 F32 = jnp.float32
 HIGHEST = lax.Precision.HIGHEST
 
-BULK = 7 * NY + 8
-BCOL = 7 * NY
+BULK = 5 * NY + 8
+BCOL = 5 * NY
 URGENT = 16
 ZURGENT = 48
 KROWS = 36
@@ -197,10 +197,11 @@
             put(at, kap_ref[a, zp + 1, 1:2], kap_ref[a, zp + 1, NY - 2 : NY - 1])
             put(at + GROUP, kap_ref[a, zp + 1, 0:1], kap_ref[a, zp + 1, NY - 1 : NY])
         put(RROW + zp, rr_ref[place(zp), 0:1], rr_ref[place(zp), NY - 1 : NY])
-    for a in range(3):
-        for s in range(2):
-            bulk_ref[(2 * a + s) * NY : (2 * a + s + 1) * NY] = kap_ref[a, NZ - s]
-    bulk_ref[6 * NY : 7 * NY] = rr_ref[place(NZ - 1)]
+    face, second = ([kap_ref[a, NZ - s] for a in range(3)] for s in range(2))
+    part_0, part_y, part_x, part_yx = pair_stiffness(face, (None, None, None), second)
+    diag = SELF * (face[0] + face[1] + face[2]) + part_0 + both(part_y, 1, 0)
+    for i, plane in enumerate(face + [rr_ref[place(NZ - 1)], diag + both(part_x + both(part_yx, 1, 0), 1, 1)]):
+        bulk_ref[i * NY : (i + 1) * NY] = plane
     planes = [kap_ref[a, NZ - s] for a in range(3) for s in range(2)] + [rr_ref[place(NZ - 1)]]
     lane = iota((NY, NX), 1)
     columns = jnp.zeros((NY, NX), F32)
@@ -332,8 +333,7 @@
     f_ref[zp + 1] = f
     for a in range(3):
         p_ref[a, zp + 1] = k[a] * f
-    if to < NZ if isinstance(to, int) else True:
-        s1_ref[to] = WEIGHT_TWO * inv
+    s1_ref[to] = WEIGHT_TWO * inv
 
 
 def image_plane(to, zp, kap_ref, f_ref, p_ref, s1_ref, s2_ref, rim):
@@ -386,13 +386,19 @@
     for a in range(3):
         for i in range(3):
             k_ref[a, i] = kap_ref[a, NZ - 2 + i]
+        k_ref[a, 3] = bulk_ref[a * NY : (a + 1) * NY]
         for i in range(2):
-            k_ref[a, 3 + i] = bulk_ref[(2 * a + i) * NY : (2 * a + i + 1) * NY]
             p_ref[a, i] = p_in[a, NZ - 2 + i]
     for i in range(2):
         f_ref[i] = f_in[NZ - 2 + i]
     first_plane(NZ - 1, 1, k_ref, rr_ref[place(NZ - 1)], f_ref, p_ref, s1_ref, rim)
-    first_plane(NZ, 2, k_ref, bulk_ref[6 * NY : 7 * NY], f_ref, p_ref, s1_ref, rim)
+    k0, k1, k2 = (k_ref[a, 2] for a in range(3))
+    diag = bulk_ref[4 * NY : 5 * NY] + 0.5 * k0 + both(0.125 * (k0 + k1), 1, 0)
+    diag = diag + both(0.125 * (k0 + k2) + both((1.0 / 24.0) * (k0 + k1 + k2), 1, 0), 1, 1)
+    f = jnp.where(rim, 0.0, WEIGHT_ONE * bulk_ref[3 * NY : 4 * NY] / diag)
+    f_ref[3] = f
+    for a in range(3):
+        p_ref[a, 3] = k_ref[a, 3] * f
     for i in range(2):
         image_plane(NZ - 2 + i, i, k_ref, f_ref, p_ref, s1_ref, s2_ref, rim)
 
@@ -739,7 +745,7 @@
             outer_kernel,
             [kap, rr, zb, f, p, s1, s2, xa],
             [vmem(NZ, NY, NX), vmem(NZ, NY, NX)],
-            [pltpu.VMEM((3, 5, NY, NX), F32), pltpu.VMEM((4, NY, NX), F32), pltpu.VMEM((3, 4, NY, NX), F32)],
+            [pltpu.VMEM((3, 4, NY, NX), F32), pltpu.VMEM((4, NY, NX), F32), pltpu.VMEM((3, 4, NY, NX), F32)],
             aliases={5: 0, 6: 1},
             us=0.25,
             name="outer",

time: 16.9 us -> 16.5 us (0.976)
  the two profiles are of different devices: /device:TPU:19 before, /device:TPU:0 now
where the time goes in v9:
time: 16.5 us; the launch traced here: 16.3 us
  starting transfers between devices  8.8 us (53%)
  Pallas kernels  6.17 us (37%)
  between operations  0.73 us (4%)
  waiting for transfers between devices  0.63 us (4%)
    ppermute x9, starting transfers between devices, exchange(): return lax.ppermute(values, ('gx', 'gy', 'gz'), pairs)  8.8 us
    pallas_call x13, Pallas kernels, call(): pl.pallas_call(kernel, out_shape=outputs, in_specs=[pl.BlockSpec(memory_s...  6.17 us
    ppermute x9, waiting for transfers between devices, exchange(): return lax.ppermute(values, ('gx', 'gy', 'gz'), pairs)  0.63 us
  transfers between devices with their start and end apart: 9, of which 2 were waited for; matrix products, arithmetic and copies ran while one was open for 0% of the time, Pallas kernels for 19%

profile of v9, /device:TPU:0, one launch (start us, length us, event | category | flops | bytes accessed | tf_op | source)
XLA Modules:
  0.0 16.3 jit_solution(6230162210637041955)
XLA Ops:
  0.6 1.7 %stiffness.1 = (f32[3,17,32,128]{3,2,1,0:T(8,128)S(1)}, f32[16,32,128]{2,1,0:T(8,128)S(1)}, f32[16,32,128]{2,1,0:T(8,128)S(1)}, f32[48,128]{1,0:T(8,128)S(1)}) custom-call(f32[16,32,128]{2,1,0:T(8,128)} %r_hbm.1, s32[16,32,128]{2,1,0:T(8,128)} %lab_hbm.1, f32[3,16,32,128]{3,2,1,0:T(8,128)} %fac_hbm.1, f32[4,8,8,8]{3,2,1,0:T(8,128)} %bas_hbm.1, ...), custom_call_target="tpu_custom_call" | custom-call | flops 1800000000 | tf_op jit(solution)/shard_map/stiffness/pallas_call | solution.py:625
  2.3 3.0 %collective-permute-start = (f32[48,128]{1,0:T(8,128)S(1)}, f32[48,128]{1,0:T(8,128)S(1)}, u32[]{:S(2)}, u32[]{:S(2)}) collective-permute-start(f32[48,128]{1,0:T(8,128)S(1)} %get-tuple-element.35.mine_ref), channel_id=1, source_target_pairs={{0,1},{1,0},{2,3},{3,2},{4,5},{5,4},{6,7},{7,6},{8,9},{9,8},{10,11... | collective-permute-start | bytes 73736 | tf_op jit(solution)/shard_map/ppermute | solution.py:650
  5.3 0.2 %rows.1 = (f32[128,128]{1,0:T(8,128)S(1)}, f32[128,128]{1,0:T(8,128)S(1)}, f32[168,128]{1,0:T(8,128)S(1)}) custom-call(f32[3,17,32,128]{3,2,1,0:T(8,128)S(1)} %get-tuple-element.36.kap_ref, f32[16,32,128]{2,1,0:T(8,128)S(1)} %get-tuple-element.37.rr_ref), custom_call_target="tpu_custom_call" | custom-call | flops 100000000 | tf_op jit(solution)/shard_map/rows/pallas_call | solution.py:625
  5.6 0.0 collective-permute-start.4
  5.6 0.5 %inner_first.1 = (f32[16,32,128]{2,1,0:T(8,128)S(1)}, f32[16,32,128]{2,1,0:T(8,128)S(1)}, f32[3,16,32,128]{3,2,1,0:T(8,128)S(1)}) custom-call(f32[3,17,32,128]{3,2,1,0:T(8,128)S(1)} %get-tuple-element.36.kap_ref, f32[16,32,128]{2,1,0:T(8,128)S(1)} %get-tuple-element.37.rr_ref), custom_call_target="tpu_custom_call" | custom-call | flops 600000000 | tf_op jit(solution)/shard_map/inner_first/pallas_call | solution.py:625
  6.1 0.7 %inner_image.1 = (f32[16,32,128]{2,1,0:T(8,128)S(1)}, f32[16,32,128]{2,1,0:T(8,128)S(1)}) custom-call(f32[3,17,32,128]{3,2,1,0:T(8,128)S(1)} %get-tuple-element.36.kap_ref, f32[16,32,128]{2,1,0:T(8,128)S(1)} %get-tuple-element.41.f_ref.f_in, f32[3,16,32,128]{3,2,1,0:T(8,128)S(1)} %get-tuple-element.42.p_ref.p_in, ...), custom_call_target="tpu_custom_call", output_to_operand_aliasing={{0}: (3, {})} | custom-call | flops 700000000 | tf_op jit(solution)/shard_map/inner_image/pallas_call | solution.py:625
  6.8 0.3 %columns.1 = (f32[32,128]{1,0:T(8,128)S(1)}, f32[32,128]{1,0:T(8,128)S(1)}, f32[8,128]{1,0:T(8,128)S(1)}) custom-call(f32[3,17,32,128]{3,2,1,0:T(8,128)S(1)} %get-tuple-element.36.kap_ref, f32[16,32,128]{2,1,0:T(8,128)S(1)} %get-tuple-element.37.rr_ref), custom_call_target="tpu_custom_call" | custom-call | flops 400000000 | tf_op jit(solution)/shard_map/columns/pallas_call | solution.py:625
  7.1 0.0 collective-permute-done.far_ref
  7.2 2.2 %collective-permute-start.1 = (f32[16,128]{1,0:T(8,128)S(1)}, f32[16,128]{1,0:T(8,128)S(1)}, u32[]{:S(2)}, u32[]{:S(2)}) collective-permute-start(f32[16,128]{1,0:T(8,128)S(1)} %get-tuple-element.45), channel_id=1, source_target_pairs={{0,2},{1,3},{2,0},{3,1},{4,12},{5,13},{6,14},{7,15},{8,10},{9,11},... | collective-permute-start | bytes 24584 | tf_op jit(solution)/shard_map/ppermute | solution.py:650
  9.3 0.0 collective-permute-start.2
  9.4 0.5 %collective-permute-start.3 = (f32[16,128]{1,0:T(8,128)S(1)}, f32[16,128]{1,0:T(8,128)S(1)}, u32[]{:S(2)}, u32[]{:S(2)}) collective-permute-start(f32[16,128]{1,0:T(8,128)S(1)} %get-tuple-element.47.after_ref.mine_ref), channel_id=1, source_target_pairs={{0,8},{1,9},{2,10},{3,11},{4,6},{5,7},{6,4},{7,5},{8,0},{9,1},{10,... | collective-permute-start | bytes 24584 | tf_op jit(solution)/shard_map/ppermute | solution.py:650
  9.9 1.3 %collective-permute-start.7 = (f32[128,128]{1,0:T(8,128)S(1)}, f32[128,128]{1,0:T(8,128)S(1)}, u32[]{:S(2)}, u32[]{:S(2)}) collective-permute-start(f32[128,128]{1,0:T(8,128)S(1)} %get-tuple-element.58.ya_ref), channel_id=1, source_target_pairs={{0,2},{1,3},{2,0},{3,1},{4,6},{5,7},{6,4},{7,5},{8,10},{9,11},{10,... | collective-permute-start | bytes 196616 | tf_op jit(solution)/shard_map/ppermute | solution.py:650
  11.2 0.1 collective-permute-start.8
  11.2 0.2 columns_beyond.1
  11.4 0.2 %columns_more.1 = (f32[48,128]{1,0:T(8,128)S(1)}, f32[48,128]{1,0:T(8,128)S(1)}, f32[40,128]{1,0:T(8,128)S(1)}, f32[40,128]{1,0:T(8,128)S(1)}, f32[4,16,128]{2,1,0:T(8,128)S(1)}) custom-call(f32[16,128]{1,0:T(8,128)S(1)} %collective-permute-done.1.r0_ref, f32[16,128]{1,0:T(8,128)S(1)} %collective-permute-done.2.r1_ref, ...), custom_call_target="tpu_custom_call" | custom-call | flops 1000000000 | tf_op jit(solution)/shard_map/columns_more/pallas_call | solution.py:625
  11.6 1.6 %collective-permute-start.5 = (f32[48,128]{1,0:T(8,128)S(1)}, f32[48,128]{1,0:T(8,128)S(1)}, u32[]{:S(2)}, u32[]{:S(2)}) collective-permute-start(f32[48,128]{1,0:T(8,128)S(1)} %get-tuple-element.53), channel_id=1, source_target_pairs={{0,24},{1,25},{2,26},{3,27},{4,28},{5,29},{6,30},{7,31},{8,16},{9,... | collective-permute-start | bytes 73736 | tf_op jit(solution)/shard_map/ppermute | solution.py:650
  13.2 0.1 collective-permute-start.6
  13.3 0.1 slab.1.slab_ref
  13.5 0.3 %outer.1 = (f32[16,32,128]{2,1,0:T(8,128)S(1)}, f32[16,32,128]{2,1,0:T(8,128)S(1)}) custom-call(f32[3,17,32,128]{3,2,1,0:T(8,128)S(1)} %get-tuple-element.36.kap_ref, f32[16,32,128]{2,1,0:T(8,128)S(1)} %get-tuple-element.37.rr_ref, f32[168,128]{1,0:T(8,128)S(1)} %collective-permute-done.4.bulk_ref, ...), custom_call_target="tpu_custom_call", output_to_operand_aliasing={{0}: (5, {}), {1}: (6, {})} | custom-call | flops 250000000 | tf_op jit(solution)/shard_map/outer/pallas_call | solution.py:625
  13.7 0.4 %collective-permute-done.7.ra_ref = f32[128,128]{1,0:T(8,128)S(1)} collective-permute-done((f32[128,128]{1,0:T(8,128)S(1)}, f32[128,128]{1,0:T(8,128)S(1)}, u32[]{:S(2)}, u32[]{:S(2)}) %collective-permute-start.7) | collective-permute-done | bytes 65568 | tf_op jit(solution)/shard_map/ppermute | solution.py:650
  14.1 0.4 %edge_rows.1 = (f32[16,32,128]{2,1,0:T(8,128)S(1)}, f32[16,32,128]{2,1,0:T(8,128)S(1)}) custom-call(f32[128,128]{1,0:T(8,128)S(1)} %get-tuple-element.58.ya_ref, f32[128,128]{1,0:T(8,128)S(1)} %get-tuple-element.59.yb_ref, f32[128,128]{1,0:T(8,128)S(1)} %collective-permute-done.7.ra_ref, ...), custom_call_target="tpu_custom_call", output_to_operand_aliasing={{0}: (4, {}), {1}: (5, {})} | custom-call | flops 400000000 | tf_op jit(solution)/shard_map/edge_rows/pallas_call | solution.py:625
  14.5 0.2 %rim.1 = (f32[32,128]{1,0:T(8,128)S(1)}, f32[32,128]{1,0:T(8,128)S(1)}) custom-call(f32[16,32,128]{2,1,0:T(8,128)S(1)} %get-tuple-element.63.s1_ref, f32[16,32,128]{2,1,0:T(8,128)S(1)} %get-tuple-element.64.s2_ref), custom_call_target="tpu_custom_call" | custom-call | flops 200000000 | tf_op jit(solution)/shard_map/rim/pallas_call | solution.py:625
  14.7 0.2 %collective-permute-done.5.rb_ref = f32[48,128]{1,0:T(8,128)S(1)} collective-permute-done((f32[48,128]{1,0:T(8,128)S(1)}, f32[48,128]{1,0:T(8,128)S(1)}, u32[]{:S(2)}, u32[]{:S(2)}) %collective-permute-start.5) | collective-permute-done | bytes 24608 | tf_op jit(solution)/shard_map/ppermute | solution.py:650
  14.9 1.4 %last.1 = (f32[16,32,128]{2,1,0:T(8,128)}, f32[2,4,16]{2,1,0:T(4,128)}) custom-call(f32[48,128]{1,0:T(8,128)S(1)} %collective-permute-done.5.rb_ref, f32[48,128]{1,0:T(8,128)S(1)} %collective-permute-done.6.ra_ref, f32[2,4,40,128]{3,2,1,0:T(8,128)S(1)} %slab.1.slab_ref, f32[4,16,128]{2,1,0:T(8,128)S(1)} %get-tuple-element.57.cor_ref, ...), custom_call_target="tpu_custom_call" | custom-call | flops 1500000000 | tf_op jit(solution)/shard_map/last/pallas_call | solution.py:625
  (7 shorter events, 0.0 us)
Async XLA Ops:
  2.3 4.8 %collective-permute-start = (f32[48,128]{1,0:T(8,128)S(1)}, f32[48,128]{1,0:T(8,128)S(1)}, u32[]{:S(2)}, u32[]{:S(2)}) collective-permute-start(f32[48,128]{1,0:T(8,128)S(1)} %get-tuple-element.35.mine_ref), channel_id=1, source_target_pairs={{0,1},{1,0},{2,3},{3,2},{4,5},{5,4},{6,7},{7,6},{8,9},{9,8},{10,11... | collective-permute-start | bytes 73736 | tf_op jit(solution)/shard_map/ppermute | solution.py:650
  5.6 5.6 %collective-permute-start.4 = (f32[168,128]{1,0:T(8,128)S(1)}, f32[168,128]{1,0:T(8,128)S(1)}, u32[]{:S(2)}, u32[]{:S(2)}) collective-permute-start(f32[168,128]{1,0:T(8,128)S(1)} %get-tuple-element.50), channel_id=1, source_target_pairs={{0,1},{1,0},{2,3},{3,2},{4,5},{5,4},{6,7},{7,6},{8,9},{9,8},{10,11... | collective-permute-start | bytes 258056 | tf_op jit(solution)/shard_map/ppermute | solution.py:650
  7.2 4.2 %collective-permute-start.1 = (f32[16,128]{1,0:T(8,128)S(1)}, f32[16,128]{1,0:T(8,128)S(1)}, u32[]{:S(2)}, u32[]{:S(2)}) collective-permute-start(f32[16,128]{1,0:T(8,128)S(1)} %get-tuple-element.45), channel_id=1, source_target_pairs={{0,2},{1,3},{2,0},{3,1},{4,12},{5,13},{6,14},{7,15},{8,10},{9,11},... | collective-permute-start | bytes 24584 | tf_op jit(solution)/shard_map/ppermute | solution.py:650
  9.3 2.1 %collective-permute-start.2 = (f32[16,128]{1,0:T(8,128)S(1)}, f32[16,128]{1,0:T(8,128)S(1)}, u32[]{:S(2)}, u32[]{:S(2)}) collective-permute-start(f32[16,128]{1,0:T(8,128)S(1)} %get-tuple-element.46), channel_id=1, source_target_pairs={{0,8},{1,9},{2,4},{3,5},{4,2},{5,3},{6,14},{7,15},{8,0},{9,1},{10,... | collective-permute-start | bytes 24584 | tf_op jit(solution)/shard_map/ppermute | solution.py:650
  9.4 2.1 %collective-permute-start.3 = (f32[16,128]{1,0:T(8,128)S(1)}, f32[16,128]{1,0:T(8,128)S(1)}, u32[]{:S(2)}, u32[]{:S(2)}) collective-permute-start(f32[16,128]{1,0:T(8,128)S(1)} %get-tuple-element.47.after_ref.mine_ref), channel_id=1, source_target_pairs={{0,8},{1,9},{2,10},{3,11},{4,6},{5,7},{6,4},{7,5},{8,0},{9,1},{10,... | collective-permute-start | bytes 24584 | tf_op jit(solution)/shard_map/ppermute | solution.py:650
  9.9 4.3 %collective-permute-start.7 = (f32[128,128]{1,0:T(8,128)S(1)}, f32[128,128]{1,0:T(8,128)S(1)}, u32[]{:S(2)}, u32[]{:S(2)}) collective-permute-start(f32[128,128]{1,0:T(8,128)S(1)} %get-tuple-element.58.ya_ref), channel_id=1, source_target_pairs={{0,2},{1,3},{2,0},{3,1},{4,6},{5,7},{6,4},{7,5},{8,10},{9,11},{10,... | collective-permute-start | bytes 196616 | tf_op jit(solution)/shard_map/ppermute | solution.py:650
  11.2 3.0 %collective-permute-start.8 = (f32[128,128]{1,0:T(8,128)S(1)}, f32[128,128]{1,0:T(8,128)S(1)}, u32[]{:S(2)}, u32[]{:S(2)}) collective-permute-start(f32[128,128]{1,0:T(8,128)S(1)} %get-tuple-element.59.yb_ref), channel_id=1, source_target_pairs={{0,8},{1,9},{2,4},{3,5},{4,2},{5,3},{6,14},{7,15},{8,0},{9,1},{10,... | collective-permute-start | bytes 196616 | tf_op jit(solution)/shard_map/ppermute | solution.py:650
  11.6 3.3 %collective-permute-start.5 = (f32[48,128]{1,0:T(8,128)S(1)}, f32[48,128]{1,0:T(8,128)S(1)}, u32[]{:S(2)}, u32[]{:S(2)}) collective-permute-start(f32[48,128]{1,0:T(8,128)S(1)} %get-tuple-element.53), channel_id=1, source_target_pairs={{0,24},{1,25},{2,26},{3,27},{4,28},{5,29},{6,30},{7,31},{8,16},{9,... | collective-permute-start | bytes 73736 | tf_op jit(solution)/shard_map/ppermute | solution.py:650
  13.2 1.7 %collective-permute-start.6 = (f32[48,128]{1,0:T(8,128)S(1)}, f32[48,128]{1,0:T(8,128)S(1)}, u32[]{:S(2)}, u32[]{:S(2)}) collective-permute-start(f32[48,128]{1,0:T(8,128)S(1)} %get-tuple-element.54.after_ref), channel_id=1, source_target_pairs={{0,8},{1,9},{2,10},{3,11},{4,12},{5,13},{6,14},{7,15},{8,0},{9,1},... | collective-permute-start | bytes 73736 | tf_op jit(solution)/shard_map/ppermute | solution.py:650
